TPU v7x, 512 devices: a whole 4x8x8 slice. The times are simulated.
512 devices in a mesh: pix: 64 (over z_lo, y, core), day: 8 (over x, z_hi).
Axes of the slice: x: 4, y: 8, z: 8 (z_hi: 2, z_lo: 4; z = z_hi * 4 + z_lo), core: 2. Of those that a mesh axis runs over, the one named last changes fastest.
Arguments:
- observed: float32 [1024, 512, 256], P('day', 'pix'), may hold values from -6 to 6
- missing: int32 [1024, 512, 256], P('day', 'pix'), may hold values 0 or 1
- land: int32 [512, 256], P('pix'), may hold values 0 or 1
- basis_start: float32 [1024, 32], P('day'), may hold values from -0.1875 to 0.1875
- day_weights: float32 [1024, 7], P('day'), may hold values from 0.05 to 0.4
Outputs:
- filled: float32 [1024, 512, 256], P('day', 'pix')
- basis: float32 [1024, 32], P('day')
All inputs are finite; a program needn't handle non-finite values. No bound on the sum of `missing` or of `land` on one device may be relied on, other than what follows from the above.
Results may differ from a plain program's by a relative error of at most 0.0001.
Values sent between devices are 32-bit elements; how exact they have to be, the bound alone decides.
No kernel may reach another device: no remote copies, remote signals or barrier semaphores. Data moves between devices by JAX's collectives and lax.ppermute only.
A program may use at most 64 MiB of HBM per device.

v0:
```python
import jax
import jax.numpy as jnp
from jax import lax
from jax.sharding import PartitionSpec as P

ITERS = 2
RADIUS = 3


exact = lax.Precision.HIGHEST
smoothing = 0.2


def extended(block, sides, width):
    for axis, dim in sides:
        count = lax.axis_size(axis)
        forward = [(i, i + 1) for i in range(count - 1)]
        backward = [(target, source) for source, target in forward]
        low = lax.ppermute(
            lax.slice_in_dim(block, block.shape[dim] - width, None, axis=dim), axis, forward
        )
        high = lax.ppermute(lax.slice_in_dim(block, 0, width, axis=dim), axis, backward)
        block = jnp.concatenate([low, block, high], axis=dim)
    return block


def lower_solve(factor, right):
    return lax.linalg.triangular_solve(factor, right, left_side=True, lower=True)


def day_filter(padded, day_weights, days_here):
    return sum(
        (day_weights[:, j : j + 1] * padded[j : j + days_here] for j in range(day_weights.shape[1]))
    )


def per_device(observed, missing, land, basis_start, day_weights):
    days_here, rows_here, columns = observed.shape
    ocean = (1 - land).astype(jnp.float32)
    ocean_rim = extended(ocean, (("pix", 0),), 1)
    ocean_pad = jnp.pad(ocean_rim, ((0, 0), (1, 1)))
    ocean_flat = ocean.reshape(-1)
    observed_flat = observed.reshape(days_here, -1)
    absent = missing.reshape(days_here, -1) == 1
    filled = jnp.where(absent, jnp.float32(0.0), observed_flat) * ocean_flat
    basis = basis_start
    for sweep in range(ITERS):
        partial_u = jnp.dot(basis.T, filled, precision=exact)
        modes_u = lax.psum(partial_u, "day")
        gram_u = lax.psum(jnp.dot(modes_u, modes_u.T, precision=exact), "pix")
        factor = jnp.linalg.cholesky(gram_u)
        modes_q = lower_solve(factor, modes_u)
        weights_w = lax.psum(jnp.dot(filled, modes_q.T, precision=exact), "pix")
        recon = jnp.dot(weights_w, modes_q, precision=exact)
        padded = extended(recon, (("day", 0),), RADIUS)
        surface = day_filter(padded, day_weights, days_here).reshape(days_here, rows_here, columns)
        rimmed = extended(surface, (("pix", 1),), 1)
        widened = jnp.pad(rimmed, ((0, 0), (0, 0), (1, 1)))
        pairs = [
            (widened[:, :-2, 1:-1], ocean_pad[:-2, 1:-1]),
            (widened[:, 2:, 1:-1], ocean_pad[2:, 1:-1]),
            (widened[:, 1:-1, :-2], ocean_pad[1:-1, :-2]),
            (widened[:, 1:-1, 2:], ocean_pad[1:-1, 2:]),
        ]
        spread_sum = sum((flag * (value - surface) for value, flag in pairs))
        smooth = surface + smoothing * spread_sum
        filled = jnp.where(absent, smooth.reshape(days_here, -1), observed_flat) * ocean_flat
        gram_w = lax.psum(jnp.dot(weights_w.T, weights_w, precision=exact), "day")
        factor_w = jnp.linalg.cholesky(gram_w)
        basis = lower_solve(factor_w, weights_w.T).T
    return (filled.reshape(days_here, rows_here, columns), basis)


def solution(mesh):
    return jax.shard_map(
        per_device,
        mesh=mesh,
        in_specs=(
            P("day", "pix", None),
            P("day", "pix", None),
            P("pix", None),
            P("day", None),
            P("day", None),
        ),
        out_specs=(P("day", "pix", None), P("day", None)),
        check_vma=False,
    )
```

profile of v0, /device:TPU:1, one launch (start us, length us, event | category | flops | bytes accessed | tf_op | source)
XLA Modules:
  0.0 1484.9 jit_solution(12165756724984835557)
XLA Ops:
  7.2 0.7 subtract_convert_fusion
  7.9 4.6 collective-permute-start.2
  12.5 5.5 collective-permute-start.4
  18.0 1.7 broadcast_select_fusion
  20.1 1.4 convolution_bitcast_fusion
  21.8 109.7 %all-reduce.6.cloned.1.call-done = f32[32,2048]{1,0:T(8,128)} async-done(((f32[32,2048]{1,0:T(8,128)}), f32[32,2048]{1,0:T(8,128)}) %all-reduce.6.cloned.1.call-update) | async-done | bytes 262160 | tf_op jit(solution)/shard_map/psum | solution.py:49
  131.5 1.4 fusion.94
  132.9 264.9 %psum.57 = f32[32,32]{0,1:T(8,128)S(1)} all-reduce(f32[32,32]{0,1:T(8,128)S(1)} %fusion.94), channel_id=1, replica_groups=mesh['pix'=64,'day'=8] {'pix'}, use_global_device_ids=true, to_apply=%region_1.2 | all-reduce | flops 1024 | bytes 8192 | tf_op jit(solution)/shard_map/psum | solution.py:50
  397.9 2.9 cholesky.74
  402.2 2.4 custom-call.10
  404.6 1.4 fusion.84
  406.0 1.1 fusion.62
  407.1 264.9 %psum.58 = f32[128,32]{0,1:T(8,128)S(1)} all-reduce(f32[128,32]{0,1:T(8,128)S(1)} %fusion.62), channel_id=1, replica_groups=mesh['pix'=64,'day'=8] {'pix'}, use_global_device_ids=true, to_apply=%region_4.7 | all-reduce | flops 4096 | bytes 32768 | tf_op jit(solution)/shard_map/psum | solution.py:53
  672.2 1.0 fusion.95
  673.2 40.7 %psum.59 = f32[32,32]{0,1:T(8,128)S(1)} all-reduce(f32[32,32]{0,1:T(8,128)S(1)} %fusion.96), channel_id=1, replica_groups=mesh['pix'=64,'day'=8] {'day'}, use_global_device_ids=true, to_apply=%region_5.8 | all-reduce | flops 1024 | bytes 8192 | tf_op jit(solution)/shard_map/psum | solution.py:68
  714.0 2.9 cholesky.85
  717.6 4.4 collective-permute-start
  722.0 1.3 collective-permute-start.1
  723.3 0.7 fusion.71
  723.9 2.4 custom-call.11
  726.4 4.2 collective-permute-done.1
  730.5 1.0 fusion.18
  732.0 11.7 collective-permute-start.3
  743.7 6.2 collective-permute-start.5
  750.7 1.9 select_maximum_fusion.2
  752.6 1.2 fusion.48
  754.1 1.4 fusion.60
  755.5 99.2 %all-reduce.8.cloned.1.call-done = f32[32,2048]{1,0:T(8,128)} async-done(((f32[32,2048]{1,0:T(8,128)}), f32[32,2048]{1,0:T(8,128)}) %all-reduce.8.cloned.1.call-update) | async-done | bytes 262160 | tf_op jit(solution)/shard_map/psum | solution.py:49
  854.8 1.4 fusion.97
  856.2 265.0 %psum.61 = f32[32,32]{0,1:T(8,128)S(1)} all-reduce(f32[32,32]{0,1:T(8,128)S(1)} %fusion.97), channel_id=1, replica_groups=mesh['pix'=64,'day'=8] {'pix'}, use_global_device_ids=true, to_apply=%region_7.11 | all-reduce | flops 1024 | bytes 8192 | tf_op jit(solution)/shard_map/psum | solution.py:50
  1121.2 2.9 cholesky.96
  1125.4 2.4 custom-call.12
  1127.9 1.4 fusion.77
  1129.3 1.1 fusion.58
  1130.3 264.9 %psum.62 = f32[128,32]{0,1:T(8,128)S(1)} all-reduce(f32[128,32]{0,1:T(8,128)S(1)} %fusion.58), channel_id=1, replica_groups=mesh['pix'=64,'day'=8] {'pix'}, use_global_device_ids=true, to_apply=%region_8.12 | all-reduce | flops 4096 | bytes 32768 | tf_op jit(solution)/shard_map/psum | solution.py:53
  1395.4 1.0 fusion.98
  1396.5 40.7 %psum.63 = f32[32,32]{0,1:T(8,128)S(1)} all-reduce(f32[32,32]{0,1:T(8,128)S(1)} %fusion.99), channel_id=1, replica_groups=mesh['pix'=64,'day'=8] {'day'}, use_global_device_ids=true, to_apply=%region_9.13 | all-reduce | flops 1024 | bytes 8192 | tf_op jit(solution)/shard_map/psum | solution.py:68
  1437.3 2.9 cholesky.107
  1440.9 4.3 collective-permute-start.6
  1445.2 1.3 collective-permute-start.7
  1447.2 2.4 custom-call.13
  1449.6 4.2 collective-permute-done.7
  1453.8 1.0 fusion.4
  1455.3 11.7 collective-permute-start.8
  1467.0 6.2 collective-permute-start.9
  1473.2 0.8 convolution_bitcast_fusion.1
  1474.0 1.9 select_maximum_fusion
  1475.9 2.2 fusion.34
  (53 shorter events, 8.1 us)
Async XLA Ops:
  7.2 13.0 copy-start
  7.2 124.3 %all-reduce.6.cloned.1.call-start = ((), (), s32[]{:S(2)}) async-start(), calls=%async_computation | async-start | bytes 524288 | tf_op jit(solution)/shard_map/psum | solution.py:49
  7.9 13.7 collective-permute-start.2
  12.5 9.1 collective-permute-start.4
  18.0 3.6 copy-start.2
  21.6 833.2 %all-reduce.8.cloned.1.call-start = ((), (), s32[]{:S(2)}) async-start(), calls=%async_computation.1 | async-start | bytes 524288 | tf_op jit(solution)/shard_map/psum | solution.py:49
  717.6 8.8 collective-permute-start
  722.0 8.6 collective-permute-start.1
  731.5 21.0 %copy-start.1 = (f32[128,8,256]{2,1,0:T(8,128)S(1)}, f32[128,8,256]{2,1,0:T(8,128)}, u32[]{:S(2)}) copy-start(f32[128,8,256]{2,1,0:T(8,128)} %param.10) | copy-start | bytes 3145732
  732.0 18.0 %collective-permute-start.3 = (f32[128,1,256]{2,1,0:T(1,128)S(1)}, f32[128,1,256]{2,1,0:T(1,128)S(1)}, u32[]{:S(2)}, u32[]{:S(2)}) collective-permute-start(f32[128,1,256]{2,1,0:T(1,128)S(1)} %get-tuple-element.11), channel_id=1, source_target_pairs={{0,8},{8,16},{16,24},{24,32},{32,40},{40,48},{48,56},{56,64},{64,7... | collective-permute-start | bytes 393224 | tf_op jit(solution)/shard_map/ppermute | solution.py:19
  743.7 6.9 collective-permute-start.5
  1440.9 8.8 collective-permute-start.6
  1445.2 8.6 collective-permute-start.7
  1455.3 18.7 %collective-permute-start.8 = (f32[128,1,256]{2,1,0:T(1,128)S(1)}, f32[128,1,256]{2,1,0:T(1,128)S(1)}, u32[]{:S(2)}, u32[]{:S(2)}) collective-permute-start(f32[128,1,256]{2,1,0:T(1,128)S(1)} %get-tuple-element.7), channel_id=1, source_target_pairs={{0,8},{8,16},{16,24},{24,32},{32,40},{40,48},{48,56},{56,64},{64,7... | collective-permute-start | bytes 393224 | tf_op jit(solution)/shard_map/ppermute | solution.py:19
  1467.0 7.0 collective-permute-start.9
Sparse Core Ops, SparseCore 0:
  21.7 109.7 all-reduce.5
  755.7 99.0 all-reduce.7
where the time goes:
time: 1490 us; the launch traced here: 1480 us
  blocking collectives  1140 us (77%)
  waiting for transfers between devices  218 us (15%)
  starting transfers between devices  57.1 us (4%)
  other arithmetic  38.5 us (3%)
    psum x2, blocking collectives, per_device(): gram_u = lax.psum(jnp.dot(modes_u, modes_u.T, precision=exact), 'pix')  530 us
    psum x2, blocking collectives, per_device(): weights_w = lax.psum(jnp.dot(filled, modes_q.T, precision=exact), 'pix')  530 us
    psum x2, waiting for transfers between devices, per_device(): modes_u = lax.psum(partial_u, 'day')  209 us
    psum x2, blocking collectives, per_device(): gram_w = lax.psum(jnp.dot(weights_w.T, weights_w, precision=exact), 'day')  81.5 us
    ppermute x5, starting transfers between devices, extended(): lax.ppermute(lax.slice_in_dim(block, block.shape[dim] - width, None, axis...  36.6 us
  transfers between devices with their start and end apart: 12, of which 5 were waited for; matrix products, arithmetic and copies ran while one was open for 1% of the time, Pallas kernels for 0%

commit v1 on v0

v1 whole, which is shorter than its diff:
```python
import jax
import jax.numpy as jnp
from jax import lax
from jax.sharding import Mesh, PartitionSpec as P

ITERS = 2
RADIUS = 3
K = 32

PIX = ("zlo", "y", "core")
DAY = ("x", "zhi")
NEAR = ("zlo", "core")

exact = lax.Precision.HIGHEST
smoothing = 0.2


def swap(blocks, axes):
    return lax.all_to_all(blocks, axes, 0, 0)


def to_all(block, axes, count):
    return swap(jnp.broadcast_to(block[None], (count,) + block.shape), axes)


def neighbours(low_edge, high_edge, axes, count):
    up = [(i, i + 1) for i in range(count - 1)]
    down = [(i + 1, i) for i in range(count - 1)]
    return lax.ppermute(high_edge, axes, up), lax.ppermute(low_edge, axes, down)


def contract(expr, a, b):
    return jnp.einsum(expr, a, b, precision=exact)


def inverse_factor(gram):
    factor = jnp.linalg.cholesky(gram)
    eye = jnp.eye(K, dtype=jnp.float32)
    return lax.linalg.triangular_solve(factor, eye, left_side=True, lower=True)


def per_device(observed, missing, land, basis_start, day_weights):
    days, rows, cols = observed.shape
    ocean = (1 - land).astype(jnp.float32)
    ocean_low, ocean_high = neighbours(ocean[:1], ocean[-1:], PIX, 64)
    zero_col = jnp.zeros((rows, 1), jnp.float32)
    flags = [
        jnp.concatenate([ocean_low, ocean[:-1]], 0),
        jnp.concatenate([ocean[1:], ocean_high], 0),
        jnp.concatenate([zero_col, ocean[:, :-1]], 1),
        jnp.concatenate([ocean[:, 1:], zero_col], 1),
    ]
    centre = 1.0 - smoothing * sum(flags)

    absent = missing == 1
    first = (jnp.where(absent, jnp.float32(0.0), observed) * ocean).transpose(1, 0, 2)
    gap = (absent.astype(jnp.float32) * ocean).transpose(1, 0, 2)

    filled = first
    weights_t = basis_start.T
    gram = None
    for sweep in range(ITERS):
        halo_low, halo_high = neighbours(
            filled[:, :RADIUS], filled[:, -RADIUS:], DAY, 8
        )
        part = contract("kd,rdc->rkc", weights_t, filled)
        if gram is None:
            modes = swap(part, DAY).sum(0)
        else:
            wide = jnp.pad(gram, ((0, 0), (0, 128 - K)))
            both = jnp.concatenate(
                [part, jnp.broadcast_to(wide[None], (8, K, 128))], axis=2
            )
            both = swap(both, DAY).sum(0)
            factor = inverse_factor(both[:, cols : cols + K])
            modes = jnp.dot(factor, both[:, :cols], precision=exact)
        modes_u = to_all(modes, DAY, 8)

        row_low, row_high = neighbours(modes_u[0], modes_u[-1], PIX, 64)
        ext = jnp.concatenate([halo_low, filled, halo_high], axis=1)
        raw = contract("rkc,rdc->kd", modes_u, ext)
        gram_u = contract("rkc,rlc->kl", modes_u, modes_u)
        joint = jnp.concatenate([gram_u, raw], axis=1).reshape(-1)
        size = joint.shape[0]
        joint = jnp.pad(joint, (0, -size % 1024)).reshape(-1, 128)
        joint = to_all(joint, NEAR, 8).sum(0)
        joint = to_all(joint, "y", 8).sum(0)
        joint = joint.reshape(-1)[:size].reshape(K, -1)

        inv_u = inverse_factor(joint[:, :K])
        wide_t = jnp.dot(inv_u, joint[:, K:], precision=exact)
        weights_t = wide_t[:, RADIUS : RADIUS + days]
        mixed = sum(
            day_weights[:, j][None] * wide_t[:, j : j + days]
            for j in range(2 * RADIUS + 1)
        )
        mixed = jnp.dot(inv_u.T, mixed, precision=exact)

        above = jnp.concatenate([row_low[None], modes_u[:-1]], 0)
        below = jnp.concatenate([modes_u[1:], row_high[None]], 0)
        left = jnp.pad(modes_u[:, :, :-1], ((0, 0), (0, 0), (1, 0)))
        right = jnp.pad(modes_u[:, :, 1:], ((0, 0), (0, 0), (0, 1)))
        smooth = centre[:, None] * modes_u + smoothing * sum(
            flag[:, None] * value
            for flag, value in zip(flags, (above, below, left, right))
        )
        gram = jnp.dot(weights_t, weights_t.T, precision=exact)
        if sweep + 1 < ITERS:
            filled = first + gap * contract("kd,rkc->rdc", mixed, smooth)
        else:
            surface = contract("kd,rkc->drc", mixed, smooth)
            filled = jnp.where(absent, surface, observed) * ocean
    gram = to_all(gram, DAY, 8).sum(0)
    basis = jnp.dot(inverse_factor(gram), weights_t, precision=exact).T
    return filled, basis


def solution(mesh):
    fine = Mesh(
        mesh.devices.reshape(4, 8, 2, 4, 2), ("zlo", "y", "core", "x", "zhi")
    )
    return jax.shard_map(
        per_device,
        mesh=fine,
        in_specs=(
            P(DAY, PIX, None),
            P(DAY, PIX, None),
            P(PIX, None),
            P(DAY, None),
            P(DAY, None),
        ),
        out_specs=(P(DAY, PIX, None), P(DAY, None)),
        check_vma=False,
    )
```

time: 1490 us -> 203 us (0.14)
  blocking collectives: 1140 us -> 15 us
  waiting for transfers between devices: 218 us -> 38 us
  starting transfers between devices: 57.1 us -> 93.3 us
    psum x6 -> x0, blocking collectives: 1140 us -> none  [the longest x2 530 us: per_device(): gram_u = lax.psum(jnp.dot(modes_u, modes_u.T, precision=exact), 'pix')]
    psum x2 -> x0, waiting for transfers between devices: 209 us -> none  [per_device(): modes_u = lax.psum(partial_u, 'day')]
    all_to_all x0 -> x8, starting transfers between devices: none -> 59.9 us  [swap(): return lax.all_to_all(blocks, axes, 0, 0)]
    all_to_all x0 -> x8, waiting for transfers between devices: none -> 31.9 us  [swap(): return lax.all_to_all(blocks, axes, 0, 0)]
    ppermute x10, starting transfers between devices: 57 us -> 33.5 us  [the longest x5 24.8 us: neighbours(): lax.ppermute(high_edge, axes, up)]
    all_to_all x0 -> x1, blocking collectives: none -> 15 us  [swap(): return lax.all_to_all(blocks, axes, 0, 0)]
  transfers between devices with their start and end apart: 12 -> 18, of which waited for: 5 -> 9; matrix products, arithmetic and copies ran while one was open for 1% -> 13% of each run, Pallas kernels for 0% -> 0%
where the time goes in v1:
time: 203 us; the launch traced here: 199 us
  starting transfers between devices  93.3 us (46%)
  waiting for transfers between devices  38 us (19%)
  other arithmetic  30.9 us (15%)
  blocking collectives  15 us (7%)
  matrix products  11.9 us (6%)
  local copies, waits for them, and re-layouts  9.14 us (5%)
    all_to_all x8, starting transfers between devices, swap(): return lax.all_to_all(blocks, axes, 0, 0)  59.9 us
    all_to_all x8, waiting for transfers between devices, swap(): return lax.all_to_all(blocks, axes, 0, 0)  31.9 us
    ppermute x5, starting transfers between devices, neighbours(): lax.ppermute(high_edge, axes, up)  24.8 us
    all_to_all x1, blocking collectives, swap(): return lax.all_to_all(blocks, axes, 0, 0)  15 us
    another operation x12, other arithmetic, inverse_factor(): factor = jnp.linalg.cholesky(gram)  14.4 us
    another operation x8, other arithmetic, inverse_factor(): return lax.linalg.triangular_solve(factor, eye, left_side=True, lower=True)  12.3 us
    ppermute x5, starting transfers between devices, neighbours(): lax.ppermute(low_edge, axes, down)  8.68 us
    dot_general x8, matrix products, contract(): return jnp.einsum(expr, a, b, precision=exact)  8.61 us
  transfers between devices with their start and end apart: 18, of which 9 were waited for; matrix products, arithmetic and copies ran while one was open for 13% of the time, Pallas kernels for 0%

profile of v1, /device:TPU:1, one launch (start us, length us, event | category | flops | bytes accessed | tf_op | source)
XLA Modules:
  0.0 199.5 jit_solution(10585219124097359611)
XLA Ops:
  1.4 2.3 %multiply_bitcast_fusion = (f32[8,128,256]{2,1,0:T(8,128)S(1)}, pred[128,8,256]{2,0,1:T(32,128)(4,1)S(1)}) fusion(f32[128,8,256]{2,1,0:T(8,128)} %param.8, f32[8,256]{1,0:T(8,128)S(1)} %subtract_convert_fusion, s32[128,8,256]{2,1,0:T(8,128)} %param.9), kind=kLoop, calls=%fused_computation.26 | loop fusion | flops 786432 | bytes 3416064 | tf_op jit(solution)/shard_map/transpose | solution.py:56
  3.7 1.4 convolution_bitcast_fusion.2
  5.1 13.3 %all-to-all-start = ((f32[8,32,256]{2,1,0:T(8,128)}), f32[8,32,256]{2,1,0:T(8,128)S(1)}, u32[]{:S(2)}, u32[]{:S(2)}) async-start(f32[8,32,256]{2,1,0:T(8,128)} %convolution_bitcast_fusion.2), calls=%async_computation | async-start | bytes 524288 | tf_op jit(solution)/shard_map/all_to_all | solution.py:19
  18.4 7.3 %collective-permute-start.4 = (f32[8,3,256]{2,1,0:T(4,128)S(1)}, f32[8,3,256]{2,1,0:T(4,128)S(1)}, u32[]{:S(2)}, u32[]{:S(2)}) collective-permute-start(f32[8,3,256]{2,1,0:T(4,128)S(1)} %get-tuple-element.19), channel_id=1, source_target_pairs={{0,1},{1,2},{2,3},{3,4},{4,5},{5,6},{6,7},{8,9},{9,10},{10,11},{11... | collective-permute-start | bytes 73736 | tf_op jit(solution)/shard_map/ppermute | solution.py:29
  25.7 1.3 collective-permute-start.5
  27.0 1.6 all-to-all-done
  28.5 0.7 broadcast_in_dim.34
  29.3 8.1 %all-to-all-start.1 = ((f32[8,32,256]{2,1,0:T(8,128)}), f32[8,32,256]{2,1,0:T(8,128)S(1)}, u32[]{:S(2)}, u32[]{:S(2)}) async-start(f32[8,32,256]{2,1,0:T(8,128)} %broadcast_in_dim.34), calls=%async_computation.1 | async-start | bytes 524288 | tf_op jit(solution)/shard_map/all_to_all | solution.py:19
  37.4 5.2 %collective-permute-start = (f32[1,256]{1,0:T(1,128)S(1)}, f32[1,256]{1,0:T(1,128)S(1)}, u32[]{:S(2)}, u32[]{:S(2)}) collective-permute-start(f32[1,256]{1,0:T(1,128)S(1)} %get-tuple-element.38), channel_id=1, source_target_pairs={{0,8},{8,16},{16,24},{24,32},{32,40},{40,48},{48,56},{56,64},{64,7... | collective-permute-start | bytes 3080 | tf_op jit(solution)/shard_map/ppermute | solution.py:29
  42.6 1.9 collective-permute-start.1
  44.6 2.9 %all-to-all-done.1 = f32[8,32,256]{2,1,0:T(8,128)S(1)} async-done(((f32[8,32,256]{2,1,0:T(8,128)}), f32[8,32,256]{2,1,0:T(8,128)S(1)}, u32[]{:S(2)}, u32[]{:S(2)}) %all-to-all-start.1) | async-done | bytes 262176 | tf_op jit(solution)/shard_map/all_to_all | solution.py:19
  47.9 1.2 fusion.18
  50.0 8.4 %all-to-all-start.2 = ((f32[8,48,128]{2,1,0:T(8,128)}), f32[8,48,128]{2,1,0:T(8,128)S(1)}, u32[]{:S(2)}, u32[]{:S(2)}) async-start(f32[8,48,128]{2,1,0:T(8,128)} %broadcast_in_dim.38), calls=%async_computation.2 | async-start | bytes 393216 | tf_op jit(solution)/shard_map/all_to_all | solution.py:19
  58.6 3.1 %collective-permute-start.2 = (f32[32,256]{1,0:T(8,128)S(1)}, f32[32,256]{1,0:T(8,128)S(1)}, u32[]{:S(2)}, u32[]{:S(2)}) collective-permute-start(f32[32,256]{1,0:T(8,128)S(1)} %get-tuple-element.32), channel_id=1, source_target_pairs={{0,8},{8,16},{16,24},{24,32},{32,40},{40,48},{48,56},{56,64},{64,7... | collective-permute-start | bytes 98312 | tf_op jit(solution)/shard_map/ppermute | solution.py:29
  61.7 1.9 collective-permute-start.3
  63.6 1.3 all-to-all-done.2
  65.6 6.8 %all-to-all-start.3 = ((f32[8,48,128]{2,1,0:T(8,128)}), f32[8,48,128]{2,1,0:T(8,128)S(1)}, u32[]{:S(2)}, u32[]{:S(2)}) async-start(f32[8,48,128]{2,1,0:T(8,128)} %broadcast_in_dim.39), calls=%async_computation.3 | async-start | bytes 393216 | tf_op jit(solution)/shard_map/all_to_all | solution.py:19
  72.5 0.7 fusion.155
  73.3 7.8 %all-to-all-done.3 = f32[8,48,128]{2,1,0:T(8,128)S(1)} async-done(((f32[8,48,128]{2,1,0:T(8,128)}), f32[8,48,128]{2,1,0:T(8,128)S(1)}, u32[]{:S(2)}, u32[]{:S(2)}) %all-to-all-start.3) | async-done | bytes 196640 | tf_op jit(solution)/shard_map/all_to_all | solution.py:19
  81.4 2.9 %cholesky.74 = f32[32,32]{1,0:T(8,128)S(1)} custom-call(f32[32,32]{1,0:T(8,128)S(1)} %fusion.111), custom_call_target="Cholesky" | custom-call | tf_op jit(solution)/shard_map/jit(cholesky)/cholesky | solution.py:37
  85.7 2.4 %custom-call.8 = f32[1,32,32]{1,2,0:T(8,128)S(1)} custom-call(f32[1,32,32]{2,1,0:T(8,128)S(1)} %fusion.77), custom_call_target="InvertDiagBlocksLowerTriangular" | custom-call | tf_op jit(solution)/shard_map/triangular_solve/custom-call.0 | solution.py:39
  89.1 2.1 %fusion.1 = f32[8,128,256]{2,1,0:T(8,128)S(1)} fusion(f32[8,128,256]{2,1,0:T(8,128)S(1)} %get-tuple-element.15, f32[32,128,1]{1,0,2:T(8,128)S(1)} %convolution_bitcast_fusion.4, pred[128,8,256]{2,0,1:T(32,128)(4,1)S(1)} %get-tuple-element.16, f32[8,256]{1,0:T(8,128)S(1)} %subtract_convert_fusion, f32[7,32,256]{2,1,0:T(8,128)} %get-tuple-element.30, ...), kind=kOutput, calls=%fused_computation.2 | convolution fusion | flops 102236160 | bytes 3733504 | tf_op jit(solution)/shard_map/kd,rkc->rdc/dot_general | solution.py:33
  92.0 15.0 %all_to_all.45 = f32[8,32,384]{2,1,0:T(8,128)S(1)} all-to-all(f32[8,32,384]{2,1,0:T(8,128)S(1)} %pad_maximum_fusion), channel_id=1, replica_groups=mesh['zlo'=4,'y'=8,'core'=2,'x'=4,'zhi'=2] {'x','zhi'}, dimensions={0} | all-to-all | bytes 786432 | tf_op jit(solution)/shard_map/all_to_all | solution.py:19
  107.1 2.9 %cholesky.85 = f32[32,32]{1,0:T(8,128)S(1)} custom-call(f32[32,32]{1,0:T(8,128)S(1)} %fusion.108), custom_call_target="Cholesky" | custom-call | tf_op jit(solution)/shard_map/jit(cholesky)/cholesky | solution.py:37
  111.4 2.4 %custom-call.9 = f32[1,32,32]{1,2,0:T(8,128)S(1)} custom-call(f32[1,32,32]{2,1,0:T(8,128)S(1)} %fusion.78), custom_call_target="InvertDiagBlocksLowerTriangular" | custom-call | tf_op jit(solution)/shard_map/triangular_solve/custom-call.0 | solution.py:39
  114.2 0.7 broadcast_in_dim.41
  115.0 3.4 %all-to-all-start.5 = ((f32[8,32,256]{2,1,0:T(8,128)}), f32[8,32,256]{2,1,0:T(8,128)S(1)}, u32[]{:S(2)}, u32[]{:S(2)}) async-start(f32[8,32,256]{2,1,0:T(8,128)} %broadcast_in_dim.41), calls=%async_computation.5 | async-start | bytes 524288 | tf_op jit(solution)/shard_map/all_to_all | solution.py:19
  118.4 7.2 %collective-permute-start.6 = (f32[8,3,256]{2,1,0:T(4,128)S(1)}, f32[8,3,256]{2,1,0:T(4,128)S(1)}, u32[]{:S(2)}, u32[]{:S(2)}) collective-permute-start(f32[8,3,256]{2,1,0:T(4,128)S(1)} %get-tuple-element.17), channel_id=1, source_target_pairs={{0,1},{1,2},{2,3},{3,4},{4,5},{5,6},{6,7},{8,9},{9,10},{10,11},{11... | collective-permute-start | bytes 73736 | tf_op jit(solution)/shard_map/ppermute | solution.py:29
  125.6 1.3 collective-permute-start.7
  126.9 1.6 all-to-all-done.5
  128.8 6.1 %collective-permute-done.7 = f32[8,3,256]{2,1,0:T(4,128)S(1)} collective-permute-done((f32[8,3,256]{2,1,0:T(4,128)S(1)}, f32[8,3,256]{2,1,0:T(4,128)S(1)}, u32[]{:S(2)}, u32[]{:S(2)}) %collective-permute-start.7) | collective-permute-done | bytes 24608 | tf_op jit(solution)/shard_map/ppermute | solution.py:29
  134.9 1.2 fusion.15
  137.0 10.9 %all-to-all-start.6 = ((f32[8,48,128]{2,1,0:T(8,128)}), f32[8,48,128]{2,1,0:T(8,128)S(1)}, u32[]{:S(2)}, u32[]{:S(2)}) async-start(f32[8,48,128]{2,1,0:T(8,128)} %broadcast_in_dim.43), calls=%async_computation.6 | async-start | bytes 393216 | tf_op jit(solution)/shard_map/all_to_all | solution.py:19
  147.9 2.1 %collective-permute-start.8 = (f32[32,256]{1,0:T(8,128)S(1)}, f32[32,256]{1,0:T(8,128)S(1)}, u32[]{:S(2)}, u32[]{:S(2)}) collective-permute-start(f32[32,256]{1,0:T(8,128)S(1)} %get-tuple-element.26), channel_id=1, source_target_pairs={{0,8},{8,16},{16,24},{24,32},{32,40},{40,48},{48,56},{56,64},{64,7... | collective-permute-start | bytes 98312 | tf_op jit(solution)/shard_map/ppermute | solution.py:29
  150.0 2.3 %collective-permute-start.9 = (f32[32,256]{1,0:T(8,128)S(1)}, f32[32,256]{1,0:T(8,128)S(1)}, u32[]{:S(2)}, u32[]{:S(2)}) collective-permute-start(f32[32,256]{1,0:T(8,128)S(1)} %get-tuple-element.25), channel_id=1, source_target_pairs={{8,0},{16,8},{24,16},{32,24},{40,32},{48,40},{56,48},{64,56},{72,6... | collective-permute-start | bytes 98312 | tf_op jit(solution)/shard_map/ppermute | solution.py:29
  152.2 2.1 %all-to-all-done.6 = f32[8,48,128]{2,1,0:T(8,128)S(1)} async-done(((f32[8,48,128]{2,1,0:T(8,128)}), f32[8,48,128]{2,1,0:T(8,128)S(1)}, u32[]{:S(2)}, u32[]{:S(2)}) %all-to-all-start.6) | async-done | bytes 196640 | tf_op jit(solution)/shard_map/all_to_all | solution.py:19
  155.1 3.4 %all-to-all-start.7 = ((f32[8,48,128]{2,1,0:T(8,128)}), f32[8,48,128]{2,1,0:T(8,128)S(1)}, u32[]{:S(2)}, u32[]{:S(2)}) async-start(f32[8,48,128]{2,1,0:T(8,128)} %broadcast_in_dim.44), calls=%async_computation.7 | async-start | bytes 393216 | tf_op jit(solution)/shard_map/all_to_all | solution.py:19
  158.7 8.5 %all-to-all-done.7 = f32[8,48,128]{2,1,0:T(8,128)S(1)} async-done(((f32[8,48,128]{2,1,0:T(8,128)}), f32[8,48,128]{2,1,0:T(8,128)S(1)}, u32[]{:S(2)}, u32[]{:S(2)}) %all-to-all-start.7) | async-done | bytes 196640 | tf_op jit(solution)/shard_map/all_to_all | solution.py:19
  167.4 2.9 %cholesky.96 = f32[32,32]{1,0:T(8,128)S(1)} custom-call(f32[32,32]{1,0:T(8,128)S(1)} %fusion.106), custom_call_target="Cholesky" | custom-call | tf_op jit(solution)/shard_map/jit(cholesky)/cholesky | solution.py:37
  171.6 2.4 %custom-call.10 = f32[1,32,32]{1,2,0:T(8,128)S(1)} custom-call(f32[1,32,32]{2,1,0:T(8,128)S(1)} %fusion.79), custom_call_target="InvertDiagBlocksLowerTriangular" | custom-call | tf_op jit(solution)/shard_map/triangular_solve/custom-call.0 | solution.py:39
  175.0 0.7 reshape.82
  175.8 5.5 %all-to-all-start.8 = ((f32[8,1,1024]{2,1,0:T(1,128)}), f32[8,1,1024]{2,1,0:T(1,128)S(1)}, u32[]{:S(2)}, u32[]{:S(2)}) async-start(f32[8,1,1024]{2,1,0:T(1,128)} %reshape.82), calls=%async_computation.8 | async-start | bytes 65536 | tf_op jit(solution)/shard_map/all_to_all | solution.py:19
  181.3 1.4 fusion.2
  182.7 1.6 copy.46
  184.2 6.0 %all-to-all-done.8 = f32[8,1,1024]{2,1,0:T(1,128)S(1)} async-done(((f32[8,1,1024]{2,1,0:T(1,128)}), f32[8,1,1024]{2,1,0:T(1,128)S(1)}, u32[]{:S(2)}, u32[]{:S(2)}) %all-to-all-start.8) | async-done | bytes 32800 | tf_op jit(solution)/shard_map/all_to_all | solution.py:19
  191.7 2.9 %cholesky.107 = f32[32,32]{1,0:T(8,128)S(1)} custom-call(f32[32,32]{1,0:T(8,128)S(1)} %fusion.104), custom_call_target="Cholesky" | custom-call | tf_op jit(solution)/shard_map/jit(cholesky)/cholesky | solution.py:37
  196.0 2.4 %custom-call.11 = f32[1,32,32]{1,2,0:T(8,128)S(1)} custom-call(f32[1,32,32]{2,1,0:T(8,128)S(1)} %fusion.80), custom_call_target="InvertDiagBlocksLowerTriangular" | custom-call | tf_op jit(solution)/shard_map/triangular_solve/custom-call.0 | solution.py:39
  198.7 0.8 fusion.119
  (91 shorter events, 15.7 us)
Async XLA Ops:
  0.6 3.0 %copy-start = (f32[128,32]{0,1:T(8,128)S(1)}, f32[128,32]{0,1:T(8,128)}, u32[]{:S(2)}) copy-start(f32[128,32]{0,1:T(8,128)} %param.11) | copy-start | bytes 49156
  5.1 23.5 %all-to-all-start = ((f32[8,32,256]{2,1,0:T(8,128)}), f32[8,32,256]{2,1,0:T(8,128)S(1)}, u32[]{:S(2)}, u32[]{:S(2)}) async-start(f32[8,32,256]{2,1,0:T(8,128)} %convolution_bitcast_fusion.2), calls=%async_computation | async-start | bytes 524288 | tf_op jit(solution)/shard_map/all_to_all | solution.py:19
  18.4 29.5 %collective-permute-start.4 = (f32[8,3,256]{2,1,0:T(4,128)S(1)}, f32[8,3,256]{2,1,0:T(4,128)S(1)}, u32[]{:S(2)}, u32[]{:S(2)}) collective-permute-start(f32[8,3,256]{2,1,0:T(4,128)S(1)} %get-tuple-element.19), channel_id=1, source_target_pairs={{0,1},{1,2},{2,3},{3,4},{4,5},{5,6},{6,7},{8,9},{9,10},{10,11},{11... | collective-permute-start | bytes 73736 | tf_op jit(solution)/shard_map/ppermute | solution.py:29
  25.7 22.3 %collective-permute-start.5 = (f32[8,3,256]{2,1,0:T(4,128)S(1)}, f32[8,3,256]{2,1,0:T(4,128)S(1)}, u32[]{:S(2)}, u32[]{:S(2)}) collective-permute-start(f32[8,3,256]{2,1,0:T(4,128)S(1)} %get-tuple-element.20), channel_id=1, source_target_pairs={{1,0},{2,1},{3,2},{4,3},{5,4},{6,5},{7,6},{9,8},{10,9},{11,10},{12... | collective-permute-start | bytes 73736 | tf_op jit(solution)/shard_map/ppermute | solution.py:29
  29.3 18.3 %all-to-all-start.1 = ((f32[8,32,256]{2,1,0:T(8,128)}), f32[8,32,256]{2,1,0:T(8,128)S(1)}, u32[]{:S(2)}, u32[]{:S(2)}) async-start(f32[8,32,256]{2,1,0:T(8,128)} %broadcast_in_dim.34), calls=%async_computation.1 | async-start | bytes 524288 | tf_op jit(solution)/shard_map/all_to_all | solution.py:19
  37.4 21.1 %collective-permute-start = (f32[1,256]{1,0:T(1,128)S(1)}, f32[1,256]{1,0:T(1,128)S(1)}, u32[]{:S(2)}, u32[]{:S(2)}) collective-permute-start(f32[1,256]{1,0:T(1,128)S(1)} %get-tuple-element.38), channel_id=1, source_target_pairs={{0,8},{8,16},{16,24},{24,32},{32,40},{40,48},{48,56},{56,64},{64,7... | collective-permute-start | bytes 3080 | tf_op jit(solution)/shard_map/ppermute | solution.py:29
  42.6 15.9 %collective-permute-start.1 = (f32[1,256]{1,0:T(1,128)S(1)}, f32[1,256]{1,0:T(1,128)S(1)}, u32[]{:S(2)}, u32[]{:S(2)}) collective-permute-start(f32[1,256]{1,0:T(1,128)S(1)} %get-tuple-element.37), channel_id=1, source_target_pairs={{8,0},{16,8},{24,16},{32,24},{40,32},{48,40},{56,48},{64,56},{72,6... | collective-permute-start | bytes 3080 | tf_op jit(solution)/shard_map/ppermute | solution.py:29
  47.9 10.6 %copy-start.2 = (f32[128,7]{0,1:T(8,128)S(1)}, f32[128,7]{0,1:T(8,128)}, u32[]{:S(2)}) copy-start(f32[128,7]{0,1:T(8,128)} %param.12) | copy-start | bytes 10756
  50.0 14.9 %all-to-all-start.2 = ((f32[8,48,128]{2,1,0:T(8,128)}), f32[8,48,128]{2,1,0:T(8,128)S(1)}, u32[]{:S(2)}, u32[]{:S(2)}) async-start(f32[8,48,128]{2,1,0:T(8,128)} %broadcast_in_dim.38), calls=%async_computation.2 | async-start | bytes 393216 | tf_op jit(solution)/shard_map/all_to_all | solution.py:19
  58.6 30.5 %collective-permute-start.2 = (f32[32,256]{1,0:T(8,128)S(1)}, f32[32,256]{1,0:T(8,128)S(1)}, u32[]{:S(2)}, u32[]{:S(2)}) collective-permute-start(f32[32,256]{1,0:T(8,128)S(1)} %get-tuple-element.32), channel_id=1, source_target_pairs={{0,8},{8,16},{16,24},{24,32},{32,40},{40,48},{48,56},{56,64},{64,7... | collective-permute-start | bytes 98312 | tf_op jit(solution)/shard_map/ppermute | solution.py:29
  61.7 27.4 %collective-permute-start.3 = (f32[32,256]{1,0:T(8,128)S(1)}, f32[32,256]{1,0:T(8,128)S(1)}, u32[]{:S(2)}, u32[]{:S(2)}) collective-permute-start(f32[32,256]{1,0:T(8,128)S(1)} %get-tuple-element.31), channel_id=1, source_target_pairs={{8,0},{16,8},{24,16},{32,24},{40,32},{48,40},{56,48},{64,56},{72,6... | collective-permute-start | bytes 98312 | tf_op jit(solution)/shard_map/ppermute | solution.py:29
  65.6 15.5 %all-to-all-start.3 = ((f32[8,48,128]{2,1,0:T(8,128)}), f32[8,48,128]{2,1,0:T(8,128)S(1)}, u32[]{:S(2)}, u32[]{:S(2)}) async-start(f32[8,48,128]{2,1,0:T(8,128)} %broadcast_in_dim.39), calls=%async_computation.3 | async-start | bytes 393216 | tf_op jit(solution)/shard_map/all_to_all | solution.py:19
  115.0 13.5 %all-to-all-start.5 = ((f32[8,32,256]{2,1,0:T(8,128)}), f32[8,32,256]{2,1,0:T(8,128)S(1)}, u32[]{:S(2)}, u32[]{:S(2)}) async-start(f32[8,32,256]{2,1,0:T(8,128)} %broadcast_in_dim.41), calls=%async_computation.5 | async-start | bytes 524288 | tf_op jit(solution)/shard_map/all_to_all | solution.py:19
  118.4 10.4 %collective-permute-start.6 = (f32[8,3,256]{2,1,0:T(4,128)S(1)}, f32[8,3,256]{2,1,0:T(4,128)S(1)}, u32[]{:S(2)}, u32[]{:S(2)}) collective-permute-start(f32[8,3,256]{2,1,0:T(4,128)S(1)} %get-tuple-element.17), channel_id=1, source_target_pairs={{0,1},{1,2},{2,3},{3,4},{4,5},{5,6},{6,7},{8,9},{9,10},{10,11},{11... | collective-permute-start | bytes 73736 | tf_op jit(solution)/shard_map/ppermute | solution.py:29
  125.6 9.3 %collective-permute-start.7 = (f32[8,3,256]{2,1,0:T(4,128)S(1)}, f32[8,3,256]{2,1,0:T(4,128)S(1)}, u32[]{:S(2)}, u32[]{:S(2)}) collective-permute-start(f32[8,3,256]{2,1,0:T(4,128)S(1)} %get-tuple-element.18), channel_id=1, source_target_pairs={{1,0},{2,1},{3,2},{4,3},{5,4},{6,5},{7,6},{9,8},{10,9},{11,10},{12... | collective-permute-start | bytes 73736 | tf_op jit(solution)/shard_map/ppermute | solution.py:29
  137.0 17.3 %all-to-all-start.6 = ((f32[8,48,128]{2,1,0:T(8,128)}), f32[8,48,128]{2,1,0:T(8,128)S(1)}, u32[]{:S(2)}, u32[]{:S(2)}) async-start(f32[8,48,128]{2,1,0:T(8,128)} %broadcast_in_dim.43), calls=%async_computation.6 | async-start | bytes 393216 | tf_op jit(solution)/shard_map/all_to_all | solution.py:19
  147.9 33.4 %collective-permute-start.8 = (f32[32,256]{1,0:T(8,128)S(1)}, f32[32,256]{1,0:T(8,128)S(1)}, u32[]{:S(2)}, u32[]{:S(2)}) collective-permute-start(f32[32,256]{1,0:T(8,128)S(1)} %get-tuple-element.26), channel_id=1, source_target_pairs={{0,8},{8,16},{16,24},{24,32},{32,40},{40,48},{48,56},{56,64},{64,7... | collective-permute-start | bytes 98312 | tf_op jit(solution)/shard_map/ppermute | solution.py:29
  150.0 31.3 %collective-permute-start.9 = (f32[32,256]{1,0:T(8,128)S(1)}, f32[32,256]{1,0:T(8,128)S(1)}, u32[]{:S(2)}, u32[]{:S(2)}) collective-permute-start(f32[32,256]{1,0:T(8,128)S(1)} %get-tuple-element.25), channel_id=1, source_target_pairs={{8,0},{16,8},{24,16},{32,24},{40,32},{48,40},{56,48},{64,56},{72,6... | collective-permute-start | bytes 98312 | tf_op jit(solution)/shard_map/ppermute | solution.py:29
  155.1 12.0 %all-to-all-start.7 = ((f32[8,48,128]{2,1,0:T(8,128)}), f32[8,48,128]{2,1,0:T(8,128)S(1)}, u32[]{:S(2)}, u32[]{:S(2)}) async-start(f32[8,48,128]{2,1,0:T(8,128)} %broadcast_in_dim.44), calls=%async_computation.7 | async-start | bytes 393216 | tf_op jit(solution)/shard_map/all_to_all | solution.py:19
  158.5 22.8 %copy-start.1 = (f32[128,8,256]{2,1,0:T(8,128)S(1)}, f32[128,8,256]{2,1,0:T(8,128)}, u32[]{:S(2)}) copy-start(f32[128,8,256]{2,1,0:T(8,128)} %param.8) | copy-start | bytes 3145732
  175.8 14.5 %all-to-all-start.8 = ((f32[8,1,1024]{2,1,0:T(1,128)}), f32[8,1,1024]{2,1,0:T(1,128)S(1)}, u32[]{:S(2)}, u32[]{:S(2)}) async-start(f32[8,1,1024]{2,1,0:T(1,128)} %reshape.82), calls=%async_computation.8 | async-start | bytes 65536 | tf_op jit(solution)/shard_map/all_to_all | solution.py:19

commit v2 on v0

v2 whole, which is shorter than its diff:
```python
import jax
import jax.numpy as jnp
from jax import lax
from jax.experimental import pallas as pl
from jax.experimental.pallas import tpu as pltpu
from jax.sharding import Mesh, PartitionSpec as P

RADIUS = 3
K = 32
LANES = 128
HALO = 8 * RADIUS

PIX = ("zlo", "y", "core")
DAY = ("x", "zhi")
NEAR = ("zlo", "core")
SIZES = (4, 8, 2, 4, 2)

exact = lax.Precision.HIGHEST
smoothing = 0.2
f32 = jnp.float32


def mul(a, b):
    return lax.dot_general(
        a, b, (((1,), (0,)), ((), ())), precision=exact, preferred_element_type=f32
    )


def mul_t(a, b):
    return lax.dot_general(
        a, b, (((1,), (1,)), ((), ())), precision=exact, preferred_element_type=f32
    )


def inverse_factor(wide):
    row = lax.broadcasted_iota(jnp.int32, (K, LANES), 0)
    lane = lax.broadcasted_iota(jnp.int32, (K, LANES), 1)
    work = jnp.where(lane < K, wide, jnp.where(lane == row + K, f32(1.0), f32(0.0)))
    below = row[:, :1]
    for k in range(K):
        pivot_row = work[k : k + 1, :]
        pivot_row = pivot_row * (1.0 / pivot_row[:, k : k + 1])
        column = jnp.where(below > k, work[:, k : k + 1], f32(0.0))
        work = work - column * pivot_row
    pivots = jnp.sum(jnp.where(lane == row, work, f32(0.0)), axis=1, keepdims=True)
    work = work * (1.0 / jnp.sqrt(pivots))
    return pltpu.roll(work, LANES - K, 1)[:, :K]


def unpack_gram(packed):
    return jnp.concatenate(
        [packed] + [pltpu.roll(packed, LANES - K * a, 1) for a in range(1, 4)], axis=0
    )


def pack_gram(weights_t):
    wide = mul_t(
        weights_t,
        jnp.concatenate([weights_t, jnp.zeros((LANES - K, LANES), f32)], axis=0),
    )
    packed = wide[:8]
    for a in range(1, 4):
        packed = packed + pltpu.roll(wide[8 * a : 8 * a + 8], K * a, 1)
    return packed


def call(body, outs, args, scratch=(), flops=1_000_000, moved=1_000_000):
    specs = [
        pl.BlockSpec(memory_space=pltpu.SMEM if a.ndim == 1 else pltpu.VMEM)
        for a in args
    ]
    many = isinstance(outs, list)
    shapes = [jax.ShapeDtypeStruct(s, f32) for s in (outs if many else [outs])]
    out_specs = [pl.BlockSpec(memory_space=pltpu.VMEM) for _ in shapes]
    return pl.pallas_call(
        body,
        out_shape=shapes if many else shapes[0],
        in_specs=specs,
        out_specs=out_specs if many else out_specs[0],
        scratch_shapes=list(scratch),
        compiler_params=pltpu.CompilerParams(vmem_limit_bytes=24 * 1024 * 1024),
        cost_estimate=pl.CostEstimate(
            flops=flops, bytes_accessed=moved, transcendentals=0
        ),
    )(*args)


def rows_of(halves, start, size):
    return jnp.concatenate(
        [half[pl.ds(start, size, stride=8), :] for half in halves], axis=1
    )


def start_body(day, observed, missing, land, basis_t, first, out, *halves):
    d = day[0]
    out[:, K:, :] = jnp.zeros((8, HALO, out.shape[2]), f32)
    ocean = 1.0 - land[...].astype(f32)
    low, high = jnp.maximum(d - 1, 0), jnp.minimum(d + 1, 7)
    days = first.shape[1]
    for c, half in enumerate(halves):
        at = slice(LANES * c, LANES * c + LANES)
        tile = jnp.where(missing[:, :, at] == 1, f32(0.0), observed[:, :, at])
        half[...] = (tile * ocean[None, :, at]).reshape(8 * days, LANES)
    for t in range(RADIUS):
        for target, source in ((low, t), (high, days - RADIUS + t)):
            tile = [half[8 * source : 8 * source + 8, :] for half in halves]
            out[target, K + 8 * t : K + 8 * t + 8, :] = jnp.concatenate(tile, axis=1)
    weights_t = basis_t[...]
    for r in range(8):
        filled = rows_of(halves, r, days)
        first[r] = filled
        out[r, :K, :] = mul(weights_t, filled)


def add_rows_body(arrived, out):
    total = arrived[0, :K, :]
    for j in range(1, arrived.shape[0]):
        total = total + arrived[j, :K, :]
    for j in range(out.shape[0]):
        out[j] = total


def add_all_body(arrived, out):
    total = arrived[0]
    for j in range(1, arrived.shape[0]):
        total = total + arrived[j]
    for j in range(out.shape[0]):
        out[j] = total


def factor_body(arrived, out):
    packed = arrived[0, K + HALO :, :LANES]
    for j in range(1, arrived.shape[0]):
        packed = packed + arrived[j, K + HALO :, :LANES]
    out[:, :K] = inverse_factor(unpack_gram(packed))
    out[:, K:] = jnp.zeros((K, LANES - K), f32)


def project_body(day, arrived, modes, filled, land, *rest):
    *factor, out, edge_low, edge_high, halo_0, halo_1 = rest
    scale = factor[0][:, :K] if factor else None
    d = day[0]
    low = arrived[jnp.maximum(d - 1, 0), K : K + HALO, :]
    high = arrived[jnp.minimum(d + 1, 7), K : K + HALO, :]
    low = jnp.where(d > 0, low, f32(0.0))
    high = jnp.where(d < 7, high, f32(0.0))
    cols = modes.shape[2]
    for c, halo in enumerate((halo_0, halo_1)):
        halo[:HALO, :] = low[:, LANES * c : LANES * c + LANES]
        halo[HALO : 2 * HALO, :] = high[:, LANES * c : LANES * c + LANES]
        halo[2 * HALO :, :] = jnp.zeros((64 - 2 * HALO, LANES), f32)
    pad = jnp.zeros((LANES - K - 8, cols), f32)
    total = jnp.zeros((K, 2 * LANES), f32)
    for r in range(8):
        modes_u = modes[r] if scale is None else mul(scale, modes[r])
        days_near = rows_of((halo_0, halo_1), r, 8)
        right = jnp.concatenate([filled[r], modes_u, days_near, pad], axis=0)
        total = total + mul_t(modes_u, right)
    extra = total[:, LANES:]
    packed = extra[:16] + pltpu.roll(extra[16:], 64, 1)
    for j in range(out.shape[0]):
        out[j, :K, :] = total[:, :LANES]
        out[j, K:, :] = packed
    ocean = 1.0 - land[...].astype(f32)
    for edge, r in ((edge_low, 0), (edge_high, 7)):
        edge[:K, :] = modes[r]
        edge[K:, :] = jnp.broadcast_to(ocean[r : r + 1], (8, cols))


def smooth_body(modes, above, below, land, out):
    cols = out.shape[2]
    lane = lax.broadcasted_iota(jnp.int32, (1, cols), 1)
    ocean = 1.0 - land[...].astype(f32)
    rows = [above[:K, :]] + [modes[r] for r in range(8)] + [below[:K, :]]
    flags = (
        [above[K : K + 1, :]]
        + [ocean[r : r + 1] for r in range(8)]
        + [below[K : K + 1, :]]
    )
    for r in range(8):
        here, flag = rows[r + 1], flags[r + 1]
        left = jnp.where(lane > 0, pltpu.roll(flag, 1, 1), f32(0.0))
        right = jnp.where(lane < cols - 1, pltpu.roll(flag, cols - 1, 1), f32(0.0))
        up, down = flags[r], flags[r + 2]
        centre = 1.0 - smoothing * (up + down + left + right)
        spread = (
            up * rows[r]
            + down * rows[r + 2]
            + left * pltpu.roll(here, 1, 1)
            + right * pltpu.roll(here, cols - 1, 1)
        )
        out[r] = centre * here + smoothing * spread


def weights_of(arrived, band, scale):
    total = arrived[0]
    for j in range(1, arrived.shape[0]):
        total = total + arrived[j]
    extra = jnp.concatenate([total[K:], pltpu.roll(total[K:], 64, 1)], axis=0)
    factor = inverse_factor(extra)
    wide = mul(factor, jnp.concatenate([total[:K], extra], axis=1))
    tempered = mul(wide, band[...])
    right = factor if scale is None else mul(factor, scale)
    return wide[:, :LANES], mul(tempered.T, right)


def refill_body(day, arrived, band, smooth, first, gap, land, filled, out):
    weights_t, mixed = weights_of(arrived, band, None)
    d = day[0]
    low, high = jnp.maximum(d - 1, 0), jnp.minimum(d + 1, 7)
    days, cols = filled.shape[1:]
    out[:, K:, :] = jnp.zeros((8, HALO + 8, cols), f32)
    packed = pack_gram(weights_t)
    for j in range(8):
        out[j, K + HALO :, :LANES] = packed
    ocean = 1.0 - land[...].astype(f32)
    for r in range(8):
        surface = mul(mixed, smooth[r])
        now = jnp.where(gap[r] == 1, surface * ocean[r : r + 1], first[r])
        filled[r] = now
        out[r, :K, :] = mul(weights_t, now)
        for t in range(RADIUS):
            at = K + 8 * t + r
            out[low, at : at + 1, :] = now[t : t + 1]
            out[high, at : at + 1, :] = now[days - RADIUS + t : days - RADIUS + t + 1]


def last_weights_body(arrived, band, scale, weights, mixed, out):
    weights_t, mix = weights_of(arrived, band, scale[:, :K])
    weights[...] = weights_t
    mixed[...] = mix
    packed = pack_gram(weights_t)
    for j in range(out.shape[0]):
        out[j] = packed


def last_fill_body(mixed, smooth, observed, missing, land, out, *halves):
    days = observed.shape[0]
    ocean = 1.0 - land[...].astype(f32)
    mix = mixed[...]
    for r in range(8):
        surface = mul(mix, smooth[r])
        for c, half in enumerate(halves):
            half[pl.ds(r, days, stride=8), :] = surface[:, LANES * c : LANES * c + LANES]
    for c, half in enumerate(halves):
        at = slice(LANES * c, LANES * c + LANES)
        surface = half[...].reshape(days, 8, LANES)
        value = jnp.where(missing[:, :, at] == 1, surface, observed[:, :, at])
        out[:, :, at] = value * ocean[None, :, at]


def basis_body(arrived, weights, out):
    packed = arrived[0]
    for j in range(1, arrived.shape[0]):
        packed = packed + arrived[j]
    factor = inverse_factor(unpack_gram(packed))
    out[...] = mul(factor, weights[...]).T


def swap(blocks, axes):
    return lax.all_to_all(blocks, axes, 0, 0)


def near_rows(edge_low, edge_high):
    count = lax.axis_size(PIX)
    up = [(i, i + 1) for i in range(count - 1)]
    down = [(i + 1, i) for i in range(count - 1)]
    return lax.ppermute(edge_high, PIX, up), lax.ppermute(edge_low, PIX, down)


def band_of(day_weights):
    days = day_weights.shape[0]
    slot = lax.broadcasted_iota(jnp.int32, (2 * LANES, days), 0)
    target = lax.broadcasted_iota(jnp.int32, (2 * LANES, days), 1)
    first = LANES + K
    source = jnp.where(slot < days, slot, 4 * days)
    source = jnp.where((slot >= first) & (slot < first + 3), slot - first - 3, source)
    source = jnp.where(
        (slot >= first + 3) & (slot < first + 6), slot - first - 3 + days, source
    )
    taps = day_weights.T
    return sum(
        jnp.where(source - target + RADIUS == j, taps[j : j + 1], f32(0.0))
        for j in range(2 * RADIUS + 1)
    )


def per_device(observed, missing, land, basis_start, day_weights):
    days, rows, cols = observed.shape
    day = lax.axis_index(DAY).reshape(1)
    near, far = lax.axis_size(NEAR), lax.axis_size("y")
    band = band_of(day_weights)

    def sum_over_pixels(joint, edges):
        joint = swap(joint, NEAR)
        joint = call(add_all_body, (far, K + 16, LANES), (joint,))
        joint, *edges = lax.optimization_barrier((joint, *edges))
        return swap(joint, "y"), near_rows(*edges)

    halo = [pltpu.VMEM((64, LANES), f32)] * 2
    halves = [pltpu.VMEM((days * rows, LANES), f32)] * 2
    edge = (K + 8, cols)
    joint_shape = (near, K + 16, LANES)
    block = (rows, K, cols)

    first, part = call(
        start_body,
        [(rows, days, cols), (rows, K + HALO, cols)],
        (day, observed, missing, land, basis_start.T),
        halves,
    )
    gap, part = lax.optimization_barrier((missing, part))
    gap = gap.transpose(1, 0, 2)
    arrived = swap(part, DAY)
    modes = swap(call(add_rows_body, block, (arrived,)), DAY)
    joint, *edges = call(
        project_body,
        [joint_shape, edge, edge],
        (day, arrived, modes, first, land),
        halo,
    )
    joint, (above, below) = sum_over_pixels(joint, edges)
    smooth = call(smooth_body, block, (modes, above, below, land))
    filled, part = call(
        refill_body,
        [(rows, days, cols), (rows, K + HALO + 8, cols)],
        (day, joint, band, smooth, first, gap, land),
    )
    arrived = swap(part, DAY)
    modes = swap(call(add_rows_body, block, (arrived,)), DAY)
    factor = call(factor_body, (K, LANES), (arrived,))
    joint, *edges = call(
        project_body,
        [joint_shape, edge, edge],
        (day, arrived, modes, filled, land, factor),
        halo,
    )
    joint, (above, below) = sum_over_pixels(joint, edges)
    smooth = call(smooth_body, block, (modes, above, below, land))
    weights, mixed, gram = call(
        last_weights_body,
        [(K, LANES), (days, K), (8, 8, LANES)],
        (joint, band, factor),
    )
    gram = swap(gram, DAY)
    filled = call(
        last_fill_body,
        (days, rows, cols),
        (mixed, smooth, observed, missing, land),
        halves,
    )
    basis = call(basis_body, (days, K), (gram, weights))
    return filled, basis


def solution(mesh):
    fine = Mesh(mesh.devices.reshape(SIZES), ("zlo", "y", "core", "x", "zhi"))
    return jax.shard_map(
        per_device,
        mesh=fine,
        in_specs=(
            P(DAY, PIX, None),
            P(DAY, PIX, None),
            P(PIX, None),
            P(DAY, None),
            P(DAY, None),
        ),
        out_specs=(P(DAY, PIX, None), P(DAY, None)),
        check_vma=False,
    )
```

time: 1490 us -> 184 us (0.12)
  blocking collectives: 1140 us -> 81.3 us
  waiting for transfers between devices: 218 us -> 22.6 us
  other arithmetic: 38.5 us -> 0.27 us
  Pallas kernels: 0 us -> 27.1 us
  starting transfers between devices: 57.1 us -> 41.6 us
    psum x6 -> x0, blocking collectives: 1140 us -> none  [the longest x2 530 us: per_device(): gram_u = lax.psum(jnp.dot(modes_u, modes_u.T, precision=exact), 'pix')]
    psum x2 -> x0, waiting for transfers between devices: 209 us -> none  [per_device(): modes_u = lax.psum(partial_u, 'day')]
    all_to_all x0 -> x5, blocking collectives: none -> 81.3 us  [swap(): return lax.all_to_all(blocks, axes, 0, 0)]
    ppermute x10 -> x4, starting transfers between devices: 57 us -> 14.8 us  [near_rows(): return (lax.ppermute(edge_high, PIX, up), lax.ppermute(edge_low, PIX, down))]
    pallas_call x0 -> x14, Pallas kernels: none -> 27.1 us  [call(): pl.pallas_call(body, out_shape=shapes if many else shapes[0], in_specs=sp...]
    another operation x20 -> x0, other arithmetic: 26.7 us -> none  [the longest x8 12.3 us: lower_solve(): lax.linalg.triangular_solve(factor, right, left_side=True, lower=True)]
    all_to_all x0 -> x4, starting transfers between devices: none -> 26.7 us  [swap(): return lax.all_to_all(blocks, axes, 0, 0)]
    all_to_all x0 -> x4, waiting for transfers between devices: none -> 15.5 us  [swap(): return lax.all_to_all(blocks, axes, 0, 0)]
  transfers between devices with their start and end apart: 12 -> 8, of which waited for: 5 -> 4; matrix products, arithmetic and copies ran while one was open for 1% -> 0% of each run, Pallas kernels for 0% -> 3%
where the time goes in v2:
time: 184 us; the launch traced here: 182 us
  blocking collectives  81.3 us (44%)
  starting transfers between devices  41.6 us (23%)
  Pallas kernels  27.1 us (15%)
  waiting for transfers between devices  22.6 us (12%)
  local copies, waits for them, and re-layouts  8.15 us (4%)
    all_to_all x5, blocking collectives, swap(): return lax.all_to_all(blocks, axes, 0, 0)  81.3 us
    pallas_call x14, Pallas kernels, call(): pl.pallas_call(body, out_shape=shapes if many else shapes[0], in_specs=sp...  27.1 us
    all_to_all x4, starting transfers between devices, swap(): return lax.all_to_all(blocks, axes, 0, 0)  26.7 us
    all_to_all x4, waiting for transfers between devices, swap(): return lax.all_to_all(blocks, axes, 0, 0)  15.5 us
    ppermute x4, starting transfers between devices, near_rows(): return (lax.ppermute(edge_high, PIX, up), lax.ppermute(edge_low, PIX, down))  14.8 us
    unnamed x35, local copies, waits for them, and re-layouts  7.8 us
    ppermute x4, waiting for transfers between devices, near_rows(): return (lax.ppermute(edge_high, PIX, up), lax.ppermute(edge_low, PIX, down))  7.05 us
  transfers between devices with their start and end apart: 8, of which 4 were waited for; matrix products, arithmetic and copies ran while one was open for 0% of the time, Pallas kernels for 3%

profile of v2, /device:TPU:1, one launch (start us, length us, event | category | flops | bytes accessed | tf_op | source)
XLA Modules:
  0.0 181.9 jit_solution(2213198065443164001)
XLA Ops:
  0.6 0.7 copy-done.8
  1.3 1.2 copy-done
  2.6 1.2 copy-done.2
  3.8 0.7 copy-done.11
  4.5 0.8 shard_map.68
  5.3 25.7 %all_to_all.45.arrived = f32[8,56,256]{2,1,0:T(8,128)S(1)} all-to-all(f32[8,56,256]{2,1,0:T(8,128)S(1)} %get-tuple-element.24), channel_id=1, replica_groups=mesh['zlo'=4,'y'=8,'core'=2,'x'=4,'zhi'=2] {'x','zhi'}, dimensions={0} | all-to-all | bytes 917504 | tf_op jit(solution)/shard_map/all_to_all | solution.py:261
  31.0 12.6 %all_to_all.46.modes = f32[8,32,256]{2,1,0:T(8,128)S(1)} all-to-all(f32[8,32,256]{2,1,0:T(8,128)S(1)} %shard_map.69), channel_id=1, replica_groups=mesh['zlo'=4,'y'=8,'core'=2,'x'=4,'zhi'=2] {'x','zhi'}, dimensions={0} | all-to-all | bytes 524288 | tf_op jit(solution)/shard_map/all_to_all | solution.py:261
  43.6 2.1 %shard_map.70 = (f32[8,48,128]{2,1,0:T(8,128)}, f32[40,256]{1,0:T(8,128)}, f32[40,256]{1,0:T(8,128)}) custom-call(s32[1]{0:T(128)} %bitcast.day, f32[8,56,256]{2,1,0:T(8,128)S(1)} %all_to_all.45.arrived, f32[8,32,256]{2,1,0:T(8,128)S(1)} %all_to_all.46.modes, f32[8,128,256]{2,1,0:T(8,128)S(1)} %get-tuple-element.25.filled.first, s32[8,256]{1,0:T(8,128)S(1)} %copy-done.8), custom_call_target="tpu_custom_call" | custom-call | flops 1000000 | bytes 1000000 | tf_op jit(solution)/shard_map/pallas_call | solution.py:75
  45.7 12.2 %all-to-all-start.2 = ((f32[8,48,128]{2,1,0:T(8,128)}), f32[8,48,128]{2,1,0:T(8,128)S(1)}, u32[]{:S(2)}, u32[]{:S(2)}) async-start(f32[8,48,128]{2,1,0:T(8,128)} %get-tuple-element.26), calls=%async_computation.2 | async-start | bytes 393216 | tf_op jit(solution)/shard_map/all_to_all | solution.py:261
  57.9 6.4 %all-to-all-done.2.arrived = f32[8,48,128]{2,1,0:T(8,128)S(1)} async-done(((f32[8,48,128]{2,1,0:T(8,128)}), f32[8,48,128]{2,1,0:T(8,128)S(1)}, u32[]{:S(2)}, u32[]{:S(2)}) %all-to-all-start.2) | async-done | bytes 196640 | tf_op jit(solution)/shard_map/all_to_all | solution.py:261
  64.4 0.7 shard_map.71
  65.1 6.8 %all-to-all-start.3 = ((f32[8,48,128]{2,1,0:T(8,128)}), f32[8,48,128]{2,1,0:T(8,128)}, u32[]{:S(2)}, u32[]{:S(2)}) async-start(f32[8,48,128]{2,1,0:T(8,128)} %shard_map.71), calls=%async_computation.3 | async-start | bytes 393216 | tf_op jit(solution)/shard_map/all_to_all | solution.py:261
  71.9 5.7 %collective-permute-start = (f32[40,256]{1,0:T(8,128)}, f32[40,256]{1,0:T(8,128)S(1)}, u32[]{:S(2)}, u32[]{:S(2)}) collective-permute-start(f32[40,256]{1,0:T(8,128)} %get-tuple-element.30), channel_id=1, source_target_pairs={{0,8},{8,16},{16,24},{24,32},{32,40},{40,48},{48,56},{56,64},{64,7... | collective-permute-start | bytes 122888 | tf_op jit(solution)/shard_map/ppermute | solution.py:268
  77.6 1.9 %collective-permute-start.1 = (f32[40,256]{1,0:T(8,128)}, f32[40,256]{1,0:T(8,128)S(1)}, u32[]{:S(2)}, u32[]{:S(2)}) collective-permute-start(f32[40,256]{1,0:T(8,128)} %get-tuple-element.31), channel_id=1, source_target_pairs={{8,0},{16,8},{24,16},{32,24},{40,32},{48,40},{56,48},{64,56},{72,6... | collective-permute-start | bytes 122888 | tf_op jit(solution)/shard_map/ppermute | solution.py:268
  79.5 0.3 select_add_fusion.band
  79.8 0.0 copy-done.1
  79.8 0.3 copy.10
  80.1 0.0 collective-permute-done.above
  80.2 3.4 %collective-permute-done.1.below = f32[40,256]{1,0:T(8,128)S(1)} collective-permute-done((f32[40,256]{1,0:T(8,128)}, f32[40,256]{1,0:T(8,128)S(1)}, u32[]{:S(2)}, u32[]{:S(2)}) %collective-permute-start.1) | collective-permute-done | bytes 40992 | tf_op jit(solution)/shard_map/ppermute | solution.py:268
  83.5 0.2 shard_map.72.smooth
  83.8 0.0 copy-start.4
  83.8 0.7 copy-done.4
  84.5 0.0 all-to-all-done.3.arrived
  84.5 0.9 copy-done.5
  85.4 7.7 %shard_map.73 = (f32[8,128,256]{2,1,0:T(8,128)S(1)}, f32[8,64,256]{2,1,0:T(8,128)S(1)}) custom-call(s32[1]{0:T(128)} %bitcast.day, f32[8,48,128]{2,1,0:T(8,128)} %all-to-all-done.3.arrived, f32[256,128]{1,0:T(8,128)S(1)} %select_add_fusion.band, f32[8,32,256]{2,1,0:T(8,128)S(1)} %copy-done.5, f32[8,128,256]{2,1,0:T(8,128)S(1)} %get-tuple-element.25.filled.first, ...), custom_call_target="tpu_custom_call" | custom-call | flops 1000000 | bytes 1000000 | tf_op jit(solution)/shard_map/pallas_call | solution.py:75
  93.2 0.0 copy-start.6
  93.2 1.0 copy-done.6
  94.2 20.0 %all_to_all.47.arrived = f32[8,64,256]{2,1,0:T(8,128)S(1)} all-to-all(f32[8,64,256]{2,1,0:T(8,128)S(1)} %get-tuple-element.33), channel_id=1, replica_groups=mesh['zlo'=4,'y'=8,'core'=2,'x'=4,'zhi'=2] {'x','zhi'}, dimensions={0} | all-to-all | bytes 1048576 | tf_op jit(solution)/shard_map/all_to_all | solution.py:261
  114.1 0.7 shard_map.74
  114.8 4.3 %all-to-all-start.5 = ((f32[8,32,256]{2,1,0:T(8,128)}), f32[8,32,256]{2,1,0:T(8,128)S(1)}, u32[]{:S(2)}, u32[]{:S(2)}) async-start(f32[8,32,256]{2,1,0:T(8,128)} %shard_map.74), calls=%async_computation.5 | async-start | bytes 524288 | tf_op jit(solution)/shard_map/all_to_all | solution.py:261
  119.1 2.8 %shard_map.75.rest_0_.scale = f32[32,128]{1,0:T(8,128)S(1)} custom-call(f32[8,64,256]{2,1,0:T(8,128)S(1)} %all_to_all.47.arrived), custom_call_target="tpu_custom_call" | custom-call | flops 1000000 | bytes 1000000 | tf_op jit(solution)/shard_map/pallas_call | solution.py:75
  121.9 9.1 %all-to-all-done.5.modes = f32[8,32,256]{2,1,0:T(8,128)S(1)} async-done(((f32[8,32,256]{2,1,0:T(8,128)}), f32[8,32,256]{2,1,0:T(8,128)S(1)}, u32[]{:S(2)}, u32[]{:S(2)}) %all-to-all-start.5) | async-done | bytes 262176 | tf_op jit(solution)/shard_map/all_to_all | solution.py:261
  130.9 2.7 %shard_map.76 = (f32[8,48,128]{2,1,0:T(8,128)S(1)}, f32[40,256]{1,0:T(8,128)S(1)}, f32[40,256]{1,0:T(8,128)S(1)}) custom-call(s32[1]{0:T(128)} %bitcast.day, f32[8,64,256]{2,1,0:T(8,128)S(1)} %all_to_all.47.arrived, f32[8,32,256]{2,1,0:T(8,128)S(1)} %all-to-all-done.5.modes, f32[8,128,256]{2,1,0:T(8,128)S(1)} %copy-done.7, s32[8,256]{1,0:T(8,128)S(1)} %copy-done.8, ...), custom_call_target="tpu_custom_call" | custom-call | flops 1000000 | bytes 1000000 | tf_op jit(solution)/shard_map/pallas_call | solution.py:75
  133.7 0.6 copy-done.14
  134.3 9.9 %all_to_all.48.arrived = f32[8,48,128]{2,1,0:T(8,128)S(1)} all-to-all(f32[8,48,128]{2,1,0:T(8,128)S(1)} %get-tuple-element.35), channel_id=1, replica_groups=mesh['zlo'=4,'y'=8,'core'=2,'x'=4,'zhi'=2] {'zlo','core'}, dimensions={0} | all-to-all | bytes 393216 | tf_op jit(solution)/shard_map/all_to_all | solution.py:261
  144.3 0.0 copy-start.10
  144.3 13.2 %all_to_all.49.arrived = f32[8,48,128]{2,1,0:T(8,128)S(1)} all-to-all(f32[8,48,128]{2,1,0:T(8,128)S(1)} %shard_map.77), channel_id=1, replica_groups=mesh['zlo'=4,'y'=8,'core'=2,'x'=4,'zhi'=2] {'y'}, dimensions={0} | all-to-all | bytes 393216 | tf_op jit(solution)/shard_map/all_to_all | solution.py:261
  157.5 3.9 %shard_map.78 = (f32[32,128]{1,0:T(8,128)S(1)}, f32[128,32]{1,0:T(8,128)S(1)}, f32[8,8,128]{2,1,0:T(8,128)}) custom-call(f32[8,48,128]{2,1,0:T(8,128)S(1)} %all_to_all.49.arrived, f32[256,128]{1,0:T(8,128)S(1)} %select_add_fusion.band, f32[32,128]{1,0:T(8,128)S(1)} %copy-done.10), custom_call_target="tpu_custom_call" | custom-call | flops 1000000 | bytes 1000000 | tf_op jit(solution)/shard_map/pallas_call | solution.py:75
  161.4 3.4 %all-to-all-start.8 = ((f32[8,8,128]{2,1,0:T(8,128)}), f32[8,8,128]{2,1,0:T(8,128)S(1)}, u32[]{:S(2)}, u32[]{:S(2)}) async-start(f32[8,8,128]{2,1,0:T(8,128)} %get-tuple-element.42), calls=%async_computation.8 | async-start | bytes 65536 | tf_op jit(solution)/shard_map/all_to_all | solution.py:261
  164.9 5.3 %collective-permute-start.2 = (f32[40,256]{1,0:T(8,128)S(1)}, f32[40,256]{1,0:T(8,128)S(1)}, u32[]{:S(2)}, u32[]{:S(2)}) collective-permute-start(f32[40,256]{1,0:T(8,128)S(1)} %copy-done.15), channel_id=1, source_target_pairs={{0,8},{8,16},{16,24},{24,32},{32,40},{40,48},{48,56},{56,64},{64,7... | collective-permute-start | bytes 122888 | tf_op jit(solution)/shard_map/ppermute | solution.py:268
  170.2 1.9 %collective-permute-start.3 = (f32[40,256]{1,0:T(8,128)S(1)}, f32[40,256]{1,0:T(8,128)S(1)}, u32[]{:S(2)}, u32[]{:S(2)}) collective-permute-start(f32[40,256]{1,0:T(8,128)S(1)} %copy-done.13), channel_id=1, source_target_pairs={{8,0},{16,8},{24,16},{32,24},{40,32},{48,40},{56,48},{64,56},{72,6... | collective-permute-start | bytes 122888 | tf_op jit(solution)/shard_map/ppermute | solution.py:268
  172.1 0.0 collective-permute-done.2.above
  172.2 3.7 %collective-permute-done.3.below = f32[40,256]{1,0:T(8,128)S(1)} collective-permute-done((f32[40,256]{1,0:T(8,128)S(1)}, f32[40,256]{1,0:T(8,128)S(1)}, u32[]{:S(2)}, u32[]{:S(2)}) %collective-permute-start.3) | collective-permute-done | bytes 40992 | tf_op jit(solution)/shard_map/ppermute | solution.py:268
  175.8 0.2 shard_map.79.smooth
  176.1 2.1 %shard_map.80 = f32[128,8,256]{2,1,0:T(8,128)} custom-call(f32[128,32]{1,0:T(8,128)S(1)} %get-tuple-element.39.mixed, f32[8,32,256]{2,1,0:T(8,128)S(1)} %shard_map.79.smooth, f32[128,8,256]{2,1,0:T(8,128)S(1)} %copy-done.3, s32[128,8,256]{2,1,0:T(8,128)S(1)} %copy-done.1, s32[8,256]{1,0:T(8,128)S(1)} %copy-done.8), custom_call_target="tpu_custom_call" | custom-call | flops 1000000 | bytes 1000000 | tf_op jit(solution)/shard_map/pallas_call | solution.py:75
  178.2 0.0 all-to-all-done.8.arrived
  178.2 3.0 %shard_map.81 = f32[128,32]{1,0:T(8,128)S(1)} custom-call(f32[8,8,128]{2,1,0:T(8,128)S(1)} %all-to-all-done.8.arrived, f32[32,128]{1,0:T(8,128)S(1)} %get-tuple-element.43.weights), custom_call_target="tpu_custom_call" | custom-call | flops 1000000 | bytes 1000000 | tf_op jit(solution)/shard_map/pallas_call | solution.py:75
  181.2 0.7 copy.8
  (28 shorter events, 0.1 us)
Async XLA Ops:
  0.6 0.7 copy-start.8
  1.3 1.2 copy-start
  2.6 1.2 copy-start.2
  3.8 0.7 copy-start.11
  43.6 14.3 %copy-start.16 = (f32[128,7]{0,1:T(8,128)S(1)}, f32[128,7]{0,1:T(8,128)}, u32[]{:S(2)}) copy-start(f32[128,7]{0,1:T(8,128)} %param.9) | copy-start | bytes 10756
  45.7 34.1 %copy-start.1 = (s32[128,8,256]{2,1,0:T(8,128)S(1)}, s32[128,8,256]{2,1,0:T(8,128)}, u32[]{:S(2)}) copy-start(s32[128,8,256]{2,1,0:T(8,128)} %missing.3) | copy-start | bytes 3145732
  45.7 18.7 %all-to-all-start.2 = ((f32[8,48,128]{2,1,0:T(8,128)}), f32[8,48,128]{2,1,0:T(8,128)S(1)}, u32[]{:S(2)}, u32[]{:S(2)}) async-start(f32[8,48,128]{2,1,0:T(8,128)} %get-tuple-element.26), calls=%async_computation.2 | async-start | bytes 393216 | tf_op jit(solution)/shard_map/all_to_all | solution.py:261
  65.1 19.4 %all-to-all-start.3 = ((f32[8,48,128]{2,1,0:T(8,128)}), f32[8,48,128]{2,1,0:T(8,128)}, u32[]{:S(2)}, u32[]{:S(2)}) async-start(f32[8,48,128]{2,1,0:T(8,128)} %shard_map.71), calls=%async_computation.3 | async-start | bytes 393216 | tf_op jit(solution)/shard_map/all_to_all | solution.py:261
  71.9 8.2 %collective-permute-start = (f32[40,256]{1,0:T(8,128)}, f32[40,256]{1,0:T(8,128)S(1)}, u32[]{:S(2)}, u32[]{:S(2)}) collective-permute-start(f32[40,256]{1,0:T(8,128)} %get-tuple-element.30), channel_id=1, source_target_pairs={{0,8},{8,16},{16,24},{24,32},{32,40},{40,48},{48,56},{56,64},{64,7... | collective-permute-start | bytes 122888 | tf_op jit(solution)/shard_map/ppermute | solution.py:268
  77.6 5.9 %collective-permute-start.1 = (f32[40,256]{1,0:T(8,128)}, f32[40,256]{1,0:T(8,128)S(1)}, u32[]{:S(2)}, u32[]{:S(2)}) collective-permute-start(f32[40,256]{1,0:T(8,128)} %get-tuple-element.31), channel_id=1, source_target_pairs={{8,0},{16,8},{24,16},{32,24},{40,32},{48,40},{56,48},{64,56},{72,6... | collective-permute-start | bytes 122888 | tf_op jit(solution)/shard_map/ppermute | solution.py:268
  83.8 0.7 copy-start.4
  84.5 1.0 copy-start.5
  93.2 1.0 copy-start.6
  114.1 16.8 %copy-start.7 = (f32[8,128,256]{2,1,0:T(8,128)S(1)}, f32[8,128,256]{2,1,0:T(8,128)}, u32[]{:S(2)}) copy-start(f32[8,128,256]{2,1,0:T(8,128)} %copy-done.6) | copy-start | bytes 3145732
  114.8 16.1 %all-to-all-start.5 = ((f32[8,32,256]{2,1,0:T(8,128)}), f32[8,32,256]{2,1,0:T(8,128)S(1)}, u32[]{:S(2)}, u32[]{:S(2)}) async-start(f32[8,32,256]{2,1,0:T(8,128)} %shard_map.74), calls=%async_computation.5 | async-start | bytes 524288 | tf_op jit(solution)/shard_map/all_to_all | solution.py:261
  121.9 11.8 %copy-start.9 = (f32[32,128]{1,0:T(8,128)}, f32[32,128]{1,0:T(8,128)S(1)}, u32[]{:S(2)}) copy-start(f32[32,128]{1,0:T(8,128)S(1)} %shard_map.75.rest_0_.scale) | copy-start | bytes 49156
  133.7 0.6 copy-start.14
  134.3 9.9 %copy-start.12 = (f32[40,256]{1,0:T(8,128)}, f32[40,256]{1,0:T(8,128)S(1)}, u32[]{:S(2)}) copy-start(f32[40,256]{1,0:T(8,128)S(1)} %get-tuple-element.41) | copy-start | bytes 122884
  134.3 41.8 %copy-start.3 = (f32[128,8,256]{2,1,0:T(8,128)S(1)}, f32[128,8,256]{2,1,0:T(8,128)}, u32[]{:S(2)}) copy-start(f32[128,8,256]{2,1,0:T(8,128)} %observed.3) | copy-start | bytes 3145732
  144.3 13.2 %copy-start.10 = (f32[32,128]{1,0:T(8,128)S(1)}, f32[32,128]{1,0:T(8,128)}, u32[]{:S(2)}) copy-start(f32[32,128]{1,0:T(8,128)} %copy-done.9) | copy-start | bytes 49156
  157.5 7.4 %copy-start.15 = (f32[40,256]{1,0:T(8,128)S(1)}, f32[40,256]{1,0:T(8,128)}, u32[]{:S(2)}) copy-start(f32[40,256]{1,0:T(8,128)} %copy-done.14) | copy-start | bytes 122884
  161.4 8.8 %copy-start.13 = (f32[40,256]{1,0:T(8,128)S(1)}, f32[40,256]{1,0:T(8,128)}, u32[]{:S(2)}) copy-start(f32[40,256]{1,0:T(8,128)} %copy-done.12) | copy-start | bytes 122884
  161.4 16.8 %all-to-all-start.8 = ((f32[8,8,128]{2,1,0:T(8,128)}), f32[8,8,128]{2,1,0:T(8,128)S(1)}, u32[]{:S(2)}, u32[]{:S(2)}) async-start(f32[8,8,128]{2,1,0:T(8,128)} %get-tuple-element.42), calls=%async_computation.8 | async-start | bytes 65536 | tf_op jit(solution)/shard_map/all_to_all | solution.py:261
  164.9 7.3 %collective-permute-start.2 = (f32[40,256]{1,0:T(8,128)S(1)}, f32[40,256]{1,0:T(8,128)S(1)}, u32[]{:S(2)}, u32[]{:S(2)}) collective-permute-start(f32[40,256]{1,0:T(8,128)S(1)} %copy-done.15), channel_id=1, source_target_pairs={{0,8},{8,16},{16,24},{24,32},{32,40},{40,48},{48,56},{56,64},{64,7... | collective-permute-start | bytes 122888 | tf_op jit(solution)/shard_map/ppermute | solution.py:268
  170.2 5.6 %collective-permute-start.3 = (f32[40,256]{1,0:T(8,128)S(1)}, f32[40,256]{1,0:T(8,128)S(1)}, u32[]{:S(2)}, u32[]{:S(2)}) collective-permute-start(f32[40,256]{1,0:T(8,128)S(1)} %copy-done.13), channel_id=1, source_target_pairs={{8,0},{16,8},{24,16},{32,24},{40,32},{48,40},{56,48},{64,56},{72,6... | collective-permute-start | bytes 122888 | tf_op jit(solution)/shard_map/ppermute | solution.py:268

commit v3 on v2

v3 whole, which is shorter than its diff:
```python
import jax
import jax.numpy as jnp
from jax import lax
from jax.experimental import pallas as pl
from jax.experimental.pallas import tpu as pltpu
from jax.sharding import Mesh, PartitionSpec as P

RADIUS = 3
K = 32
LANES = 128
HALO = 8 * RADIUS

PIX = ("zlo", "y", "core")
DAY = ("x", "zhi")
NEAR = ("zlo", "core")
SIZES = (4, 8, 2, 4, 2)

exact = lax.Precision.HIGHEST
smoothing = 0.2
f32 = jnp.float32


def mul(a, b):
    return lax.dot_general(
        a, b, (((1,), (0,)), ((), ())), precision=exact, preferred_element_type=f32
    )


def mul_t(a, b):
    return lax.dot_general(
        a, b, (((1,), (1,)), ((), ())), precision=exact, preferred_element_type=f32
    )


def inverse_factor(wide):
    row = lax.broadcasted_iota(jnp.int32, (K, LANES), 0)
    lane = lax.broadcasted_iota(jnp.int32, (K, LANES), 1)
    work = jnp.where(lane < K, wide, jnp.where(lane == row + K, f32(1.0), f32(0.0)))
    done = []
    for start in range(0, K, 8):
        size = K - start
        at = lax.broadcasted_iota(jnp.int32, (size, LANES), 0)
        spread = [
            jnp.broadcast_to(work[:, start + j : start + j + 1], (size, LANES))
            for j in range(8)
        ]
        for j in range(8):
            inverse = 1.0 / spread[j][j : j + 1, :]
            column = jnp.where(at > j, spread[j], f32(0.0))
            for l in range(j + 1, 8):
                spread[l] = spread[l] - column * (spread[l][j : j + 1, :] * inverse)
            work = work - column * (work[j : j + 1, :] * inverse)
        done.append(work[:8])
        work = work[8:]
    work = jnp.concatenate(done, axis=0)
    pivots = jnp.sum(jnp.where(lane == row, work, f32(0.0)), axis=1, keepdims=True)
    work = work * (1.0 / jnp.sqrt(pivots))
    return pltpu.roll(work, LANES - K, 1)[:, :K]


def unpack_gram(packed):
    return jnp.concatenate(
        [packed] + [pltpu.roll(packed, LANES - K * a, 1) for a in range(1, 4)], axis=0
    )


def pack_rows(wide):
    packed = wide[:8]
    for a in range(1, 4):
        packed = packed + pltpu.roll(wide[8 * a : 8 * a + 8], K * a, 1)
    return packed


def pack_gram(weights_t):
    rest = jnp.zeros((LANES - K, LANES), f32)
    return pack_rows(mul_t(weights_t, jnp.concatenate([weights_t, rest], axis=0)))


def total_of(arrived):
    total = arrived[0]
    for j in range(1, arrived.shape[0]):
        total = total + arrived[j]
    return total


def call(body, outs, args, scratch=(), limit=8, anywhere=(), alias=None, out_any=()):
    specs = []
    for i, a in enumerate(args):
        space = pltpu.SMEM if a.ndim == 1 else pltpu.VMEM
        specs.append(pl.BlockSpec(memory_space=pl.ANY if i in anywhere else space))
    many = isinstance(outs, list)
    shapes = [jax.ShapeDtypeStruct(s, f32) for s in (outs if many else [outs])]
    out_specs = [
        pl.BlockSpec(memory_space=pl.ANY if i in out_any else pltpu.VMEM)
        for i in range(len(shapes))
    ]
    return pl.pallas_call(
        body,
        out_shape=shapes if many else shapes[0],
        in_specs=specs,
        out_specs=out_specs if many else out_specs[0],
        scratch_shapes=list(scratch),
        input_output_aliases=alias or {},
        compiler_params=pltpu.CompilerParams(vmem_limit_bytes=limit * 1024 * 1024),
        cost_estimate=pl.CostEstimate(
            flops=1_000_000, bytes_accessed=1_000_000, transcendentals=0
        ),
    )(*args)


def rows_of(halves, start, size):
    return jnp.concatenate(
        [half[pl.ds(start, size, stride=8), :] for half in halves], axis=1
    )


def start_body(
    day,
    observed_hbm,
    missing_hbm,
    land_hbm,
    basis_hbm,
    first,
    out,
    observed,
    missing,
    land,
    basis_t,
    half_0,
    half_1,
    arrivals,
):
    pairs = (
        (missing_hbm, missing),
        (observed_hbm, observed),
        (land_hbm, land),
        (basis_hbm, basis_t),
    )
    copies = [
        pltpu.make_async_copy(source, target, arrivals.at[i])
        for i, (source, target) in enumerate(pairs)
    ]
    for copy in copies:
        copy.start()
    d = day[0]
    halves = (half_0, half_1)
    out[:, K:, :] = jnp.zeros((8, HALO, out.shape[2]), f32)
    for copy in copies:
        copy.wait()
    ocean = 1.0 - land[...].astype(f32)
    low, high = jnp.maximum(d - 1, 0), jnp.minimum(d + 1, 7)
    days = first.shape[1]
    for c, half in enumerate(halves):
        at = slice(LANES * c, LANES * c + LANES)
        tile = jnp.where(missing[:, :, at] == 1, f32(0.0), observed[:, :, at])
        half[...] = (tile * ocean[None, :, at]).reshape(8 * days, LANES)
    for t in range(RADIUS):
        for target, source in ((low, t), (high, days - RADIUS + t)):
            tile = [half[8 * source : 8 * source + 8, :] for half in halves]
            out[target, K + 8 * t : K + 8 * t + 8, :] = jnp.concatenate(tile, axis=1)
    weights_t = basis_t[...]
    for r in range(8):
        filled = rows_of(halves, r, days)
        first[r] = filled
        out[r, :K, :] = mul(weights_t, filled)


def add_rows_body(arrived, out):
    total = arrived[0, :K, :]
    for j in range(1, arrived.shape[0]):
        total = total + arrived[j, :K, :]
    for j in range(out.shape[0]):
        out[j] = total


def add_all_body(arrived, out):
    total = total_of(arrived)
    for j in range(out.shape[0]):
        out[j] = total


def add_last_body(arrived, out, extra):
    total = total_of(arrived)
    for j in range(out.shape[0]):
        out[j] = total[:K]
    extra[...] = total[K:]


def factor_body(arrived, out):
    packed = arrived[0, K:, :LANES]
    for j in range(1, arrived.shape[0]):
        packed = packed + arrived[j, K:, :LANES]
    out[:, :K] = inverse_factor(unpack_gram(packed))
    out[:, K:] = jnp.zeros((K, LANES - K), f32)


def edges_of(modes, land, edge_low, edge_high):
    ocean = 1.0 - land[...].astype(f32)
    for edge, r in ((edge_low, 0), (edge_high, 7)):
        edge[:K, :] = modes[r]
        edge[K:, :] = jnp.broadcast_to(ocean[r : r + 1], (8, ocean.shape[1]))


def project_again_body(modes, filled, land, factor, out, edge_low, edge_high):
    cols = modes.shape[2]
    scale = factor[:, :K]
    pad = jnp.zeros((LANES - K, cols), f32)
    total = jnp.zeros((K, 2 * LANES), f32)
    for r in range(8):
        modes_u = mul(scale, modes[r])
        right = jnp.concatenate([filled[r], modes_u, pad], axis=0)
        total = total + mul_t(modes_u, right)
    packed = pack_rows(total[:, LANES:])
    for j in range(out.shape[0]):
        out[j, :K, :] = total[:, :LANES]
        out[j, K:, :] = packed
    edges_of(modes, land, edge_low, edge_high)


def project_body(
    day, arrived, modes, filled, land, out, edge_low, edge_high, halo_0, halo_1
):
    d = day[0]
    low = arrived[jnp.maximum(d - 1, 0), K : K + HALO, :]
    high = arrived[jnp.minimum(d + 1, 7), K : K + HALO, :]
    low = jnp.where(d > 0, low, f32(0.0))
    high = jnp.where(d < 7, high, f32(0.0))
    cols = modes.shape[2]
    for c, halo in enumerate((halo_0, halo_1)):
        halo[:HALO, :] = low[:, LANES * c : LANES * c + LANES]
        halo[HALO : 2 * HALO, :] = high[:, LANES * c : LANES * c + LANES]
        halo[2 * HALO :, :] = jnp.zeros((64 - 2 * HALO, LANES), f32)
    pad = jnp.zeros((LANES - K - 8, cols), f32)
    total = jnp.zeros((K, 2 * LANES), f32)
    for r in range(8):
        modes_u = modes[r]
        days_near = rows_of((halo_0, halo_1), r, 8)
        right = jnp.concatenate([filled[r], modes_u, days_near, pad], axis=0)
        total = total + mul_t(modes_u, right)
    extra = total[:, LANES:]
    packed = extra[:16] + pltpu.roll(extra[16:], 64, 1)
    for j in range(out.shape[0]):
        out[j, :K, :] = total[:, :LANES]
        out[j, K:, :] = packed
    edges_of(modes, land, edge_low, edge_high)


def smooth_body(modes, above, below, land, out):
    cols = out.shape[2]
    lane = lax.broadcasted_iota(jnp.int32, (1, cols), 1)
    ocean = 1.0 - land[...].astype(f32)
    rows = [above[:K, :]] + [modes[r] for r in range(8)] + [below[:K, :]]
    flags = (
        [above[K : K + 1, :]]
        + [ocean[r : r + 1] for r in range(8)]
        + [below[K : K + 1, :]]
    )
    for r in range(8):
        here, flag = rows[r + 1], flags[r + 1]
        left = jnp.where(lane > 0, pltpu.roll(flag, 1, 1), f32(0.0))
        right = jnp.where(lane < cols - 1, pltpu.roll(flag, cols - 1, 1), f32(0.0))
        up, down = flags[r], flags[r + 2]
        centre = 1.0 - smoothing * (up + down + left + right)
        spread = (
            up * rows[r]
            + down * rows[r + 2]
            + left * pltpu.roll(here, 1, 1)
            + right * pltpu.roll(here, cols - 1, 1)
        )
        out[r] = centre * here + smoothing * spread


def refill_body(day, arrived, band, smooth, first, gap, land, filled, out):
    total = total_of(arrived)
    extra = jnp.concatenate([total[K:], pltpu.roll(total[K:], 64, 1)], axis=0)
    raw = jnp.concatenate([total[:K], extra], axis=1)
    tempered_t = mul(raw, band[...]).T
    factor = inverse_factor(extra)
    weights_t = mul(factor, total[:K])
    mixed = mul(tempered_t, mul(factor.T, factor))
    d = day[0]
    low, high = jnp.maximum(d - 1, 0), jnp.minimum(d + 1, 7)
    days, cols = filled.shape[1:]
    packed = pack_gram(weights_t)
    for j in range(8):
        out[j, K:, :LANES] = packed
        out[j, K:, LANES:] = jnp.zeros((8, cols - LANES), f32)
    ocean = 1.0 - land[...].astype(f32)
    for r in range(8):
        surface = mul(mixed, smooth[r])
        now = jnp.where(gap[r] == 1, surface * ocean[r : r + 1], first[r])
        filled[r] = now
        out[r, :K, :] = mul(weights_t, now)


def last_weights_body(raw, extra, band, scale, mixed, right, factor):
    tempered_t = mul(raw[0], band[:LANES, :]).T
    found = inverse_factor(unpack_gram(extra[...]))
    inner = mul(found.T, mul(found, scale[:, :K]))
    mixed[...] = mul(tempered_t, inner)
    right[...] = inner
    factor[...] = found


def last_fill_body(mixed, smooth, observed, missing, land, out, *halves):
    days = observed.shape[0]
    ocean = 1.0 - land[...].astype(f32)
    mix = mixed[...]
    for r in range(8):
        surface = mul(mix, smooth[r])
        for c, half in enumerate(halves):
            half[pl.ds(r, days, stride=8), :] = surface[:, LANES * c : LANES * c + LANES]
    for c, half in enumerate(halves):
        at = slice(LANES * c, LANES * c + LANES)
        surface = half[...].reshape(days, 8, LANES)
        value = jnp.where(missing[:, :, at] == 1, surface, observed[:, :, at])
        out[:, :, at] = value * ocean[None, :, at]


def finish_body(
    day,
    arrived,
    band,
    factor,
    right,
    mixed,
    smooth,
    observed_low,
    observed_high,
    missing_low,
    missing_high,
    land,
    filled_in,
    basis_t,
    filled,
    edges,
    halves,
    sent,
):
    del filled_in
    d = day[0]
    low = arrived[jnp.maximum(d - 1, 0)]
    high = arrived[jnp.minimum(d + 1, 7)]
    low = jnp.where(d > 0, low, f32(0.0))
    high = jnp.where(d < 7, high, f32(0.0))
    near = mul(jnp.concatenate([low, high], axis=1), band[2 * LANES :, :]).T
    near = mixed[...] + mul(near, right[...])
    days = near.shape[0]
    near = jnp.concatenate([near[:8], near[days - 8 :]], axis=0)
    for r in range(8):
        surface = mul(near, smooth[r])
        for c in range(2):
            halves[c, pl.ds(r, 16, stride=8), :] = surface[:, LANES * c : LANES * c + LANES]
    ocean = 1.0 - land[...].astype(f32)
    sides = ((observed_low, missing_low), (observed_high, missing_high))
    copies = []
    for e, (observed, missing) in enumerate(sides):
        for c in range(2):
            at = slice(LANES * c, LANES * c + LANES)
            surface = halves[c, 64 * e : 64 * e + 64, :].reshape(8, 8, LANES)
            value = jnp.where(missing[:, :, at] == 1, surface, observed[:, :, at])
            edges[e, :, :, at] = value * ocean[None, :, at]
        copy = pltpu.make_async_copy(
            edges.at[e], filled.at[pl.ds((days - 8) * e, 8)], sent.at[e]
        )
        copy.start()
        copies.append(copy)
    found = factor[...]
    gram = jnp.zeros((K, LANES), f32)
    rest = jnp.zeros((LANES - K, LANES), f32)
    for j in range(arrived.shape[0]):
        weights_t = mul(found, arrived[j])
        gram = gram + mul_t(weights_t, jnp.concatenate([weights_t, rest], axis=0))
    basis_t[...] = mul(inverse_factor(gram), mul(found, arrived[d]))
    for copy in copies:
        copy.wait()


def swap(blocks, axes):
    return lax.all_to_all(blocks, axes, 0, 0)


def near_rows(edge_low, edge_high):
    count = lax.axis_size(PIX)
    up = [(i, i + 1) for i in range(count - 1)]
    down = [(i + 1, i) for i in range(count - 1)]
    return lax.ppermute(edge_high, PIX, up), lax.ppermute(edge_low, PIX, down)


def band_of(day_weights):
    days = day_weights.shape[0]
    slot = lax.broadcasted_iota(jnp.int32, (4 * LANES, days), 0)
    target = lax.broadcasted_iota(jnp.int32, (4 * LANES, days), 1)
    first = LANES + K
    source = jnp.where(slot < days, slot, 4 * days)
    source = jnp.where((slot >= first) & (slot < first + 3), slot - first - 3, source)
    source = jnp.where(
        (slot >= first + 3) & (slot < first + 6), slot - first - 3 + days, source
    )
    source = jnp.where(slot >= 2 * LANES, slot - 3 * LANES, source)
    source = jnp.where(slot >= 3 * LANES, slot - 3 * LANES + days, source)
    taps = day_weights.T
    return sum(
        jnp.where(source - target + RADIUS == j, taps[j : j + 1], f32(0.0))
        for j in range(2 * RADIUS + 1)
    )


def per_device(observed, missing, land, basis_start, day_weights):
    days, rows, cols = observed.shape
    day = lax.axis_index(DAY).reshape(1)
    near, far = lax.axis_size(NEAR), lax.axis_size("y")
    band = band_of(day_weights)

    halo = [pltpu.VMEM((64, LANES), f32)] * 2
    halves = [pltpu.VMEM((days * rows, LANES), f32)] * 2
    edge = (K + 8, cols)
    block = (rows, K, cols)

    def add_near(joint, edges):
        joint = call(add_all_body, (far,) + joint.shape[1:], (swap(joint, NEAR),))
        return lax.optimization_barrier((joint, *edges))

    def smooth_beside(joint, low, high, modes):
        above, below = near_rows(low, high)
        joint = swap(joint, "y")
        smooth = call(smooth_body, block, (modes, above, below, land))
        return lax.optimization_barrier((joint, smooth))

    first, part = call(
        start_body,
        [(rows, days, cols), (rows, K + HALO, cols)],
        (day, observed, missing, land, basis_start.T),
        [
            pltpu.VMEM((days, rows, cols), f32),
            pltpu.VMEM((days, rows, cols), jnp.int32),
            pltpu.VMEM((rows, cols), jnp.int32),
            pltpu.VMEM((K, days), f32),
            *halves,
            pltpu.SemaphoreType.DMA((4,)),
        ],
        limit=56,
        anywhere=(1, 2, 3, 4),
    )
    gap, part = lax.optimization_barrier((missing, part))
    gap = gap.transpose(1, 0, 2)
    arrived = swap(part, DAY)
    modes = swap(call(add_rows_body, block, (arrived,)), DAY)
    joint, *edges = call(
        project_body,
        [(near, K + 16, LANES), edge, edge],
        (day, arrived, modes, first, land),
        halo,
    )
    joint, low, high = add_near(joint, edges)
    joint, smooth = smooth_beside(joint, low, high, modes)
    filled, part = call(
        refill_body,
        [(rows, days, cols), (rows, K + 8, cols)],
        (day, joint, band[: 2 * LANES], smooth, first, gap, land),
    )
    arrived = swap(part, DAY)
    modes = swap(call(add_rows_body, block, (arrived,)), DAY)
    factor = call(factor_body, (K, LANES), (arrived,))
    joint, *edges = call(
        project_again_body,
        [(near, K + 8, LANES), edge, edge],
        (modes, filled, land, factor),
    )
    joint, low, high = add_near(joint, edges)
    joint, smooth = smooth_beside(joint, low, high, modes)
    raw, extra = call(add_last_body, [(8, K, LANES), (8, LANES)], (joint,))
    arrived = swap(raw, DAY)
    mixed, right, found = call(
        last_weights_body,
        [(days, K), (K, K), (K, K)],
        (raw, extra, band, factor),
    )
    filled = call(
        last_fill_body,
        (days, rows, cols),
        (mixed, smooth, observed, missing, land),
        halves,
    )
    ends = (slice(0, 8), slice(days - 8, days))
    basis_t, filled = call(
        finish_body,
        [(K, days), (days, rows, cols)],
        (day, arrived, band, found, right, mixed, smooth)
        + tuple(observed[e] for e in ends)
        + tuple(missing[e] for e in ends)
        + (land, filled),
        [
            pltpu.VMEM((2, 8, rows, cols), f32),
            pltpu.VMEM((2, 128, LANES), f32),
            pltpu.SemaphoreType.DMA((2,)),
        ],
        anywhere=(12,),
        out_any=(1,),
        alias={12: 1},
    )
    return filled, basis_t.T


def solution(mesh):
    fine = Mesh(mesh.devices.reshape(SIZES), ("zlo", "y", "core", "x", "zhi"))
    return jax.shard_map(
        per_device,
        mesh=fine,
        in_specs=(
            P(DAY, PIX, None),
            P(DAY, PIX, None),
            P(PIX, None),
            P(DAY, None),
            P(DAY, None),
        ),
        out_specs=(P(DAY, PIX, None), P(DAY, None)),
        check_vma=False,
    )
```

time: 184 us -> 174 us (0.946)
  blocking collectives: 81.3 us -> 53.6 us
  waiting for transfers between devices: 22.6 us -> 37 us
  starting transfers between devices: 41.6 us -> 48.8 us
  local copies, waits for them, and re-layouts: 8.15 us -> 4.96 us
    all_to_all x5 -> x3, blocking collectives: 81.3 us -> 53.6 us  [swap(): return lax.all_to_all(blocks, axes, 0, 0)]
    all_to_all x4 -> x6, waiting for transfers between devices: 15.5 us -> 30.5 us  [swap(): return lax.all_to_all(blocks, axes, 0, 0)]
    all_to_all x4 -> x6, starting transfers between devices: 26.7 us -> 34.2 us  [swap(): return lax.all_to_all(blocks, axes, 0, 0)]
    unnamed x35 -> x22, local copies, waits for them, and re-layouts: 7.8 us -> 4.58 us
    pallas_call x14 -> x15, Pallas kernels: 27.1 us -> 25.9 us  [call(): pl.pallas_call(body, out_shape=shapes if many else shapes[0], in_specs=sp...]
  transfers between devices with their start and end apart: 8 -> 10, of which waited for: 4 -> 6; matrix products, arithmetic and copies ran while one was open for 0% -> 1% of each run, Pallas kernels for 3% -> 3%
where the time goes in v3:
time: 174 us; the launch traced here: 172 us
  blocking collectives  53.6 us (31%)
  starting transfers between devices  48.8 us (28%)
  waiting for transfers between devices  37 us (21%)
  Pallas kernels  25.9 us (15%)
  local copies, waits for them, and re-layouts  4.96 us (3%)
    all_to_all x3, blocking collectives, swap(): return lax.all_to_all(blocks, axes, 0, 0)  53.6 us
    all_to_all x6, starting transfers between devices, swap(): return lax.all_to_all(blocks, axes, 0, 0)  34.2 us
    all_to_all x6, waiting for transfers between devices, swap(): return lax.all_to_all(blocks, axes, 0, 0)  30.5 us
    pallas_call x15, Pallas kernels, call(): pl.pallas_call(body, out_shape=shapes if many else shapes[0], in_specs=sp...  25.9 us
    ppermute x4, starting transfers between devices, near_rows(): return (lax.ppermute(edge_high, PIX, up), lax.ppermute(edge_low, PIX, down))  14.6 us
    ppermute x4, waiting for transfers between devices, near_rows(): return (lax.ppermute(edge_high, PIX, up), lax.ppermute(edge_low, PIX, down))  6.48 us
    unnamed x22, local copies, waits for them, and re-layouts  4.58 us
  transfers between devices with their start and end apart: 10, of which 6 were waited for; matrix products, arithmetic and copies ran while one was open for 1% of the time, Pallas kernels for 3%

profile of v3, /device:TPU:1, one launch (start us, length us, event | category | flops | bytes accessed | tf_op | source)
XLA Modules:
  0.0 172.1 jit_solution(18132623595571164351)
XLA Ops:
  0.6 3.3 %shard_map.68 = (f32[8,128,256]{2,1,0:T(8,128)}, f32[8,56,256]{2,1,0:T(8,128)}) custom-call(s32[1]{0:T(128)} %bitcast.day, f32[128,8,256]{2,1,0:T(8,128)} %observed.1, s32[128,8,256]{2,1,0:T(8,128)} %missing.1, s32[8,256]{1,0:T(8,128)} %land.13, f32[32,128]{1,0:T(8,128)} %bitcast.22), custom_call_target="tpu_custom_call" | custom-call | flops 1000000 | bytes 1000000 | tf_op jit(solution)/shard_map/pallas_call | solution.py:97
  3.9 0.0 copy-start.2
  3.9 26.0 %all_to_all.45.arrived = f32[8,56,256]{2,1,0:T(8,128)S(1)} all-to-all(f32[8,56,256]{2,1,0:T(8,128)} %get-tuple-element.32), channel_id=1, replica_groups=mesh['zlo'=4,'y'=8,'core'=2,'x'=4,'zhi'=2] {'x','zhi'}, dimensions={0} | all-to-all | bytes 917504 | tf_op jit(solution)/shard_map/all_to_all | solution.py:380
  30.0 0.7 shard_map.69
  30.7 3.5 %all-to-all-start.1 = ((f32[8,32,256]{2,1,0:T(8,128)}), f32[8,32,256]{2,1,0:T(8,128)S(1)}, u32[]{:S(2)}, u32[]{:S(2)}) async-start(f32[8,32,256]{2,1,0:T(8,128)} %shard_map.69), calls=%async_computation.1 | async-start | bytes 524288 | tf_op jit(solution)/shard_map/all_to_all | solution.py:380
  34.3 10.0 %all-to-all-done.1.modes = f32[8,32,256]{2,1,0:T(8,128)S(1)} async-done(((f32[8,32,256]{2,1,0:T(8,128)}), f32[8,32,256]{2,1,0:T(8,128)S(1)}, u32[]{:S(2)}, u32[]{:S(2)}) %all-to-all-start.1) | async-done | bytes 262176 | tf_op jit(solution)/shard_map/all_to_all | solution.py:380
  44.2 2.1 %shard_map.70 = (f32[8,48,128]{2,1,0:T(8,128)}, f32[40,256]{1,0:T(8,128)}, f32[40,256]{1,0:T(8,128)}) custom-call(s32[1]{0:T(128)} %bitcast.day, f32[8,56,256]{2,1,0:T(8,128)S(1)} %all_to_all.45.arrived, f32[8,32,256]{2,1,0:T(8,128)S(1)} %all-to-all-done.1.modes, f32[8,128,256]{2,1,0:T(8,128)S(1)} %copy-done.2, s32[8,256]{1,0:T(8,128)S(1)} %copy-done.9), custom_call_target="tpu_custom_call" | custom-call | flops 1000000 | bytes 1000000 | tf_op jit(solution)/shard_map/pallas_call | solution.py:97
  46.3 0.7 copy-done.3
  47.0 11.9 %all-to-all-start.2 = ((f32[8,48,128]{2,1,0:T(8,128)}), f32[8,48,128]{2,1,0:T(8,128)S(1)}, u32[]{:S(2)}, u32[]{:S(2)}) async-start(f32[8,48,128]{2,1,0:T(8,128)} %get-tuple-element.34), calls=%async_computation.2 | async-start | bytes 393216 | tf_op jit(solution)/shard_map/all_to_all | solution.py:380
  59.0 6.4 %all-to-all-done.2.arrived = f32[8,48,128]{2,1,0:T(8,128)S(1)} async-done(((f32[8,48,128]{2,1,0:T(8,128)}), f32[8,48,128]{2,1,0:T(8,128)S(1)}, u32[]{:S(2)}, u32[]{:S(2)}) %all-to-all-start.2) | async-done | bytes 196640 | tf_op jit(solution)/shard_map/all_to_all | solution.py:380
  65.4 0.7 shard_map.71
  66.1 6.8 %all-to-all-start.3 = ((f32[8,48,128]{2,1,0:T(8,128)}), f32[8,48,128]{2,1,0:T(8,128)}, u32[]{:S(2)}, u32[]{:S(2)}) async-start(f32[8,48,128]{2,1,0:T(8,128)} %shard_map.71), calls=%async_computation.3 | async-start | bytes 393216 | tf_op jit(solution)/shard_map/all_to_all | solution.py:380
  73.0 5.7 %collective-permute-start = (f32[40,256]{1,0:T(8,128)}, f32[40,256]{1,0:T(8,128)S(1)}, u32[]{:S(2)}, u32[]{:S(2)}) collective-permute-start(f32[40,256]{1,0:T(8,128)} %get-tuple-element.38), channel_id=1, source_target_pairs={{0,8},{8,16},{16,24},{24,32},{32,40},{40,48},{48,56},{56,64},{64,7... | collective-permute-start | bytes 122888 | tf_op jit(solution)/shard_map/ppermute | solution.py:387
  78.7 1.9 %collective-permute-start.1 = (f32[40,256]{1,0:T(8,128)}, f32[40,256]{1,0:T(8,128)S(1)}, u32[]{:S(2)}, u32[]{:S(2)}) collective-permute-start(f32[40,256]{1,0:T(8,128)} %get-tuple-element.39), channel_id=1, source_target_pairs={{8,0},{16,8},{24,16},{32,24},{40,32},{48,40},{56,48},{64,56},{72,6... | collective-permute-start | bytes 122888 | tf_op jit(solution)/shard_map/ppermute | solution.py:387
  80.6 0.7 select_add_fusion.band
  81.3 0.0 copy-start.4
  81.3 0.3 copy.10
  81.7 0.0 collective-permute-done.above
  81.7 2.9 %collective-permute-done.1.below = f32[40,256]{1,0:T(8,128)S(1)} collective-permute-done((f32[40,256]{1,0:T(8,128)}, f32[40,256]{1,0:T(8,128)S(1)}, u32[]{:S(2)}, u32[]{:S(2)}) %collective-permute-start.1) | collective-permute-done | bytes 40992 | tf_op jit(solution)/shard_map/ppermute | solution.py:387
  84.6 0.2 shard_map.72.smooth
  84.8 0.0 copy-start.5
  84.9 0.7 copy-done.5
  85.6 0.0 all-to-all-done.3.arrived
  85.6 0.9 copy-done.6
  86.5 5.6 %shard_map.73 = (f32[8,128,256]{2,1,0:T(8,128)S(1)}, f32[8,40,256]{2,1,0:T(8,128)S(1)}) custom-call(s32[1]{0:T(128)} %bitcast.day, f32[8,48,128]{2,1,0:T(8,128)} %all-to-all-done.3.arrived, f32[256,128]{1,0:T(8,128)S(1)} %slice.48.band, f32[8,32,256]{2,1,0:T(8,128)S(1)} %copy-done.6, f32[8,128,256]{2,1,0:T(8,128)S(1)} %copy-done.2, ...), custom_call_target="tpu_custom_call" | custom-call | flops 1000000 | bytes 1000000 | tf_op jit(solution)/shard_map/pallas_call | solution.py:97
  92.1 1.0 copy-done.7
  93.1 15.6 %all_to_all.46.arrived = f32[8,40,256]{2,1,0:T(8,128)S(1)} all-to-all(f32[8,40,256]{2,1,0:T(8,128)S(1)} %get-tuple-element.43), channel_id=1, replica_groups=mesh['zlo'=4,'y'=8,'core'=2,'x'=4,'zhi'=2] {'x','zhi'}, dimensions={0} | all-to-all | bytes 655360 | tf_op jit(solution)/shard_map/all_to_all | solution.py:380
  108.8 0.7 shard_map.74
  109.5 3.7 %all-to-all-start.5 = ((f32[8,32,256]{2,1,0:T(8,128)}), f32[8,32,256]{2,1,0:T(8,128)S(1)}, u32[]{:S(2)}, u32[]{:S(2)}) async-start(f32[8,32,256]{2,1,0:T(8,128)} %shard_map.74), calls=%async_computation.5 | async-start | bytes 524288 | tf_op jit(solution)/shard_map/all_to_all | solution.py:380
  113.2 0.8 shard_map.75.factor.scale
  114.1 9.3 %all-to-all-done.5.modes = f32[8,32,256]{2,1,0:T(8,128)S(1)} async-done(((f32[8,32,256]{2,1,0:T(8,128)}), f32[8,32,256]{2,1,0:T(8,128)S(1)}, u32[]{:S(2)}, u32[]{:S(2)}) %all-to-all-start.5) | async-done | bytes 262176 | tf_op jit(solution)/shard_map/all_to_all | solution.py:380
  123.4 1.2 copy-done.8
  124.6 2.6 %shard_map.76 = (f32[8,40,128]{2,1,0:T(8,128)S(1)}, f32[40,256]{1,0:T(8,128)S(1)}, f32[40,256]{1,0:T(8,128)S(1)}) custom-call(f32[8,32,256]{2,1,0:T(8,128)S(1)} %all-to-all-done.5.modes, f32[8,128,256]{2,1,0:T(8,128)S(1)} %copy-done.8, s32[8,256]{1,0:T(8,128)S(1)} %copy-done.9, f32[32,128]{1,0:T(8,128)S(1)} %shard_map.75.factor.scale), custom_call_target="tpu_custom_call" | custom-call | flops 1000000 | bytes 1000000 | tf_op jit(solution)/shard_map/pallas_call | solution.py:97
  127.2 12.0 %all_to_all.47.arrived = f32[8,40,128]{2,1,0:T(8,128)S(1)} all-to-all(f32[8,40,128]{2,1,0:T(8,128)S(1)} %get-tuple-element.45), channel_id=1, replica_groups=mesh['zlo'=4,'y'=8,'core'=2,'x'=4,'zhi'=2] {'zlo','core'}, dimensions={0} | all-to-all | bytes 327680 | tf_op jit(solution)/shard_map/all_to_all | solution.py:380
  139.2 0.7 shard_map.77
  139.9 4.7 %all-to-all-start.7 = ((f32[8,40,128]{2,1,0:T(8,128)}), f32[8,40,128]{2,1,0:T(8,128)S(1)}, u32[]{:S(2)}, u32[]{:S(2)}) async-start(f32[8,40,128]{2,1,0:T(8,128)} %shard_map.77), calls=%async_computation.7 | async-start | bytes 327680 | tf_op jit(solution)/shard_map/all_to_all | solution.py:380
  144.5 5.0 %collective-permute-start.2 = (f32[40,256]{1,0:T(8,128)S(1)}, f32[40,256]{1,0:T(8,128)S(1)}, u32[]{:S(2)}, u32[]{:S(2)}) collective-permute-start(f32[40,256]{1,0:T(8,128)S(1)} %get-tuple-element.49), channel_id=1, source_target_pairs={{0,8},{8,16},{16,24},{24,32},{32,40},{40,48},{48,56},{56,64},{64,7... | collective-permute-start | bytes 122888 | tf_op jit(solution)/shard_map/ppermute | solution.py:387
  149.6 1.9 %collective-permute-start.3 = (f32[40,256]{1,0:T(8,128)S(1)}, f32[40,256]{1,0:T(8,128)S(1)}, u32[]{:S(2)}, u32[]{:S(2)}) collective-permute-start(f32[40,256]{1,0:T(8,128)S(1)} %get-tuple-element.50), channel_id=1, source_target_pairs={{8,0},{16,8},{24,16},{32,24},{40,32},{48,40},{56,48},{64,56},{72,6... | collective-permute-start | bytes 122888 | tf_op jit(solution)/shard_map/ppermute | solution.py:387
  151.5 0.0 collective-permute-done.2.above
  151.6 3.6 %collective-permute-done.3.below = f32[40,256]{1,0:T(8,128)S(1)} collective-permute-done((f32[40,256]{1,0:T(8,128)S(1)}, f32[40,256]{1,0:T(8,128)S(1)}, u32[]{:S(2)}, u32[]{:S(2)}) %collective-permute-start.3) | collective-permute-done | bytes 40992 | tf_op jit(solution)/shard_map/ppermute | solution.py:387
  155.1 0.2 shard_map.78.smooth
  155.4 0.0 all-to-all-done.7.arrived
  155.4 0.7 shard_map.79
  156.1 3.5 %all-to-all-start.8 = ((f32[8,32,128]{2,1,0:T(8,128)}), f32[8,32,128]{2,1,0:T(8,128)S(1)}, u32[]{:S(2)}, u32[]{:S(2)}) async-start(f32[8,32,128]{2,1,0:T(8,128)} %get-tuple-element.52.raw), calls=%async_computation.8 | async-start | bytes 262144 | tf_op jit(solution)/shard_map/all_to_all | solution.py:380
  159.6 2.3 %shard_map.80 = (f32[128,32]{1,0:T(8,128)S(1)}, f32[32,32]{1,0:T(8,128)S(1)}, f32[32,32]{1,0:T(8,128)S(1)}) custom-call(f32[8,32,128]{2,1,0:T(8,128)} %get-tuple-element.52.raw, f32[8,128]{1,0:T(8,128)S(1)} %get-tuple-element.53.extra, f32[512,128]{1,0:T(8,128)S(1)} %select_add_fusion.band, f32[32,128]{1,0:T(8,128)S(1)} %shard_map.75.factor.scale), custom_call_target="tpu_custom_call" | custom-call | flops 1000000 | bytes 1000000 | tf_op jit(solution)/shard_map/pallas_call | solution.py:97
  162.0 2.1 %shard_map.81.filled_in = f32[128,8,256]{2,1,0:T(8,128)} custom-call(f32[128,32]{1,0:T(8,128)S(1)} %get-tuple-element.56.mixed, f32[8,32,256]{2,1,0:T(8,128)S(1)} %shard_map.78.smooth, f32[128,8,256]{2,1,0:T(8,128)S(1)} %copy-done.1, s32[128,8,256]{2,1,0:T(8,128)S(1)} %copy-done, s32[8,256]{1,0:T(8,128)S(1)} %copy-done.9), custom_call_target="tpu_custom_call" | custom-call | flops 1000000 | bytes 1000000 | tf_op jit(solution)/shard_map/pallas_call | solution.py:97
  164.1 4.8 %all-to-all-done.8.arrived = f32[8,32,128]{2,1,0:T(8,128)S(1)} async-done(((f32[8,32,128]{2,1,0:T(8,128)}), f32[8,32,128]{2,1,0:T(8,128)S(1)}, u32[]{:S(2)}, u32[]{:S(2)}) %all-to-all-start.8) | async-done | bytes 131104 | tf_op jit(solution)/shard_map/all_to_all | solution.py:380
  168.9 3.0 %shard_map.82 = (f32[32,128]{1,0:T(8,128)}, f32[128,8,256]{2,1,0:T(8,128)}) custom-call(s32[1]{0:T(128)} %bitcast.day, f32[8,32,128]{2,1,0:T(8,128)S(1)} %all-to-all-done.8.arrived, f32[512,128]{1,0:T(8,128)S(1)} %select_add_fusion.band, f32[32,32]{1,0:T(8,128)S(1)} %get-tuple-element.54.factor, ...), custom_call_target="tpu_custom_call", output_to_operand_aliasing={{1}: (12, {})} | custom-call | flops 1000000 | bytes 1000000 | tf_op jit(solution)/shard_map/pallas_call | solution.py:97
  (23 shorter events, 0.1 us)
Async XLA Ops:
  3.9 40.3 %copy-start.2 = (f32[8,128,256]{2,1,0:T(8,128)S(1)}, f32[8,128,256]{2,1,0:T(8,128)}, u32[]{:S(2)}) copy-start(f32[8,128,256]{2,1,0:T(8,128)} %get-tuple-element.33.filled.first) | copy-start | bytes 3145732
  30.7 13.5 %copy-start.9 = (s32[8,256]{1,0:T(8,128)S(1)}, s32[8,256]{1,0:T(8,128)}, u32[]{:S(2)}) copy-start(s32[8,256]{1,0:T(8,128)} %land.13) | copy-start | bytes 24580
  30.7 13.5 %all-to-all-start.1 = ((f32[8,32,256]{2,1,0:T(8,128)}), f32[8,32,256]{2,1,0:T(8,128)S(1)}, u32[]{:S(2)}, u32[]{:S(2)}) async-start(f32[8,32,256]{2,1,0:T(8,128)} %shard_map.69), calls=%async_computation.1 | async-start | bytes 524288 | tf_op jit(solution)/shard_map/all_to_all | solution.py:380
  44.2 14.8 %copy-start.10 = (f32[128,7]{0,1:T(8,128)S(1)}, f32[128,7]{0,1:T(8,128)}, u32[]{:S(2)}) copy-start(f32[128,7]{0,1:T(8,128)} %param.9) | copy-start | bytes 10756
  46.3 0.7 copy-start.3
  47.0 34.3 %copy-start = (s32[128,8,256]{2,1,0:T(8,128)S(1)}, s32[128,8,256]{2,1,0:T(8,128)}, u32[]{:S(2)}) copy-start(s32[128,8,256]{2,1,0:T(8,128)} %missing.1) | copy-start | bytes 3145732
  47.0 18.4 %all-to-all-start.2 = ((f32[8,48,128]{2,1,0:T(8,128)}), f32[8,48,128]{2,1,0:T(8,128)S(1)}, u32[]{:S(2)}, u32[]{:S(2)}) async-start(f32[8,48,128]{2,1,0:T(8,128)} %get-tuple-element.34), calls=%async_computation.2 | async-start | bytes 393216 | tf_op jit(solution)/shard_map/all_to_all | solution.py:380
  66.1 19.4 %all-to-all-start.3 = ((f32[8,48,128]{2,1,0:T(8,128)}), f32[8,48,128]{2,1,0:T(8,128)}, u32[]{:S(2)}, u32[]{:S(2)}) async-start(f32[8,48,128]{2,1,0:T(8,128)} %shard_map.71), calls=%async_computation.3 | async-start | bytes 393216 | tf_op jit(solution)/shard_map/all_to_all | solution.py:380
  73.0 8.7 %collective-permute-start = (f32[40,256]{1,0:T(8,128)}, f32[40,256]{1,0:T(8,128)S(1)}, u32[]{:S(2)}, u32[]{:S(2)}) collective-permute-start(f32[40,256]{1,0:T(8,128)} %get-tuple-element.38), channel_id=1, source_target_pairs={{0,8},{8,16},{16,24},{24,32},{32,40},{40,48},{48,56},{56,64},{64,7... | collective-permute-start | bytes 122888 | tf_op jit(solution)/shard_map/ppermute | solution.py:387
  78.7 5.9 %collective-permute-start.1 = (f32[40,256]{1,0:T(8,128)}, f32[40,256]{1,0:T(8,128)S(1)}, u32[]{:S(2)}, u32[]{:S(2)}) collective-permute-start(f32[40,256]{1,0:T(8,128)} %get-tuple-element.39), channel_id=1, source_target_pairs={{8,0},{16,8},{24,16},{32,24},{40,32},{48,40},{56,48},{64,56},{72,6... | collective-permute-start | bytes 122888 | tf_op jit(solution)/shard_map/ppermute | solution.py:387
  81.3 3.3 %copy-start.4 = (f32[8,32,256]{2,1,0:T(8,128)S(1)}, f32[8,32,256]{2,1,0:T(8,128)}, u32[]{:S(2)}) copy-start(f32[8,32,256]{2,1,0:T(8,128)} %copy-done.3) | copy-start | bytes 786436
  84.8 0.7 copy-start.5
  85.6 1.0 copy-start.6
  92.1 1.0 copy-start.7
  109.5 13.9 %all-to-all-start.5 = ((f32[8,32,256]{2,1,0:T(8,128)}), f32[8,32,256]{2,1,0:T(8,128)S(1)}, u32[]{:S(2)}, u32[]{:S(2)}) async-start(f32[8,32,256]{2,1,0:T(8,128)} %shard_map.74), calls=%async_computation.5 | async-start | bytes 524288 | tf_op jit(solution)/shard_map/all_to_all | solution.py:380
  123.4 1.2 copy-start.8
  139.2 20.4 %copy-start.1 = (f32[128,8,256]{2,1,0:T(8,128)S(1)}, f32[128,8,256]{2,1,0:T(8,128)}, u32[]{:S(2)}) copy-start(f32[128,8,256]{2,1,0:T(8,128)} %observed.1) | copy-start | bytes 3145732
  139.9 15.5 %all-to-all-start.7 = ((f32[8,40,128]{2,1,0:T(8,128)}), f32[8,40,128]{2,1,0:T(8,128)S(1)}, u32[]{:S(2)}, u32[]{:S(2)}) async-start(f32[8,40,128]{2,1,0:T(8,128)} %shard_map.77), calls=%async_computation.7 | async-start | bytes 327680 | tf_op jit(solution)/shard_map/all_to_all | solution.py:380
  144.5 7.0 %collective-permute-start.2 = (f32[40,256]{1,0:T(8,128)S(1)}, f32[40,256]{1,0:T(8,128)S(1)}, u32[]{:S(2)}, u32[]{:S(2)}) collective-permute-start(f32[40,256]{1,0:T(8,128)S(1)} %get-tuple-element.49), channel_id=1, source_target_pairs={{0,8},{8,16},{16,24},{24,32},{32,40},{40,48},{48,56},{56,64},{64,7... | collective-permute-start | bytes 122888 | tf_op jit(solution)/shard_map/ppermute | solution.py:387
  149.6 5.5 %collective-permute-start.3 = (f32[40,256]{1,0:T(8,128)S(1)}, f32[40,256]{1,0:T(8,128)S(1)}, u32[]{:S(2)}, u32[]{:S(2)}) collective-permute-start(f32[40,256]{1,0:T(8,128)S(1)} %get-tuple-element.50), channel_id=1, source_target_pairs={{8,0},{16,8},{24,16},{32,24},{40,32},{48,40},{56,48},{64,56},{72,6... | collective-permute-start | bytes 122888 | tf_op jit(solution)/shard_map/ppermute | solution.py:387
  156.1 12.8 %all-to-all-start.8 = ((f32[8,32,128]{2,1,0:T(8,128)}), f32[8,32,128]{2,1,0:T(8,128)S(1)}, u32[]{:S(2)}, u32[]{:S(2)}) async-start(f32[8,32,128]{2,1,0:T(8,128)} %get-tuple-element.52.raw), calls=%async_computation.8 | async-start | bytes 262144 | tf_op jit(solution)/shard_map/all_to_all | solution.py:380

commit v4 on v3

--- a/solution.py
+++ b/solution.py
@@ -18,6 +18,7 @@
 exact = lax.Precision.HIGHEST
 smoothing = 0.2
 f32 = jnp.float32
+bf16 = jnp.bfloat16
 
 
 def mul(a, b):
@@ -29,6 +30,46 @@
 def mul_t(a, b):
     return lax.dot_general(
         a, b, (((1,), (1,)), ((), ())), precision=exact, preferred_element_type=f32
+    )
+
+
+def split(x):
+    high = x.astype(bf16)
+    rest = x - high.astype(f32)
+    middle = rest.astype(bf16)
+    return high, middle, (rest - middle.astype(f32)).astype(bf16)
+
+
+def parts_of(a):
+    return jnp.concatenate(split(a), axis=0)
+
+
+def mul_few(stack, b, over=0):
+    rows = stack.shape[0] // 3
+    total = None
+    for i, part in enumerate(split(b)):
+        found = lax.dot_general(
+            stack[: rows * (3 - i)],
+            part,
+            (((1,), (over,)), ((), ())),
+            preferred_element_type=f32,
+        )
+        for j in range(3 - i):
+            piece = found[rows * j : rows * j + rows]
+            total = piece if total is None else total + piece
+    return total
+
+
+def deep_parts_of(a):
+    high, middle, low = split(a)
+    return jnp.concatenate([low, middle, high, middle, high, high], axis=1)
+
+
+def mul_deep(stack, b):
+    high, middle, low = split(b)
+    right = jnp.concatenate([high, middle, low, high, middle, high], axis=0)
+    return lax.dot_general(
+        stack, right, (((1,), (0,)), ((), ())), preferred_element_type=f32
     )
 
 
@@ -120,49 +161,87 @@
     missing_hbm,
     land_hbm,
     basis_hbm,
-    first,
-    out,
+    first_hbm,
+    out_hbm,
     observed,
     missing,
     land,
     basis_t,
     half_0,
     half_1,
+    first,
+    out,
     arrivals,
+    sent,
 ):
-    pairs = (
-        (missing_hbm, missing),
-        (observed_hbm, observed),
-        (land_hbm, land),
-        (basis_hbm, basis_t),
-    )
-    copies = [
-        pltpu.make_async_copy(source, target, arrivals.at[i])
-        for i, (source, target) in enumerate(pairs)
+    parts = 4
+    days = first.shape[1]
+    size = days // parts
+    small = [
+        pltpu.make_async_copy(land_hbm, land, arrivals.at[2 * parts]),
+        pltpu.make_async_copy(basis_hbm, basis_t, arrivals.at[2 * parts + 1]),
     ]
-    for copy in copies:
+    for copy in small:
         copy.start()
+    copies = []
+    for i in range(parts):
+        at = pl.ds(size * i, size)
+        for c, (source, target) in enumerate(
+            ((missing_hbm, missing), (observed_hbm, observed))
+        ):
+            copies.append(
+                pltpu.make_async_copy(
+                    source.at[at], target.at[at], arrivals.at[2 * i + c]
+                )
+            )
+            copies[-1].start()
     d = day[0]
     halves = (half_0, half_1)
     out[:, K:, :] = jnp.zeros((8, HALO, out.shape[2]), f32)
-    for copy in copies:
+    for copy in small:
         copy.wait()
     ocean = 1.0 - land[...].astype(f32)
+    for i in range(parts):
+        copies[2 * i].wait()
+        copies[2 * i + 1].wait()
+        now = slice(size * i, size * i + size)
+        for c, half in enumerate(halves):
+            at = slice(LANES * c, LANES * c + LANES)
+            tile = jnp.where(missing[now, :, at] == 1, f32(0.0), observed[now, :, at])
+            tile = tile * ocean[None, :, at]
+            half[8 * size * i : 8 * size * (i + 1), :] = tile.reshape(8 * size, LANES)
     low, high = jnp.maximum(d - 1, 0), jnp.minimum(d + 1, 7)
-    days = first.shape[1]
-    for c, half in enumerate(halves):
-        at = slice(LANES * c, LANES * c + LANES)
-        tile = jnp.where(missing[:, :, at] == 1, f32(0.0), observed[:, :, at])
-        half[...] = (tile * ocean[None, :, at]).reshape(8 * days, LANES)
     for t in range(RADIUS):
         for target, source in ((low, t), (high, days - RADIUS + t)):
             tile = [half[8 * source : 8 * source + 8, :] for half in halves]
             out[target, K + 8 * t : K + 8 * t + 8, :] = jnp.concatenate(tile, axis=1)
-    weights_t = basis_t[...]
+    weights = parts_of(basis_t[...])
+    copies = []
     for r in range(8):
         filled = rows_of(halves, r, days)
         first[r] = filled
-        out[r, :K, :] = mul(weights_t, filled)
+        out[r, :K, :] = mul_few(weights, filled)
+        copies.append(pltpu.make_async_copy(out.at[r], out_hbm.at[r], sent.at[r]))
+        copies[-1].start()
+        copies.append(pltpu.make_async_copy(first.at[r], first_hbm.at[r], sent.at[8 + r]))
+        copies[-1].start()
+    for copy in copies:
+        copy.wait()
+
+
+def gap_body(missing_hbm, gap_hbm, missing, half_0, half_1, gap, arrivals):
+    copy = pltpu.make_async_copy(missing_hbm, missing, arrivals.at[0])
+    copy.start()
+    copy.wait()
+    days = missing.shape[0]
+    for c, half in enumerate((half_0, half_1)):
+        tile = missing[:, :, LANES * c : LANES * c + LANES].astype(f32)
+        half[...] = tile.reshape(8 * days, LANES)
+    for r in range(8):
+        gap[r] = rows_of((half_0, half_1), r, days)
+    copy = pltpu.make_async_copy(gap, gap_hbm, arrivals.at[1])
+    copy.start()
+    copy.wait()
 
 
 def add_rows_body(arrived, out):
@@ -209,7 +288,7 @@
     for r in range(8):
         modes_u = mul(scale, modes[r])
         right = jnp.concatenate([filled[r], modes_u, pad], axis=0)
-        total = total + mul_t(modes_u, right)
+        total = total + mul_few(parts_of(modes_u), right, 1)
     packed = pack_rows(total[:, LANES:])
     for j in range(out.shape[0]):
         out[j, :K, :] = total[:, :LANES]
@@ -236,7 +315,7 @@
         modes_u = modes[r]
         days_near = rows_of((halo_0, halo_1), r, 8)
         right = jnp.concatenate([filled[r], modes_u, days_near, pad], axis=0)
-        total = total + mul_t(modes_u, right)
+        total = total + mul_few(parts_of(modes_u), right, 1)
     extra = total[:, LANES:]
     packed = extra[:16] + pltpu.roll(extra[16:], 64, 1)
     for j in range(out.shape[0]):
@@ -270,27 +349,56 @@
         out[r] = centre * here + smoothing * spread
 
 
-def refill_body(day, arrived, band, smooth, first, gap, land, filled, out):
+def refill_body(
+    day,
+    arrived,
+    band,
+    smooth_hbm,
+    first_hbm,
+    gap_hbm,
+    land,
+    filled_hbm,
+    out,
+    smooth,
+    first,
+    gap,
+    filled,
+    arrivals,
+    sent,
+):
+    pairs = ((smooth_hbm, smooth), (first_hbm, first), (gap_hbm, gap))
+    copies = [
+        pltpu.make_async_copy(source, target, arrivals.at[i])
+        for i, (source, target) in enumerate(pairs)
+    ]
+    for copy in copies:
+        copy.start()
     total = total_of(arrived)
     extra = jnp.concatenate([total[K:], pltpu.roll(total[K:], 64, 1)], axis=0)
     raw = jnp.concatenate([total[:K], extra], axis=1)
     tempered_t = mul(raw, band[...]).T
     factor = inverse_factor(extra)
     weights_t = mul(factor, total[:K])
-    mixed = mul(tempered_t, mul(factor.T, factor))
-    d = day[0]
-    low, high = jnp.maximum(d - 1, 0), jnp.minimum(d + 1, 7)
+    mixed = deep_parts_of(mul(tempered_t, mul(factor.T, factor)))
+    weights = parts_of(weights_t)
     days, cols = filled.shape[1:]
     packed = pack_gram(weights_t)
     for j in range(8):
         out[j, K:, :LANES] = packed
         out[j, K:, LANES:] = jnp.zeros((8, cols - LANES), f32)
     ocean = 1.0 - land[...].astype(f32)
-    for r in range(8):
-        surface = mul(mixed, smooth[r])
+    for copy in copies:
+        copy.wait()
+    copies = []
+    for r in range(8):
+        surface = mul_deep(mixed, smooth[r])
         now = jnp.where(gap[r] == 1, surface * ocean[r : r + 1], first[r])
         filled[r] = now
-        out[r, :K, :] = mul(weights_t, now)
+        copies.append(pltpu.make_async_copy(filled.at[r], filled_hbm.at[r], sent.at[r]))
+        copies[-1].start()
+        out[r, :K, :] = mul_few(weights, now)
+    for copy in copies:
+        copy.wait()
 
 
 def last_weights_body(raw, extra, band, scale, mixed, right, factor):
@@ -305,9 +413,9 @@
 def last_fill_body(mixed, smooth, observed, missing, land, out, *halves):
     days = observed.shape[0]
     ocean = 1.0 - land[...].astype(f32)
-    mix = mixed[...]
-    for r in range(8):
-        surface = mul(mix, smooth[r])
+    mix = deep_parts_of(mixed[...])
+    for r in range(8):
+        surface = mul_deep(mix, smooth[r])
         for c, half in enumerate(halves):
             half[pl.ds(r, days, stride=8), :] = surface[:, LANES * c : LANES * c + LANES]
     for c, half in enumerate(halves):
@@ -427,23 +535,39 @@
         smooth = call(smooth_body, block, (modes, above, below, land))
         return lax.optimization_barrier((joint, smooth))
 
+    slab = pltpu.VMEM((days, rows, cols), f32)
+    turned = pltpu.VMEM((rows, days, cols), f32)
+    mask = pltpu.VMEM((days, rows, cols), jnp.int32)
+
     first, part = call(
         start_body,
         [(rows, days, cols), (rows, K + HALO, cols)],
         (day, observed, missing, land, basis_start.T),
         [
-            pltpu.VMEM((days, rows, cols), f32),
-            pltpu.VMEM((days, rows, cols), jnp.int32),
+            slab,
+            mask,
             pltpu.VMEM((rows, cols), jnp.int32),
             pltpu.VMEM((K, days), f32),
             *halves,
-            pltpu.SemaphoreType.DMA((4,)),
+            turned,
+            pltpu.VMEM((rows, K + HALO, cols), f32),
+            pltpu.SemaphoreType.DMA((10,)),
+            pltpu.SemaphoreType.DMA((16,)),
         ],
         limit=56,
         anywhere=(1, 2, 3, 4),
-    )
-    gap, part = lax.optimization_barrier((missing, part))
-    gap = gap.transpose(1, 0, 2)
+        out_any=(0, 1),
+    )
+    later, part = lax.optimization_barrier((missing, part))
+    gap = call(
+        gap_body,
+        (rows, days, cols),
+        (later,),
+        [mask, *halves, turned, pltpu.SemaphoreType.DMA((2,))],
+        limit=56,
+        anywhere=(0,),
+        out_any=(0,),
+    )
     arrived = swap(part, DAY)
     modes = swap(call(add_rows_body, block, (arrived,)), DAY)
     joint, *edges = call(
@@ -458,6 +582,17 @@
         refill_body,
         [(rows, days, cols), (rows, K + 8, cols)],
         (day, joint, band[: 2 * LANES], smooth, first, gap, land),
+        [
+            pltpu.VMEM(block, f32),
+            turned,
+            turned,
+            turned,
+            pltpu.SemaphoreType.DMA((3,)),
+            pltpu.SemaphoreType.DMA((8,)),
+        ],
+        limit=56,
+        anywhere=(3, 4, 5),
+        out_any=(0,),
     )
     arrived = swap(part, DAY)
     modes = swap(call(add_rows_body, block, (arrived,)), DAY)

time: 174 us -> 172 us (0.989)
  local copies, waits for them, and re-layouts: 4.96 us -> 2.76 us
  waiting for transfers between devices: 37 us -> 35.2 us
    ppermute x4, waiting for transfers between devices: 6.48 us -> 3.57 us  [near_rows(): return (lax.ppermute(edge_high, PIX, up), lax.ppermute(edge_low, PIX, down))]
    unnamed x22 -> x18, local copies, waits for them, and re-layouts: 4.58 us -> 2.07 us
    pallas_call x15 -> x16, Pallas kernels: 25.9 us -> 26.2 us  [call(): pl.pallas_call(body, out_shape=shapes if many else shapes[0], in_specs=sp...]
  transfers between devices with their start and end apart: 10 -> 10, of which waited for: 6 -> 5; matrix products, arithmetic and copies ran while one was open for 1% -> 1% of each run, Pallas kernels for 3% -> 4%
where the time goes in v4:
time: 172 us; the launch traced here: 169 us
  blocking collectives  55.3 us (32%)
  starting transfers between devices  48.4 us (28%)
  waiting for transfers between devices  35.2 us (20%)
  Pallas kernels  26.2 us (15%)
  local copies, waits for them, and re-layouts  2.76 us (2%)
    all_to_all x3, blocking collectives, swap(): return lax.all_to_all(blocks, axes, 0, 0)  55.3 us
    all_to_all x6, starting transfers between devices, swap(): return lax.all_to_all(blocks, axes, 0, 0)  33.8 us
    all_to_all x6, waiting for transfers between devices, swap(): return lax.all_to_all(blocks, axes, 0, 0)  31.6 us
    pallas_call x16, Pallas kernels, call(): pl.pallas_call(body, out_shape=shapes if many else shapes[0], in_specs=sp...  26.2 us
    ppermute x4, starting transfers between devices, near_rows(): return (lax.ppermute(edge_high, PIX, up), lax.ppermute(edge_low, PIX, down))  14.6 us
    ppermute x4, waiting for transfers between devices, near_rows(): return (lax.ppermute(edge_high, PIX, up), lax.ppermute(edge_low, PIX, down))  3.57 us
  transfers between devices with their start and end apart: 10, of which 5 were waited for; matrix products, arithmetic and copies ran while one was open for 1% of the time, Pallas kernels for 4%

profile of v4, /device:TPU:1, one launch (start us, length us, event | category | flops | bytes accessed | tf_op | source)
XLA Modules:
  0.0 169.4 jit_solution(6071719752612707746)
XLA Ops:
  0.6 3.2 %shard_map.68 = (f32[8,128,256]{2,1,0:T(8,128)}, f32[8,56,256]{2,1,0:T(8,128)}) custom-call(s32[1]{0:T(128)} %bitcast.day, f32[128,8,256]{2,1,0:T(8,128)} %observed.1, s32[128,8,256]{2,1,0:T(8,128)} %missing.1, s32[8,256]{1,0:T(8,128)} %land.13, f32[32,128]{1,0:T(8,128)} %bitcast.18), custom_call_target="tpu_custom_call" | custom-call | flops 1000000 | bytes 1000000 | tf_op jit(solution)/shard_map/pallas_call | solution.py:138
  3.9 0.0 copy-start.2
  3.9 26.0 %all_to_all.45.arrived = f32[8,56,256]{2,1,0:T(8,128)S(1)} all-to-all(f32[8,56,256]{2,1,0:T(8,128)} %get-tuple-element.32), channel_id=1, replica_groups=mesh['zlo'=4,'y'=8,'core'=2,'x'=4,'zhi'=2] {'x','zhi'}, dimensions={0} | all-to-all | bytes 917504 | tf_op jit(solution)/shard_map/all_to_all | solution.py:488
  29.9 0.7 shard_map.69
  30.6 3.5 %all-to-all-start.1 = ((f32[8,32,256]{2,1,0:T(8,128)}), f32[8,32,256]{2,1,0:T(8,128)S(1)}, u32[]{:S(2)}, u32[]{:S(2)}) async-start(f32[8,32,256]{2,1,0:T(8,128)} %shard_map.69), calls=%async_computation.1 | async-start | bytes 524288 | tf_op jit(solution)/shard_map/all_to_all | solution.py:488
  34.2 10.0 %all-to-all-done.1.modes = f32[8,32,256]{2,1,0:T(8,128)S(1)} async-done(((f32[8,32,256]{2,1,0:T(8,128)}), f32[8,32,256]{2,1,0:T(8,128)S(1)}, u32[]{:S(2)}, u32[]{:S(2)}) %all-to-all-start.1) | async-done | bytes 262176 | tf_op jit(solution)/shard_map/all_to_all | solution.py:488
  44.2 0.0 copy-done.5
  44.2 1.6 shard_map.70
  45.8 11.8 %all-to-all-start.2 = ((f32[8,48,128]{2,1,0:T(8,128)}), f32[8,48,128]{2,1,0:T(8,128)S(1)}, u32[]{:S(2)}, u32[]{:S(2)}) async-start(f32[8,48,128]{2,1,0:T(8,128)} %get-tuple-element.34), calls=%async_computation.2 | async-start | bytes 393216 | tf_op jit(solution)/shard_map/all_to_all | solution.py:488
  57.6 0.7 copy-done.8
  58.3 5.8 %all-to-all-done.2.arrived = f32[8,48,128]{2,1,0:T(8,128)S(1)} async-done(((f32[8,48,128]{2,1,0:T(8,128)}), f32[8,48,128]{2,1,0:T(8,128)S(1)}, u32[]{:S(2)}, u32[]{:S(2)}) %all-to-all-start.2) | async-done | bytes 196640 | tf_op jit(solution)/shard_map/all_to_all | solution.py:488
  64.1 0.7 shard_map.71
  64.8 6.8 %all-to-all-start.3 = ((f32[8,48,128]{2,1,0:T(8,128)}), f32[8,48,128]{2,1,0:T(8,128)S(1)}, u32[]{:S(2)}, u32[]{:S(2)}) async-start(f32[8,48,128]{2,1,0:T(8,128)} %shard_map.71), calls=%async_computation.3 | async-start | bytes 393216 | tf_op jit(solution)/shard_map/all_to_all | solution.py:488
  71.6 5.7 %collective-permute-start = (f32[40,256]{1,0:T(8,128)S(1)}, f32[40,256]{1,0:T(8,128)S(1)}, u32[]{:S(2)}, u32[]{:S(2)}) collective-permute-start(f32[40,256]{1,0:T(8,128)S(1)} %get-tuple-element.38), channel_id=1, source_target_pairs={{0,8},{8,16},{16,24},{24,32},{32,40},{40,48},{48,56},{56,64},{64,7... | collective-permute-start | bytes 122888 | tf_op jit(solution)/shard_map/ppermute | solution.py:495
  77.3 1.9 %collective-permute-start.1 = (f32[40,256]{1,0:T(8,128)S(1)}, f32[40,256]{1,0:T(8,128)S(1)}, u32[]{:S(2)}, u32[]{:S(2)}) collective-permute-start(f32[40,256]{1,0:T(8,128)S(1)} %get-tuple-element.39), channel_id=1, source_target_pairs={{8,0},{16,8},{24,16},{32,24},{40,32},{48,40},{56,48},{64,56},{72,6... | collective-permute-start | bytes 122888 | tf_op jit(solution)/shard_map/ppermute | solution.py:495
  79.2 0.7 select_add_fusion.band
  79.9 0.7 slice.48.band
  80.6 2.5 %shard_map.73.gap_hbm = f32[8,128,256]{2,1,0:T(8,128)} custom-call(s32[128,8,256]{2,1,0:T(8,128)} %missing.1), custom_call_target="tpu_custom_call" | custom-call | flops 1000000 | bytes 1000000 | tf_op jit(solution)/shard_map/pallas_call | solution.py:138
  83.1 0.0 collective-permute-done.above
  83.1 0.0 collective-permute-done.1.below
  83.1 0.2 shard_map.72.smooth_hbm
  83.3 0.0 copy-start.3
  83.4 0.7 copy-done.3
  84.1 0.0 all-to-all-done.3.arrived
  84.1 0.7 copy-done.7
  84.7 5.0 %shard_map.74 = (f32[8,128,256]{2,1,0:T(8,128)}, f32[8,40,256]{2,1,0:T(8,128)}) custom-call(s32[1]{0:T(128)} %bitcast.day, f32[8,48,128]{2,1,0:T(8,128)} %copy-done.7, f32[256,128]{1,0:T(8,128)} %slice.48.band, f32[8,32,256]{2,1,0:T(8,128)} %copy-done.3, f32[8,128,256]{2,1,0:T(8,128)} %get-tuple-element.33.filled.first_hbm, ...), custom_call_target="tpu_custom_call" | custom-call | flops 1000000 | bytes 1000000 | tf_op jit(solution)/shard_map/pallas_call | solution.py:138
  89.8 17.6 %all_to_all.46.arrived = f32[8,40,256]{2,1,0:T(8,128)S(1)} all-to-all(f32[8,40,256]{2,1,0:T(8,128)} %get-tuple-element.43), channel_id=1, replica_groups=mesh['zlo'=4,'y'=8,'core'=2,'x'=4,'zhi'=2] {'x','zhi'}, dimensions={0} | all-to-all | bytes 655360 | tf_op jit(solution)/shard_map/all_to_all | solution.py:488
  107.4 0.7 shard_map.75
  108.2 3.4 %all-to-all-start.5 = ((f32[8,32,256]{2,1,0:T(8,128)}), f32[8,32,256]{2,1,0:T(8,128)S(1)}, u32[]{:S(2)}, u32[]{:S(2)}) async-start(f32[8,32,256]{2,1,0:T(8,128)} %shard_map.75), calls=%async_computation.5 | async-start | bytes 524288 | tf_op jit(solution)/shard_map/all_to_all | solution.py:488
  111.6 0.0 copy-start.6
  111.6 0.8 shard_map.76.factor.scale
  112.4 10.3 %all-to-all-done.5.modes = f32[8,32,256]{2,1,0:T(8,128)S(1)} async-done(((f32[8,32,256]{2,1,0:T(8,128)}), f32[8,32,256]{2,1,0:T(8,128)S(1)}, u32[]{:S(2)}, u32[]{:S(2)}) %all-to-all-start.5) | async-done | bytes 262176 | tf_op jit(solution)/shard_map/all_to_all | solution.py:488
  122.7 2.2 %shard_map.77 = (f32[8,40,128]{2,1,0:T(8,128)S(1)}, f32[40,256]{1,0:T(8,128)S(1)}, f32[40,256]{1,0:T(8,128)S(1)}) custom-call(f32[8,32,256]{2,1,0:T(8,128)S(1)} %all-to-all-done.5.modes, f32[8,128,256]{2,1,0:T(8,128)S(1)} %copy-done.4, s32[8,256]{1,0:T(8,128)S(1)} %copy-done.6, f32[32,128]{1,0:T(8,128)S(1)} %shard_map.76.factor.scale), custom_call_target="tpu_custom_call" | custom-call | flops 1000000 | bytes 1000000 | tf_op jit(solution)/shard_map/pallas_call | solution.py:138
  124.9 11.7 %all_to_all.47.arrived = f32[8,40,128]{2,1,0:T(8,128)S(1)} all-to-all(f32[8,40,128]{2,1,0:T(8,128)S(1)} %get-tuple-element.45), channel_id=1, replica_groups=mesh['zlo'=4,'y'=8,'core'=2,'x'=4,'zhi'=2] {'zlo','core'}, dimensions={0} | all-to-all | bytes 327680 | tf_op jit(solution)/shard_map/all_to_all | solution.py:488
  136.6 0.7 shard_map.78
  137.3 4.9 %all-to-all-start.7 = ((f32[8,40,128]{2,1,0:T(8,128)}), f32[8,40,128]{2,1,0:T(8,128)S(1)}, u32[]{:S(2)}, u32[]{:S(2)}) async-start(f32[8,40,128]{2,1,0:T(8,128)} %shard_map.78), calls=%async_computation.7 | async-start | bytes 327680 | tf_op jit(solution)/shard_map/all_to_all | solution.py:488
  142.1 5.0 %collective-permute-start.2 = (f32[40,256]{1,0:T(8,128)S(1)}, f32[40,256]{1,0:T(8,128)S(1)}, u32[]{:S(2)}, u32[]{:S(2)}) collective-permute-start(f32[40,256]{1,0:T(8,128)S(1)} %get-tuple-element.49), channel_id=1, source_target_pairs={{0,8},{8,16},{16,24},{24,32},{32,40},{40,48},{48,56},{56,64},{64,7... | collective-permute-start | bytes 122888 | tf_op jit(solution)/shard_map/ppermute | solution.py:495
  147.2 1.9 %collective-permute-start.3 = (f32[40,256]{1,0:T(8,128)S(1)}, f32[40,256]{1,0:T(8,128)S(1)}, u32[]{:S(2)}, u32[]{:S(2)}) collective-permute-start(f32[40,256]{1,0:T(8,128)S(1)} %get-tuple-element.50), channel_id=1, source_target_pairs={{8,0},{16,8},{24,16},{32,24},{40,32},{48,40},{56,48},{64,56},{72,6... | collective-permute-start | bytes 122888 | tf_op jit(solution)/shard_map/ppermute | solution.py:495
  149.1 0.0 collective-permute-done.2.above
  149.1 3.6 %collective-permute-done.3.below = f32[40,256]{1,0:T(8,128)S(1)} collective-permute-done((f32[40,256]{1,0:T(8,128)S(1)}, f32[40,256]{1,0:T(8,128)S(1)}, u32[]{:S(2)}, u32[]{:S(2)}) %collective-permute-start.3) | collective-permute-done | bytes 40992 | tf_op jit(solution)/shard_map/ppermute | solution.py:495
  152.7 0.2 shard_map.79.smooth
  152.9 0.0 all-to-all-done.7.arrived
  153.0 0.7 shard_map.80
  153.6 3.4 %all-to-all-start.8 = ((f32[8,32,128]{2,1,0:T(8,128)}), f32[8,32,128]{2,1,0:T(8,128)S(1)}, u32[]{:S(2)}, u32[]{:S(2)}) async-start(f32[8,32,128]{2,1,0:T(8,128)} %get-tuple-element.52.raw), calls=%async_computation.8 | async-start | bytes 262144 | tf_op jit(solution)/shard_map/all_to_all | solution.py:488
  157.0 2.3 %shard_map.81 = (f32[128,32]{1,0:T(8,128)S(1)}, f32[32,32]{1,0:T(8,128)S(1)}, f32[32,32]{1,0:T(8,128)S(1)}) custom-call(f32[8,32,128]{2,1,0:T(8,128)} %get-tuple-element.52.raw, f32[8,128]{1,0:T(8,128)S(1)} %get-tuple-element.53.extra, f32[512,128]{1,0:T(8,128)S(1)} %select_add_fusion.band, f32[32,128]{1,0:T(8,128)S(1)} %shard_map.76.factor.scale), custom_call_target="tpu_custom_call" | custom-call | flops 1000000 | bytes 1000000 | tf_op jit(solution)/shard_map/pallas_call | solution.py:138
  159.3 1.5 shard_map.82.filled_in
  160.9 5.6 %all-to-all-done.8.arrived = f32[8,32,128]{2,1,0:T(8,128)S(1)} async-done(((f32[8,32,128]{2,1,0:T(8,128)}), f32[8,32,128]{2,1,0:T(8,128)S(1)}, u32[]{:S(2)}, u32[]{:S(2)}) %all-to-all-start.8) | async-done | bytes 131104 | tf_op jit(solution)/shard_map/all_to_all | solution.py:488
  166.4 3.0 %shard_map.83 = (f32[32,128]{1,0:T(8,128)}, f32[128,8,256]{2,1,0:T(8,128)}) custom-call(s32[1]{0:T(128)} %bitcast.day, f32[8,32,128]{2,1,0:T(8,128)S(1)} %all-to-all-done.8.arrived, f32[512,128]{1,0:T(8,128)S(1)} %select_add_fusion.band, f32[32,32]{1,0:T(8,128)S(1)} %get-tuple-element.54.factor, ...), custom_call_target="tpu_custom_call", output_to_operand_aliasing={{1}: (12, {})} | custom-call | flops 1000000 | bytes 1000000 | tf_op jit(solution)/shard_map/pallas_call | solution.py:138
  (19 shorter events, 0.1 us)
Async XLA Ops:
  3.9 40.3 %copy-start.2 = (f32[8,128,256]{2,1,0:T(8,128)S(1)}, f32[8,128,256]{2,1,0:T(8,128)}, u32[]{:S(2)}) copy-start(f32[8,128,256]{2,1,0:T(8,128)} %get-tuple-element.33.filled.first_hbm) | copy-start | bytes 3145732
  30.6 13.5 %copy-start.5 = (s32[8,256]{1,0:T(8,128)S(1)}, s32[8,256]{1,0:T(8,128)}, u32[]{:S(2)}) copy-start(s32[8,256]{1,0:T(8,128)} %land.13) | copy-start | bytes 24580
  30.6 13.5 %all-to-all-start.1 = ((f32[8,32,256]{2,1,0:T(8,128)}), f32[8,32,256]{2,1,0:T(8,128)S(1)}, u32[]{:S(2)}, u32[]{:S(2)}) async-start(f32[8,32,256]{2,1,0:T(8,128)} %shard_map.69), calls=%async_computation.1 | async-start | bytes 524288 | tf_op jit(solution)/shard_map/all_to_all | solution.py:488
  45.8 18.3 %all-to-all-start.2 = ((f32[8,48,128]{2,1,0:T(8,128)}), f32[8,48,128]{2,1,0:T(8,128)S(1)}, u32[]{:S(2)}, u32[]{:S(2)}) async-start(f32[8,48,128]{2,1,0:T(8,128)} %get-tuple-element.34), calls=%async_computation.2 | async-start | bytes 393216 | tf_op jit(solution)/shard_map/all_to_all | solution.py:488
  57.6 0.7 copy-start.8
  64.8 19.3 %all-to-all-start.3 = ((f32[8,48,128]{2,1,0:T(8,128)}), f32[8,48,128]{2,1,0:T(8,128)S(1)}, u32[]{:S(2)}, u32[]{:S(2)}) async-start(f32[8,48,128]{2,1,0:T(8,128)} %shard_map.71), calls=%async_computation.3 | async-start | bytes 393216 | tf_op jit(solution)/shard_map/all_to_all | solution.py:488
  71.6 11.5 %collective-permute-start = (f32[40,256]{1,0:T(8,128)S(1)}, f32[40,256]{1,0:T(8,128)S(1)}, u32[]{:S(2)}, u32[]{:S(2)}) collective-permute-start(f32[40,256]{1,0:T(8,128)S(1)} %get-tuple-element.38), channel_id=1, source_target_pairs={{0,8},{8,16},{16,24},{24,32},{32,40},{40,48},{48,56},{56,64},{64,7... | collective-permute-start | bytes 122888 | tf_op jit(solution)/shard_map/ppermute | solution.py:495
  77.3 5.8 %collective-permute-start.1 = (f32[40,256]{1,0:T(8,128)S(1)}, f32[40,256]{1,0:T(8,128)S(1)}, u32[]{:S(2)}, u32[]{:S(2)}) collective-permute-start(f32[40,256]{1,0:T(8,128)S(1)} %get-tuple-element.39), channel_id=1, source_target_pairs={{8,0},{16,8},{24,16},{32,24},{40,32},{48,40},{56,48},{64,56},{72,6... | collective-permute-start | bytes 122888 | tf_op jit(solution)/shard_map/ppermute | solution.py:495
  83.3 0.7 copy-start.3
  84.1 0.7 copy-start.7
  89.8 32.9 %copy-start.4 = (f32[8,128,256]{2,1,0:T(8,128)S(1)}, f32[8,128,256]{2,1,0:T(8,128)}, u32[]{:S(2)}) copy-start(f32[8,128,256]{2,1,0:T(8,128)} %get-tuple-element.44.filled) | copy-start | bytes 3145732
  108.2 14.6 %all-to-all-start.5 = ((f32[8,32,256]{2,1,0:T(8,128)}), f32[8,32,256]{2,1,0:T(8,128)S(1)}, u32[]{:S(2)}, u32[]{:S(2)}) async-start(f32[8,32,256]{2,1,0:T(8,128)} %shard_map.75), calls=%async_computation.5 | async-start | bytes 524288 | tf_op jit(solution)/shard_map/all_to_all | solution.py:488
  111.6 11.2 %copy-start.6 = (s32[8,256]{1,0:T(8,128)S(1)}, s32[8,256]{1,0:T(8,128)}, u32[]{:S(2)}) copy-start(s32[8,256]{1,0:T(8,128)} %land.13) | copy-start | bytes 24580
  122.7 26.4 %copy-start = (s32[128,8,256]{2,1,0:T(8,128)S(1)}, s32[128,8,256]{2,1,0:T(8,128)}, u32[]{:S(2)}) copy-start(s32[128,8,256]{2,1,0:T(8,128)} %missing.1) | copy-start | bytes 3145732
  136.6 20.4 %copy-start.1 = (f32[128,8,256]{2,1,0:T(8,128)S(1)}, f32[128,8,256]{2,1,0:T(8,128)}, u32[]{:S(2)}) copy-start(f32[128,8,256]{2,1,0:T(8,128)} %observed.1) | copy-start | bytes 3145732
  137.3 15.7 %all-to-all-start.7 = ((f32[8,40,128]{2,1,0:T(8,128)}), f32[8,40,128]{2,1,0:T(8,128)S(1)}, u32[]{:S(2)}, u32[]{:S(2)}) async-start(f32[8,40,128]{2,1,0:T(8,128)} %shard_map.78), calls=%async_computation.7 | async-start | bytes 327680 | tf_op jit(solution)/shard_map/all_to_all | solution.py:488
  142.1 7.0 %collective-permute-start.2 = (f32[40,256]{1,0:T(8,128)S(1)}, f32[40,256]{1,0:T(8,128)S(1)}, u32[]{:S(2)}, u32[]{:S(2)}) collective-permute-start(f32[40,256]{1,0:T(8,128)S(1)} %get-tuple-element.49), channel_id=1, source_target_pairs={{0,8},{8,16},{16,24},{24,32},{32,40},{40,48},{48,56},{56,64},{64,7... | collective-permute-start | bytes 122888 | tf_op jit(solution)/shard_map/ppermute | solution.py:495
  147.2 5.5 %collective-permute-start.3 = (f32[40,256]{1,0:T(8,128)S(1)}, f32[40,256]{1,0:T(8,128)S(1)}, u32[]{:S(2)}, u32[]{:S(2)}) collective-permute-start(f32[40,256]{1,0:T(8,128)S(1)} %get-tuple-element.50), channel_id=1, source_target_pairs={{8,0},{16,8},{24,16},{32,24},{40,32},{48,40},{56,48},{64,56},{72,6... | collective-permute-start | bytes 122888 | tf_op jit(solution)/shard_map/ppermute | solution.py:495
  153.6 12.8 %all-to-all-start.8 = ((f32[8,32,128]{2,1,0:T(8,128)}), f32[8,32,128]{2,1,0:T(8,128)S(1)}, u32[]{:S(2)}, u32[]{:S(2)}) async-start(f32[8,32,128]{2,1,0:T(8,128)} %get-tuple-element.52.raw), calls=%async_computation.8 | async-start | bytes 262144 | tf_op jit(solution)/shard_map/all_to_all | solution.py:488

commit v5 on v4

--- a/solution.py
+++ b/solution.py
@@ -161,7 +161,6 @@
     missing_hbm,
     land_hbm,
     basis_hbm,
-    first_hbm,
     out_hbm,
     observed,
     missing,
@@ -169,13 +168,12 @@
     basis_t,
     half_0,
     half_1,
-    first,
     out,
     arrivals,
     sent,
 ):
     parts = 4
-    days = first.shape[1]
+    days = observed.shape[0]
     size = days // parts
     small = [
         pltpu.make_async_copy(land_hbm, land, arrivals.at[2 * parts]),
@@ -218,30 +216,59 @@
     weights = parts_of(basis_t[...])
     copies = []
     for r in range(8):
-        filled = rows_of(halves, r, days)
-        first[r] = filled
-        out[r, :K, :] = mul_few(weights, filled)
+        out[r, :K, :] = mul_few(weights, rows_of(halves, r, days))
         copies.append(pltpu.make_async_copy(out.at[r], out_hbm.at[r], sent.at[r]))
         copies[-1].start()
-        copies.append(pltpu.make_async_copy(first.at[r], first_hbm.at[r], sent.at[8 + r]))
-        copies[-1].start()
     for copy in copies:
         copy.wait()
 
 
-def gap_body(missing_hbm, gap_hbm, missing, half_0, half_1, gap, arrivals):
-    copy = pltpu.make_async_copy(missing_hbm, missing, arrivals.at[0])
-    copy.start()
-    copy.wait()
+def turn_body(
+    observed_hbm,
+    missing_hbm,
+    land,
+    first_hbm,
+    gap_hbm,
+    observed,
+    missing,
+    half_0,
+    half_1,
+    mask_0,
+    mask_1,
+    first,
+    gap,
+    arrivals,
+    sent,
+):
+    pairs = ((missing_hbm, missing), (observed_hbm, observed))
+    copies = [
+        pltpu.make_async_copy(source, target, arrivals.at[i])
+        for i, (source, target) in enumerate(pairs)
+    ]
+    for copy in copies:
+        copy.start()
+    for copy in copies:
+        copy.wait()
     days = missing.shape[0]
-    for c, half in enumerate((half_0, half_1)):
-        tile = missing[:, :, LANES * c : LANES * c + LANES].astype(f32)
-        half[...] = tile.reshape(8 * days, LANES)
+    ocean = 1.0 - land[...].astype(f32)
+    halves, masks = (half_0, half_1), (mask_0, mask_1)
+    for c in range(2):
+        at = slice(LANES * c, LANES * c + LANES)
+        absent = missing[:, :, at] == 1
+        tile = jnp.where(absent, f32(0.0), observed[:, :, at]) * ocean[None, :, at]
+        halves[c][...] = tile.reshape(8 * days, LANES)
+        masks[c][...] = absent.astype(f32).reshape(8 * days, LANES)
     for r in range(8):
-        gap[r] = rows_of((half_0, half_1), r, days)
-    copy = pltpu.make_async_copy(gap, gap_hbm, arrivals.at[1])
-    copy.start()
-    copy.wait()
+        first[r] = rows_of(halves, r, days)
+        gap[r] = rows_of(masks, r, days)
+    copies = [
+        pltpu.make_async_copy(first, first_hbm, sent.at[0]),
+        pltpu.make_async_copy(gap, gap_hbm, sent.at[1]),
+    ]
+    for copy in copies:
+        copy.start()
+    for copy in copies:
+        copy.wait()
 
 
 def add_rows_body(arrived, out):
@@ -376,7 +403,7 @@
     total = total_of(arrived)
     extra = jnp.concatenate([total[K:], pltpu.roll(total[K:], 64, 1)], axis=0)
     raw = jnp.concatenate([total[:K], extra], axis=1)
-    tempered_t = mul(raw, band[...]).T
+    tempered_t = mul(raw, band[: 2 * LANES, :]).T
     factor = inverse_factor(extra)
     weights_t = mul(factor, total[:K])
     mixed = deep_parts_of(mul(tempered_t, mul(factor.T, factor)))
@@ -433,19 +460,33 @@
     right,
     mixed,
     smooth,
-    observed_low,
-    observed_high,
-    missing_low,
-    missing_high,
+    observed_hbm,
+    missing_hbm,
     land,
     filled_in,
     basis_t,
     filled,
     edges,
     halves,
+    observed,
+    missing,
+    arrivals,
     sent,
 ):
     del filled_in
+    fetches = []
+    total_days = observed_hbm.shape[0]
+    for e in range(2):
+        at = pl.ds((total_days - 8) * e, 8)
+        for c, (source, target) in enumerate(
+            ((observed_hbm, observed), (missing_hbm, missing))
+        ):
+            fetches.append(
+                pltpu.make_async_copy(
+                    source.at[at], target.at[e], arrivals.at[2 * e + c]
+                )
+            )
+            fetches[-1].start()
     d = day[0]
     low = arrived[jnp.maximum(d - 1, 0)]
     high = arrived[jnp.minimum(d + 1, 7)]
@@ -460,13 +501,16 @@
         for c in range(2):
             halves[c, pl.ds(r, 16, stride=8), :] = surface[:, LANES * c : LANES * c + LANES]
     ocean = 1.0 - land[...].astype(f32)
-    sides = ((observed_low, missing_low), (observed_high, missing_high))
+    for fetch in fetches:
+        fetch.wait()
     copies = []
-    for e, (observed, missing) in enumerate(sides):
+    for e in range(2):
         for c in range(2):
             at = slice(LANES * c, LANES * c + LANES)
             surface = halves[c, 64 * e : 64 * e + 64, :].reshape(8, 8, LANES)
-            value = jnp.where(missing[:, :, at] == 1, surface, observed[:, :, at])
+            value = jnp.where(
+                missing[e, :, :, at] == 1, surface, observed[e, :, :, at]
+            )
             edges[e, :, :, at] = value * ocean[None, :, at]
         copy = pltpu.make_async_copy(
             edges.at[e], filled.at[pl.ds((days - 8) * e, 8)], sent.at[e]
@@ -474,11 +518,12 @@
         copy.start()
         copies.append(copy)
     found = factor[...]
-    gram = jnp.zeros((K, LANES), f32)
-    rest = jnp.zeros((LANES - K, LANES), f32)
-    for j in range(arrived.shape[0]):
-        weights_t = mul(found, arrived[j])
-        gram = gram + mul_t(weights_t, jnp.concatenate([weights_t, rest], axis=0))
+    raw = [arrived[j] for j in range(arrived.shape[0])]
+    weights_t = mul(found, jnp.concatenate(raw, axis=1))
+    rest = jnp.zeros((LANES - K, weights_t.shape[1]), f32)
+    gram = mul_few(
+        parts_of(weights_t), jnp.concatenate([weights_t, rest], axis=0), 1
+    )
     basis_t[...] = mul(inverse_factor(gram), mul(found, arrived[d]))
     for copy in copies:
         copy.wait()
@@ -518,8 +563,6 @@
     days, rows, cols = observed.shape
     day = lax.axis_index(DAY).reshape(1)
     near, far = lax.axis_size(NEAR), lax.axis_size("y")
-    band = band_of(day_weights)
-
     halo = [pltpu.VMEM((64, LANES), f32)] * 2
     halves = [pltpu.VMEM((days * rows, LANES), f32)] * 2
     edge = (K + 8, cols)
@@ -539,9 +582,9 @@
     turned = pltpu.VMEM((rows, days, cols), f32)
     mask = pltpu.VMEM((days, rows, cols), jnp.int32)
 
-    first, part = call(
+    part = call(
         start_body,
-        [(rows, days, cols), (rows, K + HALO, cols)],
+        (rows, K + HALO, cols),
         (day, observed, missing, land, basis_start.T),
         [
             slab,
@@ -549,26 +592,29 @@
             pltpu.VMEM((rows, cols), jnp.int32),
             pltpu.VMEM((K, days), f32),
             *halves,
-            turned,
             pltpu.VMEM((rows, K + HALO, cols), f32),
             pltpu.SemaphoreType.DMA((10,)),
-            pltpu.SemaphoreType.DMA((16,)),
+            pltpu.SemaphoreType.DMA((8,)),
         ],
         limit=56,
         anywhere=(1, 2, 3, 4),
+        out_any=(0,),
+    )
+    later, taps, part = lax.optimization_barrier((missing, day_weights, part))
+    band = band_of(taps)
+    first, gap = call(
+        turn_body,
+        [(rows, days, cols)] * 2,
+        (observed, later, land),
+        [slab, mask, *halves, *halves, turned, turned]
+        + [pltpu.SemaphoreType.DMA((2,))] * 2,
+        limit=56,
+        anywhere=(0, 1),
         out_any=(0, 1),
     )
-    later, part = lax.optimization_barrier((missing, part))
-    gap = call(
-        gap_body,
-        (rows, days, cols),
-        (later,),
-        [mask, *halves, turned, pltpu.SemaphoreType.DMA((2,))],
-        limit=56,
-        anywhere=(0,),
-        out_any=(0,),
-    )
-    arrived = swap(part, DAY)
+    arrived, first, gap, band = lax.optimization_barrier(
+        (swap(part, DAY), first, gap, band)
+    )
     modes = swap(call(add_rows_body, block, (arrived,)), DAY)
     joint, *edges = call(
         project_body,
@@ -581,7 +627,7 @@
     filled, part = call(
         refill_body,
         [(rows, days, cols), (rows, K + 8, cols)],
-        (day, joint, band[: 2 * LANES], smooth, first, gap, land),
+        (day, joint, band, smooth, first, gap, land),
         [
             pltpu.VMEM(block, f32),
             turned,
@@ -590,7 +636,7 @@
             pltpu.SemaphoreType.DMA((3,)),
             pltpu.SemaphoreType.DMA((8,)),
         ],
-        limit=56,
+        limit=53,
         anywhere=(3, 4, 5),
         out_any=(0,),
     )
@@ -617,22 +663,22 @@
         (mixed, smooth, observed, missing, land),
         halves,
     )
-    ends = (slice(0, 8), slice(days - 8, days))
     basis_t, filled = call(
         finish_body,
         [(K, days), (days, rows, cols)],
         (day, arrived, band, found, right, mixed, smooth)
-        + tuple(observed[e] for e in ends)
-        + tuple(missing[e] for e in ends)
-        + (land, filled),
+        + (observed, missing, land, filled),
         [
             pltpu.VMEM((2, 8, rows, cols), f32),
             pltpu.VMEM((2, 128, LANES), f32),
+            pltpu.VMEM((2, 8, rows, cols), f32),
+            pltpu.VMEM((2, 8, rows, cols), jnp.int32),
+            pltpu.SemaphoreType.DMA((4,)),
             pltpu.SemaphoreType.DMA((2,)),
         ],
-        anywhere=(12,),
+        anywhere=(7, 8, 10),
         out_any=(1,),
-        alias={12: 1},
+        alias={10: 1},
     )
     return filled, basis_t.T
 

time: 172 us -> 167 us (0.971)
  waiting for transfers between devices: 35.2 us -> 31.7 us
  local copies, waits for them, and re-layouts: 2.76 us -> 0.04 us
  blocking collectives: 55.3 us -> 57.2 us
    all_to_all x6 -> x5, waiting for transfers between devices: 31.6 us -> 24.5 us  [swap(): return lax.all_to_all(blocks, axes, 0, 0)]
    ppermute x4, waiting for transfers between devices: 3.57 us -> 7.27 us  [near_rows(): return (lax.ppermute(edge_high, PIX, up), lax.ppermute(edge_low, PIX, down))]
    unnamed x18 -> x12, local copies, waits for them, and re-layouts: 2.07 us -> 0.03 us
    all_to_all x3 -> x4, blocking collectives: 55.3 us -> 57.2 us  [swap(): return lax.all_to_all(blocks, axes, 0, 0)]
    all_to_all x6 -> x5, starting transfers between devices: 33.8 us -> 32.5 us  [swap(): return lax.all_to_all(blocks, axes, 0, 0)]
  transfers between devices with their start and end apart: 10 -> 9, of which waited for: 5 -> 5; matrix products, arithmetic and copies ran while one was open for 1% -> 0% of each run, Pallas kernels for 4% -> 6%
where the time goes in v5:
time: 167 us; the launch traced here: 165 us
  blocking collectives  57.2 us (34%)
  starting transfers between devices  47.1 us (28%)
  waiting for transfers between devices  31.7 us (19%)
  Pallas kernels  27.4 us (16%)
    all_to_all x4, blocking collectives, swap(): return lax.all_to_all(blocks, axes, 0, 0)  57.2 us
    all_to_all x5, starting transfers between devices, swap(): return lax.all_to_all(blocks, axes, 0, 0)  32.5 us
    pallas_call x16, Pallas kernels, call(): pl.pallas_call(body, out_shape=shapes if many else shapes[0], in_specs=sp...  27.4 us
    all_to_all x5, waiting for transfers between devices, swap(): return lax.all_to_all(blocks, axes, 0, 0)  24.5 us
    ppermute x4, starting transfers between devices, near_rows(): return (lax.ppermute(edge_high, PIX, up), lax.ppermute(edge_low, PIX, down))  14.6 us
    ppermute x4, waiting for transfers between devices, near_rows(): return (lax.ppermute(edge_high, PIX, up), lax.ppermute(edge_low, PIX, down))  7.27 us
  transfers between devices with their start and end apart: 9, of which 5 were waited for; matrix products, arithmetic and copies ran while one was open for 0% of the time, Pallas kernels for 6%

profile of v5, /device:TPU:1, one launch (start us, length us, event | category | flops | bytes accessed | tf_op | source)
XLA Modules:
  0.0 165.0 jit_solution(1731725113898993098)
XLA Ops:
  0.6 2.9 %shard_map.68 = f32[8,56,256]{2,1,0:T(8,128)} custom-call(s32[1]{0:T(128)} %bitcast.day, f32[128,8,256]{2,1,0:T(8,128)} %observed_hbm.5, s32[128,8,256]{2,1,0:T(8,128)} %missing_hbm.4, s32[8,256]{1,0:T(8,128)} %land.15, f32[32,128]{1,0:T(8,128)} %bitcast.18), custom_call_target="tpu_custom_call" | custom-call | flops 1000000 | bytes 1000000 | tf_op jit(solution)/shard_map/pallas_call | solution.py:138
  3.6 13.3 %all-to-all-start = ((f32[8,56,256]{2,1,0:T(8,128)}), f32[8,56,256]{2,1,0:T(8,128)S(1)}, u32[]{:S(2)}, u32[]{:S(2)}) async-start(f32[8,56,256]{2,1,0:T(8,128)} %shard_map.68), calls=%async_computation | async-start | bytes 917504 | tf_op jit(solution)/shard_map/all_to_all | solution.py:533
  16.9 0.0 copy-start.5
  16.9 4.3 %shard_map.69 = (f32[8,128,256]{2,1,0:T(8,128)}, f32[8,128,256]{2,1,0:T(8,128)}) custom-call(f32[128,8,256]{2,1,0:T(8,128)} %observed_hbm.5, s32[128,8,256]{2,1,0:T(8,128)} %missing_hbm.4, s32[8,256]{1,0:T(8,128)} %land.15), custom_call_target="tpu_custom_call" | custom-call | flops 1000000 | bytes 1000000 | tf_op jit(solution)/shard_map/pallas_call | solution.py:138
  21.2 0.0 copy-start.2
  21.3 0.0 copy-done.5
  21.3 0.7 select_add_fusion.band
  22.0 7.4 %all-to-all-done.arrived = f32[8,56,256]{2,1,0:T(8,128)S(1)} async-done(((f32[8,56,256]{2,1,0:T(8,128)}), f32[8,56,256]{2,1,0:T(8,128)S(1)}, u32[]{:S(2)}, u32[]{:S(2)}) %all-to-all-start) | async-done | bytes 458784 | tf_op jit(solution)/shard_map/all_to_all | solution.py:533
  29.5 0.0 copy-start.4
  29.5 12.6 %all_to_all.45.modes = f32[8,32,256]{2,1,0:T(8,128)S(1)} all-to-all(f32[8,32,256]{2,1,0:T(8,128)S(1)} %shard_map.70), channel_id=1, replica_groups=mesh['zlo'=4,'y'=8,'core'=2,'x'=4,'zhi'=2] {'x','zhi'}, dimensions={0} | all-to-all | bytes 524288 | tf_op jit(solution)/shard_map/all_to_all | solution.py:533
  42.1 0.0 copy-done.2
  42.1 0.0 copy-done.4
  42.1 1.0 shard_map.71
  43.1 18.3 %all_to_all.46.arrived = f32[8,48,128]{2,1,0:T(8,128)S(1)} all-to-all(f32[8,48,128]{2,1,0:T(8,128)S(1)} %get-tuple-element.43), channel_id=1, replica_groups=mesh['zlo'=4,'y'=8,'core'=2,'x'=4,'zhi'=2] {'zlo','core'}, dimensions={0} | all-to-all | bytes 393216 | tf_op jit(solution)/shard_map/all_to_all | solution.py:533
  61.4 0.7 shard_map.72
  62.0 6.8 %all-to-all-start.3 = ((f32[8,48,128]{2,1,0:T(8,128)}), f32[8,48,128]{2,1,0:T(8,128)S(1)}, u32[]{:S(2)}, u32[]{:S(2)}) async-start(f32[8,48,128]{2,1,0:T(8,128)} %shard_map.72), calls=%async_computation.3 | async-start | bytes 393216 | tf_op jit(solution)/shard_map/all_to_all | solution.py:533
  68.9 5.7 %collective-permute-start = (f32[40,256]{1,0:T(8,128)S(1)}, f32[40,256]{1,0:T(8,128)S(1)}, u32[]{:S(2)}, u32[]{:S(2)}) collective-permute-start(f32[40,256]{1,0:T(8,128)S(1)} %get-tuple-element.47), channel_id=1, source_target_pairs={{0,8},{8,16},{16,24},{24,32},{32,40},{40,48},{48,56},{56,64},{64,7... | collective-permute-start | bytes 122888 | tf_op jit(solution)/shard_map/ppermute | solution.py:540
  74.6 1.9 %collective-permute-start.1 = (f32[40,256]{1,0:T(8,128)S(1)}, f32[40,256]{1,0:T(8,128)S(1)}, u32[]{:S(2)}, u32[]{:S(2)}) collective-permute-start(f32[40,256]{1,0:T(8,128)S(1)} %get-tuple-element.48), channel_id=1, source_target_pairs={{8,0},{16,8},{24,16},{32,24},{40,32},{48,40},{56,48},{64,56},{72,6... | collective-permute-start | bytes 122888 | tf_op jit(solution)/shard_map/ppermute | solution.py:540
  76.5 0.0 collective-permute-done.above
  76.5 3.7 %collective-permute-done.1.below = f32[40,256]{1,0:T(8,128)S(1)} collective-permute-done((f32[40,256]{1,0:T(8,128)S(1)}, f32[40,256]{1,0:T(8,128)S(1)}, u32[]{:S(2)}, u32[]{:S(2)}) %collective-permute-start.1) | collective-permute-done | bytes 40992 | tf_op jit(solution)/shard_map/ppermute | solution.py:540
  80.2 0.2 shard_map.73.smooth_hbm
  80.4 0.0 all-to-all-done.3.arrived
  80.4 5.3 %shard_map.74 = (f32[8,128,256]{2,1,0:T(8,128)}, f32[8,40,256]{2,1,0:T(8,128)}) custom-call(s32[1]{0:T(128)} %bitcast.day, f32[8,48,128]{2,1,0:T(8,128)S(1)} %all-to-all-done.3.arrived, f32[512,128]{1,0:T(8,128)S(1)} %select_add_fusion.band, f32[8,32,256]{2,1,0:T(8,128)S(1)} %shard_map.73.smooth_hbm, f32[8,128,256]{2,1,0:T(8,128)} %get-tuple-element.42.filled.first_hbm, ...), custom_call_target="tpu_custom_call" | custom-call | flops 1000000 | bytes 1000000 | tf_op jit(solution)/shard_map/pallas_call | solution.py:138
  85.7 0.0 copy-start.3
  85.7 15.8 %all_to_all.47.arrived = f32[8,40,256]{2,1,0:T(8,128)S(1)} all-to-all(f32[8,40,256]{2,1,0:T(8,128)} %get-tuple-element.53), channel_id=1, replica_groups=mesh['zlo'=4,'y'=8,'core'=2,'x'=4,'zhi'=2] {'x','zhi'}, dimensions={0} | all-to-all | bytes 655360 | tf_op jit(solution)/shard_map/all_to_all | solution.py:533
  101.5 0.7 shard_map.75
  102.3 4.2 %all-to-all-start.5 = ((f32[8,32,256]{2,1,0:T(8,128)}), f32[8,32,256]{2,1,0:T(8,128)S(1)}, u32[]{:S(2)}, u32[]{:S(2)}) async-start(f32[8,32,256]{2,1,0:T(8,128)} %shard_map.75), calls=%async_computation.5 | async-start | bytes 524288 | tf_op jit(solution)/shard_map/all_to_all | solution.py:533
  106.4 0.8 shard_map.76.factor.scale
  107.3 11.5 %all-to-all-done.5.modes = f32[8,32,256]{2,1,0:T(8,128)S(1)} async-done(((f32[8,32,256]{2,1,0:T(8,128)}), f32[8,32,256]{2,1,0:T(8,128)S(1)}, u32[]{:S(2)}, u32[]{:S(2)}) %all-to-all-start.5) | async-done | bytes 262176 | tf_op jit(solution)/shard_map/all_to_all | solution.py:533
  118.7 0.0 copy-done.3
  118.7 2.2 %shard_map.77 = (f32[8,40,128]{2,1,0:T(8,128)S(1)}, f32[40,256]{1,0:T(8,128)S(1)}, f32[40,256]{1,0:T(8,128)S(1)}) custom-call(f32[8,32,256]{2,1,0:T(8,128)S(1)} %all-to-all-done.5.modes, f32[8,128,256]{2,1,0:T(8,128)S(1)} %copy-done.3, s32[8,256]{1,0:T(8,128)S(1)} %copy-done.4, f32[32,128]{1,0:T(8,128)S(1)} %shard_map.76.factor.scale), custom_call_target="tpu_custom_call" | custom-call | flops 1000000 | bytes 1000000 | tf_op jit(solution)/shard_map/pallas_call | solution.py:138
  120.9 10.5 %all_to_all.48.arrived = f32[8,40,128]{2,1,0:T(8,128)S(1)} all-to-all(f32[8,40,128]{2,1,0:T(8,128)S(1)} %get-tuple-element.55), channel_id=1, replica_groups=mesh['zlo'=4,'y'=8,'core'=2,'x'=4,'zhi'=2] {'zlo','core'}, dimensions={0} | all-to-all | bytes 327680 | tf_op jit(solution)/shard_map/all_to_all | solution.py:533
  131.4 0.7 shard_map.78
  132.1 4.8 %all-to-all-start.7 = ((f32[8,40,128]{2,1,0:T(8,128)}), f32[8,40,128]{2,1,0:T(8,128)S(1)}, u32[]{:S(2)}, u32[]{:S(2)}) async-start(f32[8,40,128]{2,1,0:T(8,128)} %shard_map.78), calls=%async_computation.7 | async-start | bytes 327680 | tf_op jit(solution)/shard_map/all_to_all | solution.py:533
  136.9 5.0 %collective-permute-start.2 = (f32[40,256]{1,0:T(8,128)S(1)}, f32[40,256]{1,0:T(8,128)S(1)}, u32[]{:S(2)}, u32[]{:S(2)}) collective-permute-start(f32[40,256]{1,0:T(8,128)S(1)} %get-tuple-element.59), channel_id=1, source_target_pairs={{0,8},{8,16},{16,24},{24,32},{32,40},{40,48},{48,56},{56,64},{64,7... | collective-permute-start | bytes 122888 | tf_op jit(solution)/shard_map/ppermute | solution.py:540
  142.0 1.9 %collective-permute-start.3 = (f32[40,256]{1,0:T(8,128)S(1)}, f32[40,256]{1,0:T(8,128)S(1)}, u32[]{:S(2)}, u32[]{:S(2)}) collective-permute-start(f32[40,256]{1,0:T(8,128)S(1)} %get-tuple-element.60), channel_id=1, source_target_pairs={{8,0},{16,8},{24,16},{32,24},{40,32},{48,40},{56,48},{64,56},{72,6... | collective-permute-start | bytes 122888 | tf_op jit(solution)/shard_map/ppermute | solution.py:540
  143.9 0.0 collective-permute-done.2.above
  143.9 3.6 %collective-permute-done.3.below = f32[40,256]{1,0:T(8,128)S(1)} collective-permute-done((f32[40,256]{1,0:T(8,128)S(1)}, f32[40,256]{1,0:T(8,128)S(1)}, u32[]{:S(2)}, u32[]{:S(2)}) %collective-permute-start.3) | collective-permute-done | bytes 40992 | tf_op jit(solution)/shard_map/ppermute | solution.py:540
  147.5 0.2 shard_map.79.smooth
  147.8 0.0 all-to-all-done.7.arrived
  147.8 0.7 shard_map.80
  148.4 3.4 %all-to-all-start.8 = ((f32[8,32,128]{2,1,0:T(8,128)}), f32[8,32,128]{2,1,0:T(8,128)S(1)}, u32[]{:S(2)}, u32[]{:S(2)}) async-start(f32[8,32,128]{2,1,0:T(8,128)} %get-tuple-element.62.raw), calls=%async_computation.8 | async-start | bytes 262144 | tf_op jit(solution)/shard_map/all_to_all | solution.py:533
  151.8 2.3 %shard_map.81 = (f32[128,32]{1,0:T(8,128)S(1)}, f32[32,32]{1,0:T(8,128)S(1)}, f32[32,32]{1,0:T(8,128)S(1)}) custom-call(f32[8,32,128]{2,1,0:T(8,128)} %get-tuple-element.62.raw, f32[8,128]{1,0:T(8,128)S(1)} %get-tuple-element.63.extra, f32[512,128]{1,0:T(8,128)S(1)} %select_add_fusion.band, f32[32,128]{1,0:T(8,128)S(1)} %shard_map.76.factor.scale), custom_call_target="tpu_custom_call" | custom-call | flops 1000000 | bytes 1000000 | tf_op jit(solution)/shard_map/pallas_call | solution.py:138
  154.1 0.0 copy-done
  154.2 0.0 copy-done.1
  154.2 1.5 shard_map.82.filled_in
  155.7 5.5 %all-to-all-done.8.arrived = f32[8,32,128]{2,1,0:T(8,128)S(1)} async-done(((f32[8,32,128]{2,1,0:T(8,128)}), f32[8,32,128]{2,1,0:T(8,128)S(1)}, u32[]{:S(2)}, u32[]{:S(2)}) %all-to-all-start.8) | async-done | bytes 131104 | tf_op jit(solution)/shard_map/all_to_all | solution.py:533
  161.2 3.8 %shard_map.83 = (f32[32,128]{1,0:T(8,128)}, f32[128,8,256]{2,1,0:T(8,128)}) custom-call(s32[1]{0:T(128)} %bitcast.day, f32[8,32,128]{2,1,0:T(8,128)S(1)} %all-to-all-done.8.arrived, f32[512,128]{1,0:T(8,128)S(1)} %select_add_fusion.band, f32[32,32]{1,0:T(8,128)S(1)} %get-tuple-element.64.factor, ...), custom_call_target="tpu_custom_call", output_to_operand_aliasing={{1}: (10, {})} | custom-call | flops 1000000 | bytes 1000000 | tf_op jit(solution)/shard_map/pallas_call | solution.py:138
  (9 shorter events, 0.1 us)
Async XLA Ops:
  3.6 25.9 %all-to-all-start = ((f32[8,56,256]{2,1,0:T(8,128)}), f32[8,56,256]{2,1,0:T(8,128)S(1)}, u32[]{:S(2)}, u32[]{:S(2)}) async-start(f32[8,56,256]{2,1,0:T(8,128)} %shard_map.68), calls=%async_computation | async-start | bytes 917504 | tf_op jit(solution)/shard_map/all_to_all | solution.py:533
  16.9 4.4 %copy-start.5 = (f32[128,7]{0,1:T(8,128)S(1)}, f32[128,7]{0,1:T(8,128)}, u32[]{:S(2)}) copy-start(f32[128,7]{0,1:T(8,128)} %param.9) | copy-start | bytes 10756
  21.2 20.8 %copy-start.2 = (f32[8,128,256]{2,1,0:T(8,128)S(1)}, f32[8,128,256]{2,1,0:T(8,128)}, u32[]{:S(2)}) copy-start(f32[8,128,256]{2,1,0:T(8,128)} %get-tuple-element.42.filled.first_hbm) | copy-start | bytes 3145732
  29.5 12.6 %copy-start.4 = (s32[8,256]{1,0:T(8,128)S(1)}, s32[8,256]{1,0:T(8,128)}, u32[]{:S(2)}) copy-start(s32[8,256]{1,0:T(8,128)} %land.15) | copy-start | bytes 24580
  62.0 18.4 %all-to-all-start.3 = ((f32[8,48,128]{2,1,0:T(8,128)}), f32[8,48,128]{2,1,0:T(8,128)S(1)}, u32[]{:S(2)}, u32[]{:S(2)}) async-start(f32[8,48,128]{2,1,0:T(8,128)} %shard_map.72), calls=%async_computation.3 | async-start | bytes 393216 | tf_op jit(solution)/shard_map/all_to_all | solution.py:533
  68.9 7.6 %collective-permute-start = (f32[40,256]{1,0:T(8,128)S(1)}, f32[40,256]{1,0:T(8,128)S(1)}, u32[]{:S(2)}, u32[]{:S(2)}) collective-permute-start(f32[40,256]{1,0:T(8,128)S(1)} %get-tuple-element.47), channel_id=1, source_target_pairs={{0,8},{8,16},{16,24},{24,32},{32,40},{40,48},{48,56},{56,64},{64,7... | collective-permute-start | bytes 122888 | tf_op jit(solution)/shard_map/ppermute | solution.py:540
  74.6 5.6 %collective-permute-start.1 = (f32[40,256]{1,0:T(8,128)S(1)}, f32[40,256]{1,0:T(8,128)S(1)}, u32[]{:S(2)}, u32[]{:S(2)}) collective-permute-start(f32[40,256]{1,0:T(8,128)S(1)} %get-tuple-element.48), channel_id=1, source_target_pairs={{8,0},{16,8},{24,16},{32,24},{40,32},{48,40},{56,48},{64,56},{72,6... | collective-permute-start | bytes 122888 | tf_op jit(solution)/shard_map/ppermute | solution.py:540
  85.7 33.0 %copy-start.3 = (f32[8,128,256]{2,1,0:T(8,128)S(1)}, f32[8,128,256]{2,1,0:T(8,128)}, u32[]{:S(2)}) copy-start(f32[8,128,256]{2,1,0:T(8,128)} %get-tuple-element.54.filled) | copy-start | bytes 3145732
  102.3 16.5 %all-to-all-start.5 = ((f32[8,32,256]{2,1,0:T(8,128)}), f32[8,32,256]{2,1,0:T(8,128)S(1)}, u32[]{:S(2)}, u32[]{:S(2)}) async-start(f32[8,32,256]{2,1,0:T(8,128)} %shard_map.75), calls=%async_computation.5 | async-start | bytes 524288 | tf_op jit(solution)/shard_map/all_to_all | solution.py:533
  131.4 22.7 %copy-start = (f32[128,8,256]{2,1,0:T(8,128)S(1)}, f32[128,8,256]{2,1,0:T(8,128)}, u32[]{:S(2)}) copy-start(f32[128,8,256]{2,1,0:T(8,128)} %observed_hbm.5) | copy-start | bytes 3145732
  131.4 22.7 %copy-start.1 = (s32[128,8,256]{2,1,0:T(8,128)S(1)}, s32[128,8,256]{2,1,0:T(8,128)}, u32[]{:S(2)}) copy-start(s32[128,8,256]{2,1,0:T(8,128)} %missing_hbm.4) | copy-start | bytes 3145732
  132.1 15.7 %all-to-all-start.7 = ((f32[8,40,128]{2,1,0:T(8,128)}), f32[8,40,128]{2,1,0:T(8,128)S(1)}, u32[]{:S(2)}, u32[]{:S(2)}) async-start(f32[8,40,128]{2,1,0:T(8,128)} %shard_map.78), calls=%async_computation.7 | async-start | bytes 327680 | tf_op jit(solution)/shard_map/all_to_all | solution.py:533
  136.9 7.0 %collective-permute-start.2 = (f32[40,256]{1,0:T(8,128)S(1)}, f32[40,256]{1,0:T(8,128)S(1)}, u32[]{:S(2)}, u32[]{:S(2)}) collective-permute-start(f32[40,256]{1,0:T(8,128)S(1)} %get-tuple-element.59), channel_id=1, source_target_pairs={{0,8},{8,16},{16,24},{24,32},{32,40},{40,48},{48,56},{56,64},{64,7... | collective-permute-start | bytes 122888 | tf_op jit(solution)/shard_map/ppermute | solution.py:540
  142.0 5.5 %collective-permute-start.3 = (f32[40,256]{1,0:T(8,128)S(1)}, f32[40,256]{1,0:T(8,128)S(1)}, u32[]{:S(2)}, u32[]{:S(2)}) collective-permute-start(f32[40,256]{1,0:T(8,128)S(1)} %get-tuple-element.60), channel_id=1, source_target_pairs={{8,0},{16,8},{24,16},{32,24},{40,32},{48,40},{56,48},{64,56},{72,6... | collective-permute-start | bytes 122888 | tf_op jit(solution)/shard_map/ppermute | solution.py:540
  148.4 12.8 %all-to-all-start.8 = ((f32[8,32,128]{2,1,0:T(8,128)}), f32[8,32,128]{2,1,0:T(8,128)S(1)}, u32[]{:S(2)}, u32[]{:S(2)}) async-start(f32[8,32,128]{2,1,0:T(8,128)} %get-tuple-element.62.raw), calls=%async_computation.8 | async-start | bytes 262144 | tf_op jit(solution)/shard_map/all_to_all | solution.py:533

commit v6 on v5

--- a/solution.py
+++ b/solution.py
@@ -130,7 +130,10 @@
         space = pltpu.SMEM if a.ndim == 1 else pltpu.VMEM
         specs.append(pl.BlockSpec(memory_space=pl.ANY if i in anywhere else space))
     many = isinstance(outs, list)
-    shapes = [jax.ShapeDtypeStruct(s, f32) for s in (outs if many else [outs])]
+    shapes = [
+        s if isinstance(s, jax.ShapeDtypeStruct) else jax.ShapeDtypeStruct(s, f32)
+        for s in (outs if many else [outs])
+    ]
     out_specs = [
         pl.BlockSpec(memory_space=pl.ANY if i in out_any else pltpu.VMEM)
         for i in range(len(shapes))
@@ -260,7 +263,7 @@
         masks[c][...] = absent.astype(f32).reshape(8 * days, LANES)
     for r in range(8):
         first[r] = rows_of(halves, r, days)
-        gap[r] = rows_of(masks, r, days)
+        gap[r] = rows_of(masks, r, days).astype(bf16)
     copies = [
         pltpu.make_async_copy(first, first_hbm, sent.at[0]),
         pltpu.make_async_copy(gap, gap_hbm, sent.at[1]),
@@ -300,31 +303,34 @@
     out[:, K:] = jnp.zeros((K, LANES - K), f32)
 
 
-def edges_of(modes, land, edge_low, edge_high):
+def edges_of(day, modes, land, edge_near, edge_far):
     ocean = 1.0 - land[...].astype(f32)
-    for edge, r in ((edge_low, 0), (edge_high, 7)):
-        edge[:K, :] = modes[r]
-        edge[K:, :] = jnp.broadcast_to(ocean[r : r + 1], (8, ocean.shape[1]))
-
-
-def project_again_body(modes, filled, land, factor, out, edge_low, edge_high):
+    upper = day[1] == 0
+    for edge, r, q in ((edge_near, 7, 0), (edge_far, 0, 7)):
+        edge[:K, :] = jnp.where(upper, modes[r], modes[q])
+        flag = jnp.where(upper, ocean[r : r + 1], ocean[q : q + 1])
+        edge[K:, :] = jnp.broadcast_to(flag, (8, ocean.shape[1]))
+
+
+def project_again_body(day, modes, filled, land, factor, out, edge_near, edge_far):
     cols = modes.shape[2]
-    scale = factor[:, :K]
+    wide = jnp.concatenate([modes[r] for r in range(8)], axis=1)
+    wide = mul_deep(deep_parts_of(factor[:, :K]), wide)
     pad = jnp.zeros((LANES - K, cols), f32)
     total = jnp.zeros((K, 2 * LANES), f32)
     for r in range(8):
-        modes_u = mul(scale, modes[r])
+        modes_u = wide[:, cols * r : cols * r + cols]
         right = jnp.concatenate([filled[r], modes_u, pad], axis=0)
         total = total + mul_few(parts_of(modes_u), right, 1)
     packed = pack_rows(total[:, LANES:])
     for j in range(out.shape[0]):
         out[j, :K, :] = total[:, :LANES]
         out[j, K:, :] = packed
-    edges_of(modes, land, edge_low, edge_high)
+    edges_of(day, modes, land, edge_near, edge_far)
 
 
 def project_body(
-    day, arrived, modes, filled, land, out, edge_low, edge_high, halo_0, halo_1
+    day, arrived, modes, filled, land, out, edge_near, edge_far, halo_0, halo_1
 ):
     d = day[0]
     low = arrived[jnp.maximum(d - 1, 0), K : K + HALO, :]
@@ -348,10 +354,13 @@
     for j in range(out.shape[0]):
         out[j, :K, :] = total[:, :LANES]
         out[j, K:, :] = packed
-    edges_of(modes, land, edge_low, edge_high)
-
-
-def smooth_body(modes, above, below, land, out):
+    edges_of(day, modes, land, edge_near, edge_far)
+
+
+def smooth_body(day, modes, near, far, land, out):
+    upper = day[1] == 0
+    above = jnp.where(upper, far[...], near[...])
+    below = jnp.where(upper, near[...], far[...])
     cols = out.shape[2]
     lane = lax.broadcasted_iota(jnp.int32, (1, cols), 1)
     ocean = 1.0 - land[...].astype(f32)
@@ -385,21 +394,28 @@
     gap_hbm,
     land,
     filled_hbm,
-    out,
+    out_hbm,
     smooth,
     first,
     gap,
     filled,
+    out,
     arrivals,
     sent,
 ):
-    pairs = ((smooth_hbm, smooth), (first_hbm, first), (gap_hbm, gap))
-    copies = [
-        pltpu.make_async_copy(source, target, arrivals.at[i])
-        for i, (source, target) in enumerate(pairs)
+    def start(source, target, semaphore):
+        copy = pltpu.make_async_copy(source, target, semaphore)
+        copy.start()
+        return copy
+
+    waits = [start(smooth_hbm, smooth, arrivals.at[16])]
+    fetches = [
+        (
+            start(first_hbm.at[r], first.at[r], arrivals.at[2 * r]),
+            start(gap_hbm.at[r], gap.at[r], arrivals.at[2 * r + 1]),
+        )
+        for r in range(8)
     ]
-    for copy in copies:
-        copy.start()
     total = total_of(arrived)
     extra = jnp.concatenate([total[K:], pltpu.roll(total[K:], 64, 1)], axis=0)
     raw = jnp.concatenate([total[:K], extra], axis=1)
@@ -408,23 +424,28 @@
     weights_t = mul(factor, total[:K])
     mixed = deep_parts_of(mul(tempered_t, mul(factor.T, factor)))
     weights = parts_of(weights_t)
-    days, cols = filled.shape[1:]
+    cols = filled.shape[2]
     packed = pack_gram(weights_t)
     for j in range(8):
         out[j, K:, :LANES] = packed
         out[j, K:, LANES:] = jnp.zeros((8, cols - LANES), f32)
     ocean = 1.0 - land[...].astype(f32)
-    for copy in copies:
+    for copy in waits:
         copy.wait()
-    copies = []
-    for r in range(8):
-        surface = mul_deep(mixed, smooth[r])
-        now = jnp.where(gap[r] == 1, surface * ocean[r : r + 1], first[r])
-        filled[r] = now
-        copies.append(pltpu.make_async_copy(filled.at[r], filled_hbm.at[r], sent.at[r]))
-        copies[-1].start()
-        out[r, :K, :] = mul_few(weights, now)
-    for copy in copies:
+    sends = []
+    for r in range(0, 8, 2):
+        for copy in fetches[r] + fetches[r + 1]:
+            copy.wait()
+        for q in (r, r + 1):
+            surface = mul_deep(mixed, smooth[q])
+            absent = gap[q].astype(f32) == 1
+            now = jnp.where(absent, surface * ocean[q : q + 1], first[q])
+            filled[q] = now
+            out[q, :K, :] = mul_few(weights, now)
+        for q in (r, r + 1):
+            sends.append(start(filled.at[q], filled_hbm.at[q], sent.at[2 * q]))
+            sends.append(start(out.at[q], out_hbm.at[q], sent.at[2 * q + 1]))
+    for copy in sends:
         copy.wait()
 
 
@@ -460,33 +481,19 @@
     right,
     mixed,
     smooth,
-    observed_hbm,
-    missing_hbm,
+    observed_low,
+    observed_high,
+    missing_low,
+    missing_high,
     land,
     filled_in,
     basis_t,
     filled,
     edges,
     halves,
-    observed,
-    missing,
-    arrivals,
     sent,
 ):
     del filled_in
-    fetches = []
-    total_days = observed_hbm.shape[0]
-    for e in range(2):
-        at = pl.ds((total_days - 8) * e, 8)
-        for c, (source, target) in enumerate(
-            ((observed_hbm, observed), (missing_hbm, missing))
-        ):
-            fetches.append(
-                pltpu.make_async_copy(
-                    source.at[at], target.at[e], arrivals.at[2 * e + c]
-                )
-            )
-            fetches[-1].start()
     d = day[0]
     low = arrived[jnp.maximum(d - 1, 0)]
     high = arrived[jnp.minimum(d + 1, 7)]
@@ -496,21 +503,19 @@
     near = mixed[...] + mul(near, right[...])
     days = near.shape[0]
     near = jnp.concatenate([near[:8], near[days - 8 :]], axis=0)
+    near = deep_parts_of(near)
     for r in range(8):
-        surface = mul(near, smooth[r])
+        surface = mul_deep(near, smooth[r])
         for c in range(2):
             halves[c, pl.ds(r, 16, stride=8), :] = surface[:, LANES * c : LANES * c + LANES]
     ocean = 1.0 - land[...].astype(f32)
-    for fetch in fetches:
-        fetch.wait()
+    sides = ((observed_low, missing_low), (observed_high, missing_high))
     copies = []
-    for e in range(2):
+    for e, (observed, missing) in enumerate(sides):
         for c in range(2):
             at = slice(LANES * c, LANES * c + LANES)
             surface = halves[c, 64 * e : 64 * e + 64, :].reshape(8, 8, LANES)
-            value = jnp.where(
-                missing[e, :, :, at] == 1, surface, observed[e, :, :, at]
-            )
+            value = jnp.where(missing[:, :, at] == 1, surface, observed[:, :, at])
             edges[e, :, :, at] = value * ocean[None, :, at]
         copy = pltpu.make_async_copy(
             edges.at[e], filled.at[pl.ds((days - 8) * e, 8)], sent.at[e]
@@ -533,11 +538,12 @@
     return lax.all_to_all(blocks, axes, 0, 0)
 
 
-def near_rows(edge_low, edge_high):
+def near_rows(edge_near, edge_far):
     count = lax.axis_size(PIX)
-    up = [(i, i + 1) for i in range(count - 1)]
-    down = [(i + 1, i) for i in range(count - 1)]
-    return lax.ppermute(edge_high, PIX, up), lax.ppermute(edge_low, PIX, down)
+    up = [(i, i + 1) for i in range(1, count - 1, 2)]
+    down = [(i + 1, i) for i in range(1, count - 1, 2)]
+    near = lax.ppermute(edge_near, "core", [(0, 1), (1, 0)])
+    return near, lax.ppermute(edge_far, PIX, up + down)
 
 
 def band_of(day_weights):
@@ -561,7 +567,7 @@
 
 def per_device(observed, missing, land, basis_start, day_weights):
     days, rows, cols = observed.shape
-    day = lax.axis_index(DAY).reshape(1)
+    day = jnp.stack([lax.axis_index(DAY), lax.axis_index("core")])
     near, far = lax.axis_size(NEAR), lax.axis_size("y")
     halo = [pltpu.VMEM((64, LANES), f32)] * 2
     halves = [pltpu.VMEM((days * rows, LANES), f32)] * 2
@@ -573,9 +579,9 @@
         return lax.optimization_barrier((joint, *edges))
 
     def smooth_beside(joint, low, high, modes):
-        above, below = near_rows(low, high)
+        beside, beyond = near_rows(low, high)
         joint = swap(joint, "y")
-        smooth = call(smooth_body, block, (modes, above, below, land))
+        smooth = call(smooth_body, block, (day, modes, beside, beyond, land))
         return lax.optimization_barrier((joint, smooth))
 
     slab = pltpu.VMEM((days, rows, cols), f32)
@@ -604,9 +610,9 @@
     band = band_of(taps)
     first, gap = call(
         turn_body,
-        [(rows, days, cols)] * 2,
+        [(rows, days, cols), jax.ShapeDtypeStruct((rows, days, cols), bf16)],
         (observed, later, land),
-        [slab, mask, *halves, *halves, turned, turned]
+        [slab, mask, *halves, *halves, turned, pltpu.VMEM((rows, days, cols), bf16)]
         + [pltpu.SemaphoreType.DMA((2,))] * 2,
         limit=56,
         anywhere=(0, 1),
@@ -631,14 +637,15 @@
         [
             pltpu.VMEM(block, f32),
             turned,
+            pltpu.VMEM((rows, days, cols), bf16),
             turned,
-            turned,
-            pltpu.SemaphoreType.DMA((3,)),
-            pltpu.SemaphoreType.DMA((8,)),
+            pltpu.VMEM((rows, K + 8, cols), f32),
+            pltpu.SemaphoreType.DMA((17,)),
+            pltpu.SemaphoreType.DMA((16,)),
         ],
         limit=53,
         anywhere=(3, 4, 5),
-        out_any=(0,),
+        out_any=(0, 1),
     )
     arrived = swap(part, DAY)
     modes = swap(call(add_rows_body, block, (arrived,)), DAY)
@@ -646,7 +653,7 @@
     joint, *edges = call(
         project_again_body,
         [(near, K + 8, LANES), edge, edge],
-        (modes, filled, land, factor),
+        (day, modes, filled, land, factor),
     )
     joint, low, high = add_near(joint, edges)
     joint, smooth = smooth_beside(joint, low, high, modes)
@@ -663,22 +670,22 @@
         (mixed, smooth, observed, missing, land),
         halves,
     )
+    ends = (slice(0, 8), slice(days - 8, days))
     basis_t, filled = call(
         finish_body,
         [(K, days), (days, rows, cols)],
         (day, arrived, band, found, right, mixed, smooth)
-        + (observed, missing, land, filled),
+        + tuple(observed[e] for e in ends)
+        + tuple(missing[e] for e in ends)
+        + (land, filled),
         [
             pltpu.VMEM((2, 8, rows, cols), f32),
             pltpu.VMEM((2, 128, LANES), f32),
-            pltpu.VMEM((2, 8, rows, cols), f32),
-            pltpu.VMEM((2, 8, rows, cols), jnp.int32),
-            pltpu.SemaphoreType.DMA((4,)),
             pltpu.SemaphoreType.DMA((2,)),
         ],
-        anywhere=(7, 8, 10),
+        anywhere=(12,),
         out_any=(1,),
-        alias={10: 1},
+        alias={12: 1},
     )
     return filled, basis_t.T
 

time: 167 us -> 168 us (level)
  waiting for transfers between devices: 31.7 us -> 26.4 us
  blocking collectives: 57.2 us -> 59.6 us
    ppermute x4, waiting for transfers between devices: 7.27 us -> 4.16 us  [the longest x2 4.16 us: near_rows(): return (near, lax.ppermute(edge_far, PIX, up + down))]
    all_to_all x4, blocking collectives: 57.2 us -> 59.6 us  [swap(): return lax.all_to_all(blocks, axes, 0, 0)]
    all_to_all x5, waiting for transfers between devices: 24.5 us -> 22.3 us  [swap(): return lax.all_to_all(blocks, axes, 0, 0)]
where the time goes in v6:
time: 168 us; the launch traced here: 167 us
  blocking collectives  59.6 us (35%)
  starting transfers between devices  48.3 us (29%)
  Pallas kernels  28.7 us (17%)
  waiting for transfers between devices  26.4 us (16%)
    all_to_all x4, blocking collectives, swap(): return lax.all_to_all(blocks, axes, 0, 0)  59.6 us
    all_to_all x5, starting transfers between devices, swap(): return lax.all_to_all(blocks, axes, 0, 0)  33.7 us
    pallas_call x16, Pallas kernels, call(): pl.pallas_call(body, out_shape=shapes if many else shapes[0], in_specs=sp...  28.7 us
    all_to_all x5, waiting for transfers between devices, swap(): return lax.all_to_all(blocks, axes, 0, 0)  22.3 us
    ppermute x2, starting transfers between devices, near_rows(): near = lax.ppermute(edge_near, 'core', [(0, 1), (1, 0)])  7.47 us
    ppermute x2, starting transfers between devices, near_rows(): return (near, lax.ppermute(edge_far, PIX, up + down))  7.09 us
    ppermute x2, waiting for transfers between devices, near_rows(): return (near, lax.ppermute(edge_far, PIX, up + down))  4.16 us
  transfers between devices with their start and end apart: 9, of which 5 were waited for; matrix products, arithmetic and copies ran while one was open for 0% of the time, Pallas kernels for 6%

profile of v6, /device:TPU:1, one launch (start us, length us, event | category | flops | bytes accessed | tf_op | source)
XLA Modules:
  0.0 166.6 jit_solution(9247834968309179892)
XLA Ops:
  0.6 0.7 pad_add_fusion.day
  1.3 3.6 %shard_map.68 = f32[8,56,256]{2,1,0:T(8,128)} custom-call(s32[2]{0:T(128)} %pad_add_fusion.day, f32[128,8,256]{2,1,0:T(8,128)} %observed.1, s32[128,8,256]{2,1,0:T(8,128)} %missing.1, s32[8,256]{1,0:T(8,128)} %land.15, f32[32,128]{1,0:T(8,128)} %bitcast.19), custom_call_target="tpu_custom_call" | custom-call | flops 1000000 | bytes 1000000 | tf_op jit(solution)/shard_map/pallas_call | solution.py:141
  4.9 13.3 %all-to-all-start = ((f32[8,56,256]{2,1,0:T(8,128)}), f32[8,56,256]{2,1,0:T(8,128)S(1)}, u32[]{:S(2)}, u32[]{:S(2)}) async-start(f32[8,56,256]{2,1,0:T(8,128)} %shard_map.68), calls=%async_computation | async-start | bytes 917504 | tf_op jit(solution)/shard_map/all_to_all | solution.py:538
  18.2 0.0 copy-start.6
  18.2 4.1 %shard_map.69 = (f32[8,128,256]{2,1,0:T(8,128)}, bf16[8,128,256]{2,1,0:T(8,128)(2,1)}) custom-call(f32[128,8,256]{2,1,0:T(8,128)} %observed.1, s32[128,8,256]{2,1,0:T(8,128)} %missing.1, s32[8,256]{1,0:T(8,128)} %land.15), custom_call_target="tpu_custom_call" | custom-call | flops 1000000 | bytes 1000000 | tf_op jit(solution)/shard_map/pallas_call | solution.py:141
  22.4 0.0 copy-start.2
  22.4 0.0 copy-done.6
  22.4 0.7 select_add_fusion.band
  23.1 7.6 %all-to-all-done.arrived = f32[8,56,256]{2,1,0:T(8,128)S(1)} async-done(((f32[8,56,256]{2,1,0:T(8,128)}), f32[8,56,256]{2,1,0:T(8,128)S(1)}, u32[]{:S(2)}, u32[]{:S(2)}) %all-to-all-start) | async-done | bytes 458784 | tf_op jit(solution)/shard_map/all_to_all | solution.py:538
  30.8 0.0 copy-start.4
  30.8 0.0 copy-start.5
  30.8 12.6 %all_to_all.45.modes = f32[8,32,256]{2,1,0:T(8,128)S(1)} all-to-all(f32[8,32,256]{2,1,0:T(8,128)S(1)} %shard_map.70), channel_id=1, replica_groups=mesh['zlo'=4,'y'=8,'core'=2,'x'=4,'zhi'=2] {'x','zhi'}, dimensions={0} | all-to-all | bytes 524288 | tf_op jit(solution)/shard_map/all_to_all | solution.py:538
  43.4 0.0 copy-done.2
  43.4 0.0 copy-done.4
  43.4 1.5 shard_map.71
  44.9 18.3 %all_to_all.46.arrived = f32[8,48,128]{2,1,0:T(8,128)S(1)} all-to-all(f32[8,48,128]{2,1,0:T(8,128)S(1)} %get-tuple-element.43), channel_id=1, replica_groups=mesh['zlo'=4,'y'=8,'core'=2,'x'=4,'zhi'=2] {'zlo','core'}, dimensions={0} | all-to-all | bytes 393216 | tf_op jit(solution)/shard_map/all_to_all | solution.py:538
  63.2 0.7 shard_map.72
  63.9 6.8 %all-to-all-start.3 = ((f32[8,48,128]{2,1,0:T(8,128)}), f32[8,48,128]{2,1,0:T(8,128)S(1)}, u32[]{:S(2)}, u32[]{:S(2)}) async-start(f32[8,48,128]{2,1,0:T(8,128)} %shard_map.72), calls=%async_computation.3 | async-start | bytes 393216 | tf_op jit(solution)/shard_map/all_to_all | solution.py:538
  70.8 4.1 %collective-permute-start = (f32[40,256]{1,0:T(8,128)S(1)}, f32[40,256]{1,0:T(8,128)S(1)}, u32[]{:S(2)}, u32[]{:S(2)}) collective-permute-start(f32[40,256]{1,0:T(8,128)S(1)} %get-tuple-element.47), channel_id=1, source_target_pairs={{0,8},{8,0},{1,9},{9,1},{2,10},{10,2},{3,11},{11,3},{4,12},{12,4},... | collective-permute-start | bytes 122888 | tf_op jit(solution)/shard_map/ppermute | solution.py:545
  74.8 3.5 %collective-permute-start.1 = (f32[40,256]{1,0:T(8,128)S(1)}, f32[40,256]{1,0:T(8,128)S(1)}, u32[]{:S(2)}, u32[]{:S(2)}) collective-permute-start(f32[40,256]{1,0:T(8,128)S(1)} %get-tuple-element.48), channel_id=1, source_target_pairs={{8,16},{24,32},{40,48},{56,64},{72,80},{88,96},{104,112},{120,128}... | collective-permute-start | bytes 122888 | tf_op jit(solution)/shard_map/ppermute | solution.py:546
  78.4 0.0 collective-permute-done.near
  78.4 2.1 %collective-permute-done.1.far = f32[40,256]{1,0:T(8,128)S(1)} collective-permute-done((f32[40,256]{1,0:T(8,128)S(1)}, f32[40,256]{1,0:T(8,128)S(1)}, u32[]{:S(2)}, u32[]{:S(2)}) %collective-permute-start.1) | collective-permute-done | bytes 40992 | tf_op jit(solution)/shard_map/ppermute | solution.py:546
  80.5 0.8 shard_map.73.smooth_hbm
  81.3 0.0 all-to-all-done.3.arrived
  81.3 5.0 %shard_map.74 = (f32[8,128,256]{2,1,0:T(8,128)}, f32[8,40,256]{2,1,0:T(8,128)}) custom-call(s32[2]{0:T(128)S(1)} %copy-done.5, f32[8,48,128]{2,1,0:T(8,128)S(1)} %all-to-all-done.3.arrived, f32[512,128]{1,0:T(8,128)S(1)} %select_add_fusion.band, f32[8,32,256]{2,1,0:T(8,128)S(1)} %shard_map.73.smooth_hbm, f32[8,128,256]{2,1,0:T(8,128)} %get-tuple-element.42.filled.first_hbm, ...), custom_call_target="tpu_custom_call" | custom-call | flops 1000000 | bytes 1000000 | tf_op jit(solution)/shard_map/pallas_call | solution.py:141
  86.3 14.0 %all_to_all.47.arrived = f32[8,40,256]{2,1,0:T(8,128)S(1)} all-to-all(f32[8,40,256]{2,1,0:T(8,128)} %get-tuple-element.53), channel_id=1, replica_groups=mesh['zlo'=4,'y'=8,'core'=2,'x'=4,'zhi'=2] {'x','zhi'}, dimensions={0} | all-to-all | bytes 655360 | tf_op jit(solution)/shard_map/all_to_all | solution.py:538
  100.3 0.7 shard_map.75
  101.0 3.4 %all-to-all-start.5 = ((f32[8,32,256]{2,1,0:T(8,128)}), f32[8,32,256]{2,1,0:T(8,128)S(1)}, u32[]{:S(2)}, u32[]{:S(2)}) async-start(f32[8,32,256]{2,1,0:T(8,128)} %shard_map.75), calls=%async_computation.5 | async-start | bytes 524288 | tf_op jit(solution)/shard_map/all_to_all | solution.py:538
  104.4 0.8 shard_map.76.factor.scale
  105.2 9.2 %all-to-all-done.5.modes = f32[8,32,256]{2,1,0:T(8,128)S(1)} async-done(((f32[8,32,256]{2,1,0:T(8,128)}), f32[8,32,256]{2,1,0:T(8,128)S(1)}, u32[]{:S(2)}, u32[]{:S(2)}) %all-to-all-start.5) | async-done | bytes 262176 | tf_op jit(solution)/shard_map/all_to_all | solution.py:538
  114.4 1.2 copy-done.3
  115.6 1.7 %shard_map.77 = (f32[8,40,128]{2,1,0:T(8,128)S(1)}, f32[40,256]{1,0:T(8,128)S(1)}, f32[40,256]{1,0:T(8,128)S(1)}) custom-call(s32[2]{0:T(128)S(1)} %copy-done.5, f32[8,32,256]{2,1,0:T(8,128)S(1)} %all-to-all-done.5.modes, f32[8,128,256]{2,1,0:T(8,128)S(1)} %copy-done.3, s32[8,256]{1,0:T(8,128)S(1)} %copy-done.4, f32[32,128]{1,0:T(8,128)S(1)} %shard_map.76.factor.scale), custom_call_target="tpu_custom_call" | custom-call | flops 1000000 | bytes 1000000 | tf_op jit(solution)/shard_map/pallas_call | solution.py:141
  117.4 14.7 %all_to_all.48.arrived = f32[8,40,128]{2,1,0:T(8,128)S(1)} all-to-all(f32[8,40,128]{2,1,0:T(8,128)S(1)} %get-tuple-element.55), channel_id=1, replica_groups=mesh['zlo'=4,'y'=8,'core'=2,'x'=4,'zhi'=2] {'zlo','core'}, dimensions={0} | all-to-all | bytes 327680 | tf_op jit(solution)/shard_map/all_to_all | solution.py:538
  132.1 0.7 shard_map.78
  132.8 6.8 %all-to-all-start.7 = ((f32[8,40,128]{2,1,0:T(8,128)}), f32[8,40,128]{2,1,0:T(8,128)S(1)}, u32[]{:S(2)}, u32[]{:S(2)}) async-start(f32[8,40,128]{2,1,0:T(8,128)} %shard_map.78), calls=%async_computation.7 | async-start | bytes 327680 | tf_op jit(solution)/shard_map/all_to_all | solution.py:538
  139.6 3.4 %collective-permute-start.2 = (f32[40,256]{1,0:T(8,128)S(1)}, f32[40,256]{1,0:T(8,128)S(1)}, u32[]{:S(2)}, u32[]{:S(2)}) collective-permute-start(f32[40,256]{1,0:T(8,128)S(1)} %get-tuple-element.59), channel_id=1, source_target_pairs={{0,8},{8,0},{1,9},{9,1},{2,10},{10,2},{3,11},{11,3},{4,12},{12,4},... | collective-permute-start | bytes 122888 | tf_op jit(solution)/shard_map/ppermute | solution.py:545
  143.0 3.5 %collective-permute-start.3 = (f32[40,256]{1,0:T(8,128)S(1)}, f32[40,256]{1,0:T(8,128)S(1)}, u32[]{:S(2)}, u32[]{:S(2)}) collective-permute-start(f32[40,256]{1,0:T(8,128)S(1)} %get-tuple-element.60), channel_id=1, source_target_pairs={{8,16},{24,32},{40,48},{56,64},{72,80},{88,96},{104,112},{120,128}... | collective-permute-start | bytes 122888 | tf_op jit(solution)/shard_map/ppermute | solution.py:546
  146.6 0.0 copy-done.1
  146.6 0.0 collective-permute-done.2.near
  146.6 2.0 %collective-permute-done.3.far = f32[40,256]{1,0:T(8,128)S(1)} collective-permute-done((f32[40,256]{1,0:T(8,128)S(1)}, f32[40,256]{1,0:T(8,128)S(1)}, u32[]{:S(2)}, u32[]{:S(2)}) %collective-permute-start.3) | collective-permute-done | bytes 40992 | tf_op jit(solution)/shard_map/ppermute | solution.py:546
  148.6 0.8 shard_map.79.smooth
  149.4 0.0 all-to-all-done.7.arrived
  149.4 0.7 shard_map.80
  150.1 3.4 %all-to-all-start.8 = ((f32[8,32,128]{2,1,0:T(8,128)}), f32[8,32,128]{2,1,0:T(8,128)S(1)}, u32[]{:S(2)}, u32[]{:S(2)}) async-start(f32[8,32,128]{2,1,0:T(8,128)} %get-tuple-element.62.raw), calls=%async_computation.8 | async-start | bytes 262144 | tf_op jit(solution)/shard_map/all_to_all | solution.py:538
  153.5 2.3 %shard_map.81 = (f32[128,32]{1,0:T(8,128)S(1)}, f32[32,32]{1,0:T(8,128)S(1)}, f32[32,32]{1,0:T(8,128)S(1)}) custom-call(f32[8,32,128]{2,1,0:T(8,128)} %get-tuple-element.62.raw, f32[8,128]{1,0:T(8,128)S(1)} %get-tuple-element.63.extra, f32[512,128]{1,0:T(8,128)S(1)} %select_add_fusion.band, f32[32,128]{1,0:T(8,128)S(1)} %shard_map.76.factor.scale), custom_call_target="tpu_custom_call" | custom-call | flops 1000000 | bytes 1000000 | tf_op jit(solution)/shard_map/pallas_call | solution.py:141
  155.8 1.5 shard_map.82.filled_in
  157.4 5.5 %all-to-all-done.8.arrived = f32[8,32,128]{2,1,0:T(8,128)S(1)} async-done(((f32[8,32,128]{2,1,0:T(8,128)}), f32[8,32,128]{2,1,0:T(8,128)S(1)}, u32[]{:S(2)}, u32[]{:S(2)}) %all-to-all-start.8) | async-done | bytes 131104 | tf_op jit(solution)/shard_map/all_to_all | solution.py:538
  162.8 3.7 %shard_map.83 = (f32[32,128]{1,0:T(8,128)}, f32[128,8,256]{2,1,0:T(8,128)}) custom-call(s32[2]{0:T(128)S(1)} %copy-done.5, f32[8,32,128]{2,1,0:T(8,128)S(1)} %all-to-all-done.8.arrived, f32[512,128]{1,0:T(8,128)S(1)} %select_add_fusion.band, f32[32,32]{1,0:T(8,128)S(1)} %get-tuple-element.64.factor, ...), custom_call_target="tpu_custom_call", output_to_operand_aliasing={{1}: (12, {})} | custom-call | flops 1000000 | bytes 1000000 | tf_op jit(solution)/shard_map/pallas_call | solution.py:141
  (14 shorter events, 0.1 us)
Async XLA Ops:
  4.9 25.9 %all-to-all-start = ((f32[8,56,256]{2,1,0:T(8,128)}), f32[8,56,256]{2,1,0:T(8,128)S(1)}, u32[]{:S(2)}, u32[]{:S(2)}) async-start(f32[8,56,256]{2,1,0:T(8,128)} %shard_map.68), calls=%async_computation | async-start | bytes 917504 | tf_op jit(solution)/shard_map/all_to_all | solution.py:538
  18.2 4.2 %copy-start.6 = (f32[128,7]{0,1:T(8,128)S(1)}, f32[128,7]{0,1:T(8,128)}, u32[]{:S(2)}) copy-start(f32[128,7]{0,1:T(8,128)} %param.9) | copy-start | bytes 10756
  22.4 21.0 %copy-start.2 = (f32[8,128,256]{2,1,0:T(8,128)S(1)}, f32[8,128,256]{2,1,0:T(8,128)}, u32[]{:S(2)}) copy-start(f32[8,128,256]{2,1,0:T(8,128)} %get-tuple-element.42.filled.first_hbm) | copy-start | bytes 3145732
  30.8 12.6 %copy-start.4 = (s32[8,256]{1,0:T(8,128)S(1)}, s32[8,256]{1,0:T(8,128)}, u32[]{:S(2)}) copy-start(s32[8,256]{1,0:T(8,128)} %land.15) | copy-start | bytes 24580
  30.8 12.6 %copy-start.5 = (s32[2]{0:T(128)S(1)}, s32[2]{0:T(128)}, u32[]{:S(2)}) copy-start(s32[2]{0:T(128)} %pad_add_fusion.day) | copy-start | bytes 28
  63.9 17.4 %all-to-all-start.3 = ((f32[8,48,128]{2,1,0:T(8,128)}), f32[8,48,128]{2,1,0:T(8,128)S(1)}, u32[]{:S(2)}, u32[]{:S(2)}) async-start(f32[8,48,128]{2,1,0:T(8,128)} %shard_map.72), calls=%async_computation.3 | async-start | bytes 393216 | tf_op jit(solution)/shard_map/all_to_all | solution.py:538
  70.8 7.6 %collective-permute-start = (f32[40,256]{1,0:T(8,128)S(1)}, f32[40,256]{1,0:T(8,128)S(1)}, u32[]{:S(2)}, u32[]{:S(2)}) collective-permute-start(f32[40,256]{1,0:T(8,128)S(1)} %get-tuple-element.47), channel_id=1, source_target_pairs={{0,8},{8,0},{1,9},{9,1},{2,10},{10,2},{3,11},{11,3},{4,12},{12,4},... | collective-permute-start | bytes 122888 | tf_op jit(solution)/shard_map/ppermute | solution.py:545
  74.8 5.7 %collective-permute-start.1 = (f32[40,256]{1,0:T(8,128)S(1)}, f32[40,256]{1,0:T(8,128)S(1)}, u32[]{:S(2)}, u32[]{:S(2)}) collective-permute-start(f32[40,256]{1,0:T(8,128)S(1)} %get-tuple-element.48), channel_id=1, source_target_pairs={{8,16},{24,32},{40,48},{56,64},{72,80},{88,96},{104,112},{120,128}... | collective-permute-start | bytes 122888 | tf_op jit(solution)/shard_map/ppermute | solution.py:546
  101.0 13.4 %all-to-all-start.5 = ((f32[8,32,256]{2,1,0:T(8,128)}), f32[8,32,256]{2,1,0:T(8,128)S(1)}, u32[]{:S(2)}, u32[]{:S(2)}) async-start(f32[8,32,256]{2,1,0:T(8,128)} %shard_map.75), calls=%async_computation.5 | async-start | bytes 524288 | tf_op jit(solution)/shard_map/all_to_all | solution.py:538
  114.4 1.2 copy-start.3
  115.6 30.9 %copy-start.1 = (s32[128,8,256]{2,1,0:T(8,128)S(1)}, s32[128,8,256]{2,1,0:T(8,128)}, u32[]{:S(2)}) copy-start(s32[128,8,256]{2,1,0:T(8,128)} %missing.1) | copy-start | bytes 3145732
  132.1 21.4 %copy-start = (f32[128,8,256]{2,1,0:T(8,128)S(1)}, f32[128,8,256]{2,1,0:T(8,128)}, u32[]{:S(2)}) copy-start(f32[128,8,256]{2,1,0:T(8,128)} %observed.1) | copy-start | bytes 3145732
  132.8 16.6 %all-to-all-start.7 = ((f32[8,40,128]{2,1,0:T(8,128)}), f32[8,40,128]{2,1,0:T(8,128)S(1)}, u32[]{:S(2)}, u32[]{:S(2)}) async-start(f32[8,40,128]{2,1,0:T(8,128)} %shard_map.78), calls=%async_computation.7 | async-start | bytes 327680 | tf_op jit(solution)/shard_map/all_to_all | solution.py:538
  139.6 7.0 %collective-permute-start.2 = (f32[40,256]{1,0:T(8,128)S(1)}, f32[40,256]{1,0:T(8,128)S(1)}, u32[]{:S(2)}, u32[]{:S(2)}) collective-permute-start(f32[40,256]{1,0:T(8,128)S(1)} %get-tuple-element.59), channel_id=1, source_target_pairs={{0,8},{8,0},{1,9},{9,1},{2,10},{10,2},{3,11},{11,3},{4,12},{12,4},... | collective-permute-start | bytes 122888 | tf_op jit(solution)/shard_map/ppermute | solution.py:545
  143.0 5.6 %collective-permute-start.3 = (f32[40,256]{1,0:T(8,128)S(1)}, f32[40,256]{1,0:T(8,128)S(1)}, u32[]{:S(2)}, u32[]{:S(2)}) collective-permute-start(f32[40,256]{1,0:T(8,128)S(1)} %get-tuple-element.60), channel_id=1, source_target_pairs={{8,16},{24,32},{40,48},{56,64},{72,80},{88,96},{104,112},{120,128}... | collective-permute-start | bytes 122888 | tf_op jit(solution)/shard_map/ppermute | solution.py:546
  150.1 12.8 %all-to-all-start.8 = ((f32[8,32,128]{2,1,0:T(8,128)}), f32[8,32,128]{2,1,0:T(8,128)S(1)}, u32[]{:S(2)}, u32[]{:S(2)}) async-start(f32[8,32,128]{2,1,0:T(8,128)} %get-tuple-element.62.raw), calls=%async_computation.8 | async-start | bytes 262144 | tf_op jit(solution)/shard_map/all_to_all | solution.py:538

commit v7 on v6

--- a/solution.py
+++ b/solution.py
@@ -303,34 +303,57 @@
     out[:, K:] = jnp.zeros((K, LANES - K), f32)
 
 
-def edges_of(day, modes, land, edge_near, edge_far):
+def edges_of(modes, land, edge_low, edge_high):
     ocean = 1.0 - land[...].astype(f32)
-    upper = day[1] == 0
-    for edge, r, q in ((edge_near, 7, 0), (edge_far, 0, 7)):
-        edge[:K, :] = jnp.where(upper, modes[r], modes[q])
-        flag = jnp.where(upper, ocean[r : r + 1], ocean[q : q + 1])
-        edge[K:, :] = jnp.broadcast_to(flag, (8, ocean.shape[1]))
-
-
-def project_again_body(day, modes, filled, land, factor, out, edge_near, edge_far):
+    for edge, r in ((edge_low, 0), (edge_high, 7)):
+        edge[:K, :] = modes[r]
+        edge[K:, :] = jnp.broadcast_to(ocean[r : r + 1], (8, ocean.shape[1]))
+
+
+class Products:
+    def __init__(self, count):
+        self.count = count
+        self.totals = [jnp.zeros((count, K * (3 - i)), f32) for i in range(3)]
+
+    def add(self, few, many):
+        stack = parts_of(few)
+        for i, part in enumerate(split(many)):
+            self.totals[i] = self.totals[i] + lax.dot_general(
+                part,
+                stack[: K * (3 - i)],
+                (((1,), (1,)), ((), ())),
+                preferred_element_type=f32,
+            )
+
+    def result(self):
+        found = None
+        for i, total in enumerate(self.totals):
+            tall = ((0, 2 * LANES - self.count), (0, LANES - total.shape[1]))
+            total = jnp.pad(total, tall).T
+            for j in range(3 - i):
+                piece = total[K * j : K * j + K]
+                found = piece if found is None else found + piece
+        return found
+
+
+def project_again_body(modes, filled, land, factor, out, edge_low, edge_high):
     cols = modes.shape[2]
     wide = jnp.concatenate([modes[r] for r in range(8)], axis=1)
     wide = mul_deep(deep_parts_of(factor[:, :K]), wide)
-    pad = jnp.zeros((LANES - K, cols), f32)
-    total = jnp.zeros((K, 2 * LANES), f32)
+    products = Products(LANES + K)
     for r in range(8):
         modes_u = wide[:, cols * r : cols * r + cols]
-        right = jnp.concatenate([filled[r], modes_u, pad], axis=0)
-        total = total + mul_few(parts_of(modes_u), right, 1)
+        products.add(modes_u, jnp.concatenate([filled[r], modes_u], axis=0))
+    total = products.result()
     packed = pack_rows(total[:, LANES:])
     for j in range(out.shape[0]):
         out[j, :K, :] = total[:, :LANES]
         out[j, K:, :] = packed
-    edges_of(day, modes, land, edge_near, edge_far)
+    edges_of(modes, land, edge_low, edge_high)
 
 
 def project_body(
-    day, arrived, modes, filled, land, out, edge_near, edge_far, halo_0, halo_1
+    day, arrived, modes, filled, land, out, edge_low, edge_high, halo_0, halo_1
 ):
     d = day[0]
     low = arrived[jnp.maximum(d - 1, 0), K : K + HALO, :]
@@ -342,25 +365,23 @@
         halo[:HALO, :] = low[:, LANES * c : LANES * c + LANES]
         halo[HALO : 2 * HALO, :] = high[:, LANES * c : LANES * c + LANES]
         halo[2 * HALO :, :] = jnp.zeros((64 - 2 * HALO, LANES), f32)
-    pad = jnp.zeros((LANES - K - 8, cols), f32)
-    total = jnp.zeros((K, 2 * LANES), f32)
+    pad = jnp.zeros((8, cols), f32)
+    products = Products(LANES + K + 16)
     for r in range(8):
         modes_u = modes[r]
         days_near = rows_of((halo_0, halo_1), r, 8)
         right = jnp.concatenate([filled[r], modes_u, days_near, pad], axis=0)
-        total = total + mul_few(parts_of(modes_u), right, 1)
+        products.add(modes_u, right)
+    total = products.result()
     extra = total[:, LANES:]
     packed = extra[:16] + pltpu.roll(extra[16:], 64, 1)
     for j in range(out.shape[0]):
         out[j, :K, :] = total[:, :LANES]
         out[j, K:, :] = packed
-    edges_of(day, modes, land, edge_near, edge_far)
-
-
-def smooth_body(day, modes, near, far, land, out):
-    upper = day[1] == 0
-    above = jnp.where(upper, far[...], near[...])
-    below = jnp.where(upper, near[...], far[...])
+    edges_of(modes, land, edge_low, edge_high)
+
+
+def smooth_body(modes, above, below, land, out):
     cols = out.shape[2]
     lane = lax.broadcasted_iota(jnp.int32, (1, cols), 1)
     ocean = 1.0 - land[...].astype(f32)
@@ -538,12 +559,11 @@
     return lax.all_to_all(blocks, axes, 0, 0)
 
 
-def near_rows(edge_near, edge_far):
+def near_rows(edge_low, edge_high):
     count = lax.axis_size(PIX)
-    up = [(i, i + 1) for i in range(1, count - 1, 2)]
-    down = [(i + 1, i) for i in range(1, count - 1, 2)]
-    near = lax.ppermute(edge_near, "core", [(0, 1), (1, 0)])
-    return near, lax.ppermute(edge_far, PIX, up + down)
+    up = [(i, i + 1) for i in range(count - 1)]
+    down = [(i + 1, i) for i in range(count - 1)]
+    return lax.ppermute(edge_high, PIX, up), lax.ppermute(edge_low, PIX, down)
 
 
 def band_of(day_weights):
@@ -567,7 +587,7 @@
 
 def per_device(observed, missing, land, basis_start, day_weights):
     days, rows, cols = observed.shape
-    day = jnp.stack([lax.axis_index(DAY), lax.axis_index("core")])
+    day = lax.axis_index(DAY).reshape(1)
     near, far = lax.axis_size(NEAR), lax.axis_size("y")
     halo = [pltpu.VMEM((64, LANES), f32)] * 2
     halves = [pltpu.VMEM((days * rows, LANES), f32)] * 2
@@ -579,9 +599,9 @@
         return lax.optimization_barrier((joint, *edges))
 
     def smooth_beside(joint, low, high, modes):
-        beside, beyond = near_rows(low, high)
+        above, below = near_rows(low, high)
         joint = swap(joint, "y")
-        smooth = call(smooth_body, block, (day, modes, beside, beyond, land))
+        smooth = call(smooth_body, block, (modes, above, below, land))
         return lax.optimization_barrier((joint, smooth))
 
     slab = pltpu.VMEM((days, rows, cols), f32)
@@ -653,7 +673,7 @@
     joint, *edges = call(
         project_again_body,
         [(near, K + 8, LANES), edge, edge],
-        (day, modes, filled, land, factor),
+        (modes, filled, land, factor),
     )
     joint, low, high = add_near(joint, edges)
     joint, smooth = smooth_beside(joint, low, high, modes)

time: 168 us -> 165 us (0.982)
  waiting for transfers between devices: 26.4 us -> 31.9 us
  Pallas kernels: 28.7 us -> 24.5 us
  blocking collectives: 59.6 us -> 57.1 us
    pallas_call x16, Pallas kernels: 28.7 us -> 24.5 us  [call(): pl.pallas_call(body, out_shape=shapes if many else shapes[0], in_specs=sp...]
    ppermute x4, waiting for transfers between devices: 4.16 us -> 7.24 us  [near_rows(): return (lax.ppermute(edge_high, PIX, up), lax.ppermute(edge_low, PIX, down))]
    all_to_all x4, blocking collectives: 59.6 us -> 57.1 us  [swap(): return lax.all_to_all(blocks, axes, 0, 0)]
    all_to_all x5, waiting for transfers between devices: 22.3 us -> 24.6 us  [swap(): return lax.all_to_all(blocks, axes, 0, 0)]
where the time goes in v7:
time: 165 us; the launch traced here: 163 us
  blocking collectives  57.1 us (35%)
  starting transfers between devices  46.9 us (28%)
  waiting for transfers between devices  31.9 us (19%)
  Pallas kernels  24.5 us (15%)
    all_to_all x4, blocking collectives, swap(): return lax.all_to_all(blocks, axes, 0, 0)  57.1 us
    all_to_all x5, starting transfers between devices, swap(): return lax.all_to_all(blocks, axes, 0, 0)  32.4 us
    all_to_all x5, waiting for transfers between devices, swap(): return lax.all_to_all(blocks, axes, 0, 0)  24.6 us
    pallas_call x16, Pallas kernels, call(): pl.pallas_call(body, out_shape=shapes if many else shapes[0], in_specs=sp...  24.5 us
    ppermute x4, starting transfers between devices, near_rows(): return (lax.ppermute(edge_high, PIX, up), lax.ppermute(edge_low, PIX, down))  14.6 us
    ppermute x4, waiting for transfers between devices, near_rows(): return (lax.ppermute(edge_high, PIX, up), lax.ppermute(edge_low, PIX, down))  7.24 us
  transfers between devices with their start and end apart: 9, of which 5 were waited for; matrix products, arithmetic and copies ran while one was open for 0% of the time, Pallas kernels for 6%

profile of v7, /device:TPU:1, one launch (start us, length us, event | category | flops | bytes accessed | tf_op | source)
XLA Modules:
  0.0 163.3 jit_solution(11023160321866367522)
XLA Ops:
  0.6 2.9 %shard_map.68 = f32[8,56,256]{2,1,0:T(8,128)} custom-call(s32[1]{0:T(128)} %bitcast.day, f32[128,8,256]{2,1,0:T(8,128)} %observed.1, s32[128,8,256]{2,1,0:T(8,128)} %missing.1, s32[8,256]{1,0:T(8,128)} %land.15, f32[32,128]{1,0:T(8,128)} %bitcast.18), custom_call_target="tpu_custom_call" | custom-call | flops 1000000 | bytes 1000000 | tf_op jit(solution)/shard_map/pallas_call | solution.py:141
  3.6 13.3 %all-to-all-start = ((f32[8,56,256]{2,1,0:T(8,128)}), f32[8,56,256]{2,1,0:T(8,128)S(1)}, u32[]{:S(2)}, u32[]{:S(2)}) async-start(f32[8,56,256]{2,1,0:T(8,128)} %shard_map.68), calls=%async_computation | async-start | bytes 917504 | tf_op jit(solution)/shard_map/all_to_all | solution.py:559
  16.9 0.0 copy-start.5
  16.9 4.1 %shard_map.69 = (f32[8,128,256]{2,1,0:T(8,128)}, bf16[8,128,256]{2,1,0:T(8,128)(2,1)}) custom-call(f32[128,8,256]{2,1,0:T(8,128)} %observed.1, s32[128,8,256]{2,1,0:T(8,128)} %missing.1, s32[8,256]{1,0:T(8,128)} %land.15), custom_call_target="tpu_custom_call" | custom-call | flops 1000000 | bytes 1000000 | tf_op jit(solution)/shard_map/pallas_call | solution.py:141
  21.0 0.0 copy-start.2
  21.1 0.0 copy-done.5
  21.1 0.7 select_add_fusion.band
  21.8 7.6 %all-to-all-done.arrived = f32[8,56,256]{2,1,0:T(8,128)S(1)} async-done(((f32[8,56,256]{2,1,0:T(8,128)}), f32[8,56,256]{2,1,0:T(8,128)S(1)}, u32[]{:S(2)}, u32[]{:S(2)}) %all-to-all-start) | async-done | bytes 458784 | tf_op jit(solution)/shard_map/all_to_all | solution.py:559
  29.5 0.0 copy-start.4
  29.5 12.6 %all_to_all.45.modes = f32[8,32,256]{2,1,0:T(8,128)S(1)} all-to-all(f32[8,32,256]{2,1,0:T(8,128)S(1)} %shard_map.70), channel_id=1, replica_groups=mesh['zlo'=4,'y'=8,'core'=2,'x'=4,'zhi'=2] {'x','zhi'}, dimensions={0} | all-to-all | bytes 524288 | tf_op jit(solution)/shard_map/all_to_all | solution.py:559
  42.1 0.0 copy-done.2
  42.1 0.0 copy-done.4
  42.1 0.9 shard_map.71
  43.0 18.3 %all_to_all.46.arrived = f32[8,48,128]{2,1,0:T(8,128)S(1)} all-to-all(f32[8,48,128]{2,1,0:T(8,128)S(1)} %get-tuple-element.43), channel_id=1, replica_groups=mesh['zlo'=4,'y'=8,'core'=2,'x'=4,'zhi'=2] {'zlo','core'}, dimensions={0} | all-to-all | bytes 393216 | tf_op jit(solution)/shard_map/all_to_all | solution.py:559
  61.3 0.7 shard_map.72
  62.0 6.8 %all-to-all-start.3 = ((f32[8,48,128]{2,1,0:T(8,128)}), f32[8,48,128]{2,1,0:T(8,128)S(1)}, u32[]{:S(2)}, u32[]{:S(2)}) async-start(f32[8,48,128]{2,1,0:T(8,128)} %shard_map.72), calls=%async_computation.3 | async-start | bytes 393216 | tf_op jit(solution)/shard_map/all_to_all | solution.py:559
  68.8 5.7 %collective-permute-start = (f32[40,256]{1,0:T(8,128)S(1)}, f32[40,256]{1,0:T(8,128)S(1)}, u32[]{:S(2)}, u32[]{:S(2)}) collective-permute-start(f32[40,256]{1,0:T(8,128)S(1)} %get-tuple-element.47), channel_id=1, source_target_pairs={{0,8},{8,16},{16,24},{24,32},{32,40},{40,48},{48,56},{56,64},{64,7... | collective-permute-start | bytes 122888 | tf_op jit(solution)/shard_map/ppermute | solution.py:566
  74.5 1.9 %collective-permute-start.1 = (f32[40,256]{1,0:T(8,128)S(1)}, f32[40,256]{1,0:T(8,128)S(1)}, u32[]{:S(2)}, u32[]{:S(2)}) collective-permute-start(f32[40,256]{1,0:T(8,128)S(1)} %get-tuple-element.48), channel_id=1, source_target_pairs={{8,0},{16,8},{24,16},{32,24},{40,32},{48,40},{56,48},{64,56},{72,6... | collective-permute-start | bytes 122888 | tf_op jit(solution)/shard_map/ppermute | solution.py:566
  76.4 0.0 collective-permute-done.above
  76.4 3.7 %collective-permute-done.1.below = f32[40,256]{1,0:T(8,128)S(1)} collective-permute-done((f32[40,256]{1,0:T(8,128)S(1)}, f32[40,256]{1,0:T(8,128)S(1)}, u32[]{:S(2)}, u32[]{:S(2)}) %collective-permute-start.1) | collective-permute-done | bytes 40992 | tf_op jit(solution)/shard_map/ppermute | solution.py:566
  80.1 0.2 shard_map.73.smooth_hbm
  80.3 0.0 all-to-all-done.3.arrived
  80.4 4.4 %shard_map.74 = (f32[8,128,256]{2,1,0:T(8,128)}, f32[8,40,256]{2,1,0:T(8,128)}) custom-call(s32[1]{0:T(128)} %bitcast.day, f32[8,48,128]{2,1,0:T(8,128)S(1)} %all-to-all-done.3.arrived, f32[512,128]{1,0:T(8,128)S(1)} %select_add_fusion.band, f32[8,32,256]{2,1,0:T(8,128)S(1)} %shard_map.73.smooth_hbm, f32[8,128,256]{2,1,0:T(8,128)} %get-tuple-element.42.filled.first_hbm, ...), custom_call_target="tpu_custom_call" | custom-call | flops 1000000 | bytes 1000000 | tf_op jit(solution)/shard_map/pallas_call | solution.py:141
  84.8 15.7 %all_to_all.47.arrived = f32[8,40,256]{2,1,0:T(8,128)S(1)} all-to-all(f32[8,40,256]{2,1,0:T(8,128)} %get-tuple-element.53), channel_id=1, replica_groups=mesh['zlo'=4,'y'=8,'core'=2,'x'=4,'zhi'=2] {'x','zhi'}, dimensions={0} | all-to-all | bytes 655360 | tf_op jit(solution)/shard_map/all_to_all | solution.py:559
  100.4 0.7 shard_map.75
  101.2 4.2 %all-to-all-start.5 = ((f32[8,32,256]{2,1,0:T(8,128)}), f32[8,32,256]{2,1,0:T(8,128)S(1)}, u32[]{:S(2)}, u32[]{:S(2)}) async-start(f32[8,32,256]{2,1,0:T(8,128)} %shard_map.75), calls=%async_computation.5 | async-start | bytes 524288 | tf_op jit(solution)/shard_map/all_to_all | solution.py:559
  105.3 0.8 shard_map.76.factor.scale
  106.2 11.5 %all-to-all-done.5.modes = f32[8,32,256]{2,1,0:T(8,128)S(1)} async-done(((f32[8,32,256]{2,1,0:T(8,128)}), f32[8,32,256]{2,1,0:T(8,128)S(1)}, u32[]{:S(2)}, u32[]{:S(2)}) %all-to-all-start.5) | async-done | bytes 262176 | tf_op jit(solution)/shard_map/all_to_all | solution.py:559
  117.6 0.0 copy-start.3
  117.6 1.2 copy-done.3
  118.8 1.0 shard_map.77
  119.9 10.6 %all_to_all.48.arrived = f32[8,40,128]{2,1,0:T(8,128)S(1)} all-to-all(f32[8,40,128]{2,1,0:T(8,128)S(1)} %get-tuple-element.55), channel_id=1, replica_groups=mesh['zlo'=4,'y'=8,'core'=2,'x'=4,'zhi'=2] {'zlo','core'}, dimensions={0} | all-to-all | bytes 327680 | tf_op jit(solution)/shard_map/all_to_all | solution.py:559
  130.5 0.7 shard_map.78
  131.1 4.7 %all-to-all-start.7 = ((f32[8,40,128]{2,1,0:T(8,128)}), f32[8,40,128]{2,1,0:T(8,128)S(1)}, u32[]{:S(2)}, u32[]{:S(2)}) async-start(f32[8,40,128]{2,1,0:T(8,128)} %shard_map.78), calls=%async_computation.7 | async-start | bytes 327680 | tf_op jit(solution)/shard_map/all_to_all | solution.py:559
  135.8 5.0 %collective-permute-start.2 = (f32[40,256]{1,0:T(8,128)S(1)}, f32[40,256]{1,0:T(8,128)S(1)}, u32[]{:S(2)}, u32[]{:S(2)}) collective-permute-start(f32[40,256]{1,0:T(8,128)S(1)} %get-tuple-element.59), channel_id=1, source_target_pairs={{0,8},{8,16},{16,24},{24,32},{32,40},{40,48},{48,56},{56,64},{64,7... | collective-permute-start | bytes 122888 | tf_op jit(solution)/shard_map/ppermute | solution.py:566
  140.9 1.9 %collective-permute-start.3 = (f32[40,256]{1,0:T(8,128)S(1)}, f32[40,256]{1,0:T(8,128)S(1)}, u32[]{:S(2)}, u32[]{:S(2)}) collective-permute-start(f32[40,256]{1,0:T(8,128)S(1)} %get-tuple-element.60), channel_id=1, source_target_pairs={{8,0},{16,8},{24,16},{32,24},{40,32},{48,40},{56,48},{64,56},{72,6... | collective-permute-start | bytes 122888 | tf_op jit(solution)/shard_map/ppermute | solution.py:566
  142.8 0.0 copy-done.1
  142.8 0.0 collective-permute-done.2.above
  142.9 3.6 %collective-permute-done.3.below = f32[40,256]{1,0:T(8,128)S(1)} collective-permute-done((f32[40,256]{1,0:T(8,128)S(1)}, f32[40,256]{1,0:T(8,128)S(1)}, u32[]{:S(2)}, u32[]{:S(2)}) %collective-permute-start.3) | collective-permute-done | bytes 40992 | tf_op jit(solution)/shard_map/ppermute | solution.py:566
  146.4 0.2 shard_map.79.smooth
  146.7 0.0 all-to-all-done.7.arrived
  146.7 0.7 shard_map.80
  147.3 3.4 %all-to-all-start.8 = ((f32[8,32,128]{2,1,0:T(8,128)}), f32[8,32,128]{2,1,0:T(8,128)S(1)}, u32[]{:S(2)}, u32[]{:S(2)}) async-start(f32[8,32,128]{2,1,0:T(8,128)} %get-tuple-element.62.raw), calls=%async_computation.8 | async-start | bytes 262144 | tf_op jit(solution)/shard_map/all_to_all | solution.py:559
  150.7 0.0 copy-done
  150.7 2.3 %shard_map.81 = (f32[128,32]{1,0:T(8,128)S(1)}, f32[32,32]{1,0:T(8,128)S(1)}, f32[32,32]{1,0:T(8,128)S(1)}) custom-call(f32[8,32,128]{2,1,0:T(8,128)} %get-tuple-element.62.raw, f32[8,128]{1,0:T(8,128)S(1)} %get-tuple-element.63.extra, f32[512,128]{1,0:T(8,128)S(1)} %select_add_fusion.band, f32[32,128]{1,0:T(8,128)S(1)} %shard_map.76.factor.scale), custom_call_target="tpu_custom_call" | custom-call | flops 1000000 | bytes 1000000 | tf_op jit(solution)/shard_map/pallas_call | solution.py:141
  153.1 1.5 shard_map.82.filled_in
  154.6 5.5 %all-to-all-done.8.arrived = f32[8,32,128]{2,1,0:T(8,128)S(1)} async-done(((f32[8,32,128]{2,1,0:T(8,128)}), f32[8,32,128]{2,1,0:T(8,128)S(1)}, u32[]{:S(2)}, u32[]{:S(2)}) %all-to-all-start.8) | async-done | bytes 131104 | tf_op jit(solution)/shard_map/all_to_all | solution.py:559
  160.1 3.2 %shard_map.83 = (f32[32,128]{1,0:T(8,128)}, f32[128,8,256]{2,1,0:T(8,128)}) custom-call(s32[1]{0:T(128)} %bitcast.day, f32[8,32,128]{2,1,0:T(8,128)S(1)} %all-to-all-done.8.arrived, f32[512,128]{1,0:T(8,128)S(1)} %select_add_fusion.band, f32[32,32]{1,0:T(8,128)S(1)} %get-tuple-element.64.factor, ...), custom_call_target="tpu_custom_call", output_to_operand_aliasing={{1}: (12, {})} | custom-call | flops 1000000 | bytes 1000000 | tf_op jit(solution)/shard_map/pallas_call | solution.py:141
  (11 shorter events, 0.1 us)
Async XLA Ops:
  3.6 25.9 %all-to-all-start = ((f32[8,56,256]{2,1,0:T(8,128)}), f32[8,56,256]{2,1,0:T(8,128)S(1)}, u32[]{:S(2)}, u32[]{:S(2)}) async-start(f32[8,56,256]{2,1,0:T(8,128)} %shard_map.68), calls=%async_computation | async-start | bytes 917504 | tf_op jit(solution)/shard_map/all_to_all | solution.py:559
  16.9 4.2 %copy-start.5 = (f32[128,7]{0,1:T(8,128)S(1)}, f32[128,7]{0,1:T(8,128)}, u32[]{:S(2)}) copy-start(f32[128,7]{0,1:T(8,128)} %param.9) | copy-start | bytes 10756
  21.0 21.0 %copy-start.2 = (f32[8,128,256]{2,1,0:T(8,128)S(1)}, f32[8,128,256]{2,1,0:T(8,128)}, u32[]{:S(2)}) copy-start(f32[8,128,256]{2,1,0:T(8,128)} %get-tuple-element.42.filled.first_hbm) | copy-start | bytes 3145732
  29.5 12.6 %copy-start.4 = (s32[8,256]{1,0:T(8,128)S(1)}, s32[8,256]{1,0:T(8,128)}, u32[]{:S(2)}) copy-start(s32[8,256]{1,0:T(8,128)} %land.15) | copy-start | bytes 24580
  62.0 18.4 %all-to-all-start.3 = ((f32[8,48,128]{2,1,0:T(8,128)}), f32[8,48,128]{2,1,0:T(8,128)S(1)}, u32[]{:S(2)}, u32[]{:S(2)}) async-start(f32[8,48,128]{2,1,0:T(8,128)} %shard_map.72), calls=%async_computation.3 | async-start | bytes 393216 | tf_op jit(solution)/shard_map/all_to_all | solution.py:559
  68.8 7.6 %collective-permute-start = (f32[40,256]{1,0:T(8,128)S(1)}, f32[40,256]{1,0:T(8,128)S(1)}, u32[]{:S(2)}, u32[]{:S(2)}) collective-permute-start(f32[40,256]{1,0:T(8,128)S(1)} %get-tuple-element.47), channel_id=1, source_target_pairs={{0,8},{8,16},{16,24},{24,32},{32,40},{40,48},{48,56},{56,64},{64,7... | collective-permute-start | bytes 122888 | tf_op jit(solution)/shard_map/ppermute | solution.py:566
  74.5 5.6 %collective-permute-start.1 = (f32[40,256]{1,0:T(8,128)S(1)}, f32[40,256]{1,0:T(8,128)S(1)}, u32[]{:S(2)}, u32[]{:S(2)}) collective-permute-start(f32[40,256]{1,0:T(8,128)S(1)} %get-tuple-element.48), channel_id=1, source_target_pairs={{8,0},{16,8},{24,16},{32,24},{40,32},{48,40},{56,48},{64,56},{72,6... | collective-permute-start | bytes 122888 | tf_op jit(solution)/shard_map/ppermute | solution.py:566
  101.2 16.5 %all-to-all-start.5 = ((f32[8,32,256]{2,1,0:T(8,128)}), f32[8,32,256]{2,1,0:T(8,128)S(1)}, u32[]{:S(2)}, u32[]{:S(2)}) async-start(f32[8,32,256]{2,1,0:T(8,128)} %shard_map.75), calls=%async_computation.5 | async-start | bytes 524288 | tf_op jit(solution)/shard_map/all_to_all | solution.py:559
  117.6 1.2 copy-start.3
  118.8 24.0 %copy-start.1 = (s32[128,8,256]{2,1,0:T(8,128)S(1)}, s32[128,8,256]{2,1,0:T(8,128)}, u32[]{:S(2)}) copy-start(s32[128,8,256]{2,1,0:T(8,128)} %missing.1) | copy-start | bytes 3145732
  130.4 20.3 %copy-start = (f32[128,8,256]{2,1,0:T(8,128)S(1)}, f32[128,8,256]{2,1,0:T(8,128)}, u32[]{:S(2)}) copy-start(f32[128,8,256]{2,1,0:T(8,128)} %observed.1) | copy-start | bytes 3145732
  131.1 15.5 %all-to-all-start.7 = ((f32[8,40,128]{2,1,0:T(8,128)}), f32[8,40,128]{2,1,0:T(8,128)S(1)}, u32[]{:S(2)}, u32[]{:S(2)}) async-start(f32[8,40,128]{2,1,0:T(8,128)} %shard_map.78), calls=%async_computation.7 | async-start | bytes 327680 | tf_op jit(solution)/shard_map/all_to_all | solution.py:559
  135.8 7.0 %collective-permute-start.2 = (f32[40,256]{1,0:T(8,128)S(1)}, f32[40,256]{1,0:T(8,128)S(1)}, u32[]{:S(2)}, u32[]{:S(2)}) collective-permute-start(f32[40,256]{1,0:T(8,128)S(1)} %get-tuple-element.59), channel_id=1, source_target_pairs={{0,8},{8,16},{16,24},{24,32},{32,40},{40,48},{48,56},{56,64},{64,7... | collective-permute-start | bytes 122888 | tf_op jit(solution)/shard_map/ppermute | solution.py:566
  140.9 5.5 %collective-permute-start.3 = (f32[40,256]{1,0:T(8,128)S(1)}, f32[40,256]{1,0:T(8,128)S(1)}, u32[]{:S(2)}, u32[]{:S(2)}) collective-permute-start(f32[40,256]{1,0:T(8,128)S(1)} %get-tuple-element.60), channel_id=1, source_target_pairs={{8,0},{16,8},{24,16},{32,24},{40,32},{48,40},{56,48},{64,56},{72,6... | collective-permute-start | bytes 122888 | tf_op jit(solution)/shard_map/ppermute | solution.py:566
  147.3 12.8 %all-to-all-start.8 = ((f32[8,32,128]{2,1,0:T(8,128)}), f32[8,32,128]{2,1,0:T(8,128)S(1)}, u32[]{:S(2)}, u32[]{:S(2)}) async-start(f32[8,32,128]{2,1,0:T(8,128)} %get-tuple-element.62.raw), calls=%async_computation.8 | async-start | bytes 262144 | tf_op jit(solution)/shard_map/all_to_all | solution.py:559

commit v8 on v7

--- a/solution.py
+++ b/solution.py
@@ -131,7 +131,7 @@
         specs.append(pl.BlockSpec(memory_space=pl.ANY if i in anywhere else space))
     many = isinstance(outs, list)
     shapes = [
-        s if isinstance(s, jax.ShapeDtypeStruct) else jax.ShapeDtypeStruct(s, f32)
+        jax.ShapeDtypeStruct(s, f32) if isinstance(s, tuple) else s
         for s in (outs if many else [outs])
     ]
     out_specs = [
@@ -336,12 +336,23 @@
         return found
 
 
-def project_again_body(modes, filled, land, factor, out, edge_low, edge_high):
+def project_again_body(
+    modes, filled_hbm, land, factor, out, edge_low, edge_high, filled, arrivals
+):
+    copies = [
+        pltpu.make_async_copy(filled_hbm.at[r], filled.at[r], arrivals.at[r])
+        for r in range(8)
+    ]
+    for copy in copies:
+        copy.start()
     cols = modes.shape[2]
     wide = jnp.concatenate([modes[r] for r in range(8)], axis=1)
     wide = mul_deep(deep_parts_of(factor[:, :K]), wide)
     products = Products(LANES + K)
     for r in range(8):
+        if r % 2 == 0:
+            copies[r].wait()
+            copies[r + 1].wait()
         modes_u = wide[:, cols * r : cols * r + cols]
         products.add(modes_u, jnp.concatenate([filled[r], modes_u], axis=0))
     total = products.result()
@@ -594,13 +605,13 @@
     edge = (K + 8, cols)
     block = (rows, K, cols)
 
-    def add_near(joint, edges):
-        joint = call(add_all_body, (far,) + joint.shape[1:], (swap(joint, NEAR),))
+    def add_first(joint, edges):
+        joint = call(add_all_body, (near,) + joint.shape[1:], (swap(joint, "y"),))
         return lax.optimization_barrier((joint, *edges))
 
     def smooth_beside(joint, low, high, modes):
         above, below = near_rows(low, high)
-        joint = swap(joint, "y")
+        joint = swap(joint, NEAR)
         smooth = call(smooth_body, block, (modes, above, below, land))
         return lax.optimization_barrier((joint, smooth))
 
@@ -644,11 +655,11 @@
     modes = swap(call(add_rows_body, block, (arrived,)), DAY)
     joint, *edges = call(
         project_body,
-        [(near, K + 16, LANES), edge, edge],
+        [(far, K + 16, LANES), edge, edge],
         (day, arrived, modes, first, land),
         halo,
     )
-    joint, low, high = add_near(joint, edges)
+    joint, low, high = add_first(joint, edges)
     joint, smooth = smooth_beside(joint, low, high, modes)
     filled, part = call(
         refill_body,
@@ -672,10 +683,13 @@
     factor = call(factor_body, (K, LANES), (arrived,))
     joint, *edges = call(
         project_again_body,
-        [(near, K + 8, LANES), edge, edge],
+        [(far, K + 8, LANES), edge, edge],
         (modes, filled, land, factor),
-    )
-    joint, low, high = add_near(joint, edges)
+        [turned, pltpu.SemaphoreType.DMA((8,))],
+        limit=53,
+        anywhere=(1,),
+    )
+    joint, low, high = add_first(joint, edges)
     joint, smooth = smooth_beside(joint, low, high, modes)
     raw, extra = call(add_last_body, [(8, K, LANES), (8, LANES)], (joint,))
     arrived = swap(raw, DAY)

time: 165 us -> 168 us (1.018)
  starting transfers between devices: 46.9 us -> 51.7 us
  waiting for transfers between devices: 31.9 us -> 29.4 us
    all_to_all x5, starting transfers between devices: 32.4 us -> 43.1 us  [swap(): return lax.all_to_all(blocks, axes, 0, 0)]
    ppermute x4, starting transfers between devices: 14.6 us -> 8.63 us  [near_rows(): return (lax.ppermute(edge_high, PIX, up), lax.ppermute(edge_low, PIX, down))]
where the time goes in v8:
time: 168 us; the launch traced here: 166 us
  blocking collectives  56.9 us (34%)
  starting transfers between devices  51.7 us (31%)
  waiting for transfers between devices  29.4 us (18%)
  Pallas kernels  25.9 us (15%)
    all_to_all x4, blocking collectives, swap(): return lax.all_to_all(blocks, axes, 0, 0)  56.9 us
    all_to_all x5, starting transfers between devices, swap(): return lax.all_to_all(blocks, axes, 0, 0)  43.1 us
    pallas_call x16, Pallas kernels, call(): pl.pallas_call(body, out_shape=shapes if many else shapes[0], in_specs=sp...  25.9 us
    all_to_all x5, waiting for transfers between devices, swap(): return lax.all_to_all(blocks, axes, 0, 0)  23.1 us
    ppermute x4, starting transfers between devices, near_rows(): return (lax.ppermute(edge_high, PIX, up), lax.ppermute(edge_low, PIX, down))  8.63 us
    ppermute x4, waiting for transfers between devices, near_rows(): return (lax.ppermute(edge_high, PIX, up), lax.ppermute(edge_low, PIX, down))  6.31 us
  transfers between devices with their start and end apart: 9, of which 5 were waited for; matrix products, arithmetic and copies ran while one was open for 0% of the time, Pallas kernels for 6%

profile of v8, /device:TPU:1, one launch (start us, length us, event | category | flops | bytes accessed | tf_op | source)
XLA Modules:
  0.0 165.6 jit_solution(2010490683431092030)
XLA Ops:
  0.6 2.9 %shard_map.68 = f32[8,56,256]{2,1,0:T(8,128)} custom-call(s32[1]{0:T(128)} %bitcast.day, f32[128,8,256]{2,1,0:T(8,128)} %observed.1, s32[128,8,256]{2,1,0:T(8,128)} %missing.1, s32[8,256]{1,0:T(8,128)} %land.15, f32[32,128]{1,0:T(8,128)} %bitcast.18), custom_call_target="tpu_custom_call" | custom-call | flops 1000000 | bytes 1000000 | tf_op jit(solution)/shard_map/pallas_call | solution.py:141
  3.5 13.3 %all-to-all-start = ((f32[8,56,256]{2,1,0:T(8,128)}), f32[8,56,256]{2,1,0:T(8,128)S(1)}, u32[]{:S(2)}, u32[]{:S(2)}) async-start(f32[8,56,256]{2,1,0:T(8,128)} %shard_map.68), calls=%async_computation | async-start | bytes 917504 | tf_op jit(solution)/shard_map/all_to_all | solution.py:570
  16.9 0.0 copy-start.4
  16.9 4.1 %shard_map.69 = (f32[8,128,256]{2,1,0:T(8,128)}, bf16[8,128,256]{2,1,0:T(8,128)(2,1)}) custom-call(f32[128,8,256]{2,1,0:T(8,128)} %observed.1, s32[128,8,256]{2,1,0:T(8,128)} %missing.1, s32[8,256]{1,0:T(8,128)} %land.15), custom_call_target="tpu_custom_call" | custom-call | flops 1000000 | bytes 1000000 | tf_op jit(solution)/shard_map/pallas_call | solution.py:141
  21.0 0.0 copy-start.2
  21.1 0.0 copy-done.4
  21.1 0.7 select_add_fusion.band
  21.8 7.6 %all-to-all-done.arrived = f32[8,56,256]{2,1,0:T(8,128)S(1)} async-done(((f32[8,56,256]{2,1,0:T(8,128)}), f32[8,56,256]{2,1,0:T(8,128)S(1)}, u32[]{:S(2)}, u32[]{:S(2)}) %all-to-all-start) | async-done | bytes 458784 | tf_op jit(solution)/shard_map/all_to_all | solution.py:570
  29.5 0.0 copy-start.3
  29.5 12.6 %all_to_all.45.modes = f32[8,32,256]{2,1,0:T(8,128)S(1)} all-to-all(f32[8,32,256]{2,1,0:T(8,128)S(1)} %shard_map.70), channel_id=1, replica_groups=mesh['zlo'=4,'y'=8,'core'=2,'x'=4,'zhi'=2] {'x','zhi'}, dimensions={0} | all-to-all | bytes 524288 | tf_op jit(solution)/shard_map/all_to_all | solution.py:570
  42.1 0.0 copy-done.2
  42.1 0.0 copy-done.3
  42.1 0.9 shard_map.71
  43.0 15.3 %all_to_all.46.arrived = f32[8,48,128]{2,1,0:T(8,128)S(1)} all-to-all(f32[8,48,128]{2,1,0:T(8,128)S(1)} %get-tuple-element.43), channel_id=1, replica_groups=mesh['zlo'=4,'y'=8,'core'=2,'x'=4,'zhi'=2] {'y'}, dimensions={0} | all-to-all | bytes 393216 | tf_op jit(solution)/shard_map/all_to_all | solution.py:570
  58.2 0.7 shard_map.72
  58.9 13.9 %all-to-all-start.3 = ((f32[8,48,128]{2,1,0:T(8,128)}), f32[8,48,128]{2,1,0:T(8,128)S(1)}, u32[]{:S(2)}, u32[]{:S(2)}) async-start(f32[8,48,128]{2,1,0:T(8,128)} %shard_map.72), calls=%async_computation.3 | async-start | bytes 393216 | tf_op jit(solution)/shard_map/all_to_all | solution.py:570
  72.8 2.1 %collective-permute-start = (f32[40,256]{1,0:T(8,128)S(1)}, f32[40,256]{1,0:T(8,128)S(1)}, u32[]{:S(2)}, u32[]{:S(2)}) collective-permute-start(f32[40,256]{1,0:T(8,128)S(1)} %get-tuple-element.47), channel_id=1, source_target_pairs={{0,8},{8,16},{16,24},{24,32},{32,40},{40,48},{48,56},{56,64},{64,7... | collective-permute-start | bytes 122888 | tf_op jit(solution)/shard_map/ppermute | solution.py:577
  74.9 2.2 %collective-permute-start.1 = (f32[40,256]{1,0:T(8,128)S(1)}, f32[40,256]{1,0:T(8,128)S(1)}, u32[]{:S(2)}, u32[]{:S(2)}) collective-permute-start(f32[40,256]{1,0:T(8,128)S(1)} %get-tuple-element.48), channel_id=1, source_target_pairs={{8,0},{16,8},{24,16},{32,24},{40,32},{48,40},{56,48},{64,56},{72,6... | collective-permute-start | bytes 122888 | tf_op jit(solution)/shard_map/ppermute | solution.py:577
  77.1 0.0 collective-permute-done.above
  77.1 3.4 %collective-permute-done.1.below = f32[40,256]{1,0:T(8,128)S(1)} collective-permute-done((f32[40,256]{1,0:T(8,128)S(1)}, f32[40,256]{1,0:T(8,128)S(1)}, u32[]{:S(2)}, u32[]{:S(2)}) %collective-permute-start.1) | collective-permute-done | bytes 40992 | tf_op jit(solution)/shard_map/ppermute | solution.py:577
  80.5 0.2 shard_map.73.smooth_hbm
  80.7 0.0 all-to-all-done.3.arrived
  80.7 4.4 %shard_map.74 = (f32[8,128,256]{2,1,0:T(8,128)}, f32[8,40,256]{2,1,0:T(8,128)}) custom-call(s32[1]{0:T(128)} %bitcast.day, f32[8,48,128]{2,1,0:T(8,128)S(1)} %all-to-all-done.3.arrived, f32[512,128]{1,0:T(8,128)S(1)} %select_add_fusion.band, f32[8,32,256]{2,1,0:T(8,128)S(1)} %shard_map.73.smooth_hbm, f32[8,128,256]{2,1,0:T(8,128)} %get-tuple-element.42.filled.first_hbm, ...), custom_call_target="tpu_custom_call" | custom-call | flops 1000000 | bytes 1000000 | tf_op jit(solution)/shard_map/pallas_call | solution.py:141
  85.2 14.8 %all_to_all.47.arrived = f32[8,40,256]{2,1,0:T(8,128)S(1)} all-to-all(f32[8,40,256]{2,1,0:T(8,128)} %get-tuple-element.53), channel_id=1, replica_groups=mesh['zlo'=4,'y'=8,'core'=2,'x'=4,'zhi'=2] {'x','zhi'}, dimensions={0} | all-to-all | bytes 655360 | tf_op jit(solution)/shard_map/all_to_all | solution.py:570
  100.0 0.7 shard_map.75
  100.8 3.4 %all-to-all-start.5 = ((f32[8,32,256]{2,1,0:T(8,128)}), f32[8,32,256]{2,1,0:T(8,128)S(1)}, u32[]{:S(2)}, u32[]{:S(2)}) async-start(f32[8,32,256]{2,1,0:T(8,128)} %shard_map.75), calls=%async_computation.5 | async-start | bytes 524288 | tf_op jit(solution)/shard_map/all_to_all | solution.py:570
  104.2 0.8 shard_map.76.factor.scale
  105.0 9.1 %all-to-all-done.5.modes = f32[8,32,256]{2,1,0:T(8,128)S(1)} async-done(((f32[8,32,256]{2,1,0:T(8,128)}), f32[8,32,256]{2,1,0:T(8,128)S(1)}, u32[]{:S(2)}, u32[]{:S(2)}) %all-to-all-start.5) | async-done | bytes 262176 | tf_op jit(solution)/shard_map/all_to_all | solution.py:570
  114.2 0.0 copy-start.1
  114.2 2.4 %shard_map.77 = (f32[8,40,128]{2,1,0:T(8,128)S(1)}, f32[40,256]{1,0:T(8,128)S(1)}, f32[40,256]{1,0:T(8,128)S(1)}) custom-call(f32[8,32,256]{2,1,0:T(8,128)S(1)} %all-to-all-done.5.modes, f32[8,128,256]{2,1,0:T(8,128)} %get-tuple-element.54.filled_hbm, s32[8,256]{1,0:T(8,128)S(1)} %copy-done.3, f32[32,128]{1,0:T(8,128)S(1)} %shard_map.76.factor.scale), custom_call_target="tpu_custom_call" | custom-call | flops 1000000 | bytes 1000000 | tf_op jit(solution)/shard_map/pallas_call | solution.py:141
  116.6 14.2 %all_to_all.48.arrived = f32[8,40,128]{2,1,0:T(8,128)S(1)} all-to-all(f32[8,40,128]{2,1,0:T(8,128)S(1)} %get-tuple-element.55), channel_id=1, replica_groups=mesh['zlo'=4,'y'=8,'core'=2,'x'=4,'zhi'=2] {'y'}, dimensions={0} | all-to-all | bytes 327680 | tf_op jit(solution)/shard_map/all_to_all | solution.py:570
  130.7 0.0 copy-start
  130.7 0.7 shard_map.78
  131.4 9.1 %all-to-all-start.7 = ((f32[8,40,128]{2,1,0:T(8,128)}), f32[8,40,128]{2,1,0:T(8,128)S(1)}, u32[]{:S(2)}, u32[]{:S(2)}) async-start(f32[8,40,128]{2,1,0:T(8,128)} %shard_map.78), calls=%async_computation.7 | async-start | bytes 327680 | tf_op jit(solution)/shard_map/all_to_all | solution.py:570
  140.6 2.0 %collective-permute-start.2 = (f32[40,256]{1,0:T(8,128)S(1)}, f32[40,256]{1,0:T(8,128)S(1)}, u32[]{:S(2)}, u32[]{:S(2)}) collective-permute-start(f32[40,256]{1,0:T(8,128)S(1)} %get-tuple-element.59), channel_id=1, source_target_pairs={{0,8},{8,16},{16,24},{24,32},{32,40},{40,48},{48,56},{56,64},{64,7... | collective-permute-start | bytes 122888 | tf_op jit(solution)/shard_map/ppermute | solution.py:577
  142.6 2.3 %collective-permute-start.3 = (f32[40,256]{1,0:T(8,128)S(1)}, f32[40,256]{1,0:T(8,128)S(1)}, u32[]{:S(2)}, u32[]{:S(2)}) collective-permute-start(f32[40,256]{1,0:T(8,128)S(1)} %get-tuple-element.60), channel_id=1, source_target_pairs={{8,0},{16,8},{24,16},{32,24},{40,32},{48,40},{56,48},{64,56},{72,6... | collective-permute-start | bytes 122888 | tf_op jit(solution)/shard_map/ppermute | solution.py:577
  144.9 0.0 copy-done.1
  144.9 0.0 collective-permute-done.2.above
  144.9 2.9 %collective-permute-done.3.below = f32[40,256]{1,0:T(8,128)S(1)} collective-permute-done((f32[40,256]{1,0:T(8,128)S(1)}, f32[40,256]{1,0:T(8,128)S(1)}, u32[]{:S(2)}, u32[]{:S(2)}) %collective-permute-start.3) | collective-permute-done | bytes 40992 | tf_op jit(solution)/shard_map/ppermute | solution.py:577
  147.9 0.2 shard_map.79.smooth
  148.1 0.0 all-to-all-done.7.arrived
  148.1 0.7 shard_map.80
  148.8 3.4 %all-to-all-start.8 = ((f32[8,32,128]{2,1,0:T(8,128)}), f32[8,32,128]{2,1,0:T(8,128)S(1)}, u32[]{:S(2)}, u32[]{:S(2)}) async-start(f32[8,32,128]{2,1,0:T(8,128)} %get-tuple-element.62.raw), calls=%async_computation.8 | async-start | bytes 262144 | tf_op jit(solution)/shard_map/all_to_all | solution.py:570
  152.2 0.0 copy-done
  152.2 2.3 %shard_map.81 = (f32[128,32]{1,0:T(8,128)S(1)}, f32[32,32]{1,0:T(8,128)S(1)}, f32[32,32]{1,0:T(8,128)S(1)}) custom-call(f32[8,32,128]{2,1,0:T(8,128)} %get-tuple-element.62.raw, f32[8,128]{1,0:T(8,128)S(1)} %get-tuple-element.63.extra, f32[512,128]{1,0:T(8,128)S(1)} %select_add_fusion.band, f32[32,128]{1,0:T(8,128)S(1)} %shard_map.76.factor.scale), custom_call_target="tpu_custom_call" | custom-call | flops 1000000 | bytes 1000000 | tf_op jit(solution)/shard_map/pallas_call | solution.py:141
  154.5 1.5 shard_map.82.filled_in
  156.1 6.3 %all-to-all-done.8.arrived = f32[8,32,128]{2,1,0:T(8,128)S(1)} async-done(((f32[8,32,128]{2,1,0:T(8,128)}), f32[8,32,128]{2,1,0:T(8,128)S(1)}, u32[]{:S(2)}, u32[]{:S(2)}) %all-to-all-start.8) | async-done | bytes 131104 | tf_op jit(solution)/shard_map/all_to_all | solution.py:570
  162.4 3.2 %shard_map.83 = (f32[32,128]{1,0:T(8,128)}, f32[128,8,256]{2,1,0:T(8,128)}) custom-call(s32[1]{0:T(128)} %bitcast.day, f32[8,32,128]{2,1,0:T(8,128)S(1)} %all-to-all-done.8.arrived, f32[512,128]{1,0:T(8,128)S(1)} %select_add_fusion.band, f32[32,32]{1,0:T(8,128)S(1)} %get-tuple-element.64.factor, ...), custom_call_target="tpu_custom_call", output_to_operand_aliasing={{1}: (12, {})} | custom-call | flops 1000000 | bytes 1000000 | tf_op jit(solution)/shard_map/pallas_call | solution.py:141
  (9 shorter events, 0.1 us)
Async XLA Ops:
  3.5 25.9 %all-to-all-start = ((f32[8,56,256]{2,1,0:T(8,128)}), f32[8,56,256]{2,1,0:T(8,128)S(1)}, u32[]{:S(2)}, u32[]{:S(2)}) async-start(f32[8,56,256]{2,1,0:T(8,128)} %shard_map.68), calls=%async_computation | async-start | bytes 917504 | tf_op jit(solution)/shard_map/all_to_all | solution.py:570
  16.9 4.2 %copy-start.4 = (f32[128,7]{0,1:T(8,128)S(1)}, f32[128,7]{0,1:T(8,128)}, u32[]{:S(2)}) copy-start(f32[128,7]{0,1:T(8,128)} %param.9) | copy-start | bytes 10756
  21.0 21.0 %copy-start.2 = (f32[8,128,256]{2,1,0:T(8,128)S(1)}, f32[8,128,256]{2,1,0:T(8,128)}, u32[]{:S(2)}) copy-start(f32[8,128,256]{2,1,0:T(8,128)} %get-tuple-element.42.filled.first_hbm) | copy-start | bytes 3145732
  29.5 12.6 %copy-start.3 = (s32[8,256]{1,0:T(8,128)S(1)}, s32[8,256]{1,0:T(8,128)}, u32[]{:S(2)}) copy-start(s32[8,256]{1,0:T(8,128)} %land.15) | copy-start | bytes 24580
  58.9 21.8 %all-to-all-start.3 = ((f32[8,48,128]{2,1,0:T(8,128)}), f32[8,48,128]{2,1,0:T(8,128)S(1)}, u32[]{:S(2)}, u32[]{:S(2)}) async-start(f32[8,48,128]{2,1,0:T(8,128)} %shard_map.72), calls=%async_computation.3 | async-start | bytes 393216 | tf_op jit(solution)/shard_map/all_to_all | solution.py:570
  72.8 4.3 %collective-permute-start = (f32[40,256]{1,0:T(8,128)S(1)}, f32[40,256]{1,0:T(8,128)S(1)}, u32[]{:S(2)}, u32[]{:S(2)}) collective-permute-start(f32[40,256]{1,0:T(8,128)S(1)} %get-tuple-element.47), channel_id=1, source_target_pairs={{0,8},{8,16},{16,24},{24,32},{32,40},{40,48},{48,56},{56,64},{64,7... | collective-permute-start | bytes 122888 | tf_op jit(solution)/shard_map/ppermute | solution.py:577
  74.9 5.6 %collective-permute-start.1 = (f32[40,256]{1,0:T(8,128)S(1)}, f32[40,256]{1,0:T(8,128)S(1)}, u32[]{:S(2)}, u32[]{:S(2)}) collective-permute-start(f32[40,256]{1,0:T(8,128)S(1)} %get-tuple-element.48), channel_id=1, source_target_pairs={{8,0},{16,8},{24,16},{32,24},{40,32},{48,40},{56,48},{64,56},{72,6... | collective-permute-start | bytes 122888 | tf_op jit(solution)/shard_map/ppermute | solution.py:577
  100.8 13.4 %all-to-all-start.5 = ((f32[8,32,256]{2,1,0:T(8,128)}), f32[8,32,256]{2,1,0:T(8,128)S(1)}, u32[]{:S(2)}, u32[]{:S(2)}) async-start(f32[8,32,256]{2,1,0:T(8,128)} %shard_map.75), calls=%async_computation.5 | async-start | bytes 524288 | tf_op jit(solution)/shard_map/all_to_all | solution.py:570
  114.2 30.7 %copy-start.1 = (s32[128,8,256]{2,1,0:T(8,128)S(1)}, s32[128,8,256]{2,1,0:T(8,128)}, u32[]{:S(2)}) copy-start(s32[128,8,256]{2,1,0:T(8,128)} %missing.1) | copy-start | bytes 3145732
  130.7 21.4 %copy-start = (f32[128,8,256]{2,1,0:T(8,128)S(1)}, f32[128,8,256]{2,1,0:T(8,128)}, u32[]{:S(2)}) copy-start(f32[128,8,256]{2,1,0:T(8,128)} %observed.1) | copy-start | bytes 3145732
  131.4 16.7 %all-to-all-start.7 = ((f32[8,40,128]{2,1,0:T(8,128)}), f32[8,40,128]{2,1,0:T(8,128)S(1)}, u32[]{:S(2)}, u32[]{:S(2)}) async-start(f32[8,40,128]{2,1,0:T(8,128)} %shard_map.78), calls=%async_computation.7 | async-start | bytes 327680 | tf_op jit(solution)/shard_map/all_to_all | solution.py:570
  140.6 4.4 %collective-permute-start.2 = (f32[40,256]{1,0:T(8,128)S(1)}, f32[40,256]{1,0:T(8,128)S(1)}, u32[]{:S(2)}, u32[]{:S(2)}) collective-permute-start(f32[40,256]{1,0:T(8,128)S(1)} %get-tuple-element.59), channel_id=1, source_target_pairs={{0,8},{8,16},{16,24},{24,32},{32,40},{40,48},{48,56},{56,64},{64,7... | collective-permute-start | bytes 122888 | tf_op jit(solution)/shard_map/ppermute | solution.py:577
  142.6 5.3 %collective-permute-start.3 = (f32[40,256]{1,0:T(8,128)S(1)}, f32[40,256]{1,0:T(8,128)S(1)}, u32[]{:S(2)}, u32[]{:S(2)}) collective-permute-start(f32[40,256]{1,0:T(8,128)S(1)} %get-tuple-element.60), channel_id=1, source_target_pairs={{8,0},{16,8},{24,16},{32,24},{40,32},{48,40},{56,48},{64,56},{72,6... | collective-permute-start | bytes 122888 | tf_op jit(solution)/shard_map/ppermute | solution.py:577
  148.8 13.6 %all-to-all-start.8 = ((f32[8,32,128]{2,1,0:T(8,128)}), f32[8,32,128]{2,1,0:T(8,128)S(1)}, u32[]{:S(2)}, u32[]{:S(2)}) async-start(f32[8,32,128]{2,1,0:T(8,128)} %get-tuple-element.62.raw), calls=%async_computation.8 | async-start | bytes 262144 | tf_op jit(solution)/shard_map/all_to_all | solution.py:570

commit v9 on v7

--- a/solution.py
+++ b/solution.py
@@ -124,18 +124,19 @@
     return total
 
 
-def call(body, outs, args, scratch=(), limit=8, anywhere=(), alias=None, out_any=()):
+def call(body, outs, args, scratch=(), limit=8, anywhere=(), still=(), alias=None, out_any={}):
     specs = []
     for i, a in enumerate(args):
         space = pltpu.SMEM if a.ndim == 1 else pltpu.VMEM
-        specs.append(pl.BlockSpec(memory_space=pl.ANY if i in anywhere else space))
+        space = pl.ANY if i in anywhere else pltpu.HBM if i in still else space
+        specs.append(pl.BlockSpec(memory_space=space))
     many = isinstance(outs, list)
     shapes = [
-        s if isinstance(s, jax.ShapeDtypeStruct) else jax.ShapeDtypeStruct(s, f32)
+        jax.ShapeDtypeStruct(s, f32) if isinstance(s, tuple) else s
         for s in (outs if many else [outs])
     ]
     out_specs = [
-        pl.BlockSpec(memory_space=pl.ANY if i in out_any else pltpu.VMEM)
+        pl.BlockSpec(memory_space=out_any.get(i, pltpu.VMEM))
         for i in range(len(shapes))
     ]
     return pl.pallas_call(
@@ -282,6 +283,11 @@
         out[j] = total
 
 
+def add_rows_again_body(arrived, filled, out):
+    del filled
+    add_rows_body(arrived, out)
+
+
 def add_all_body(arrived, out):
     total = total_of(arrived)
     for j in range(out.shape[0]):
@@ -411,16 +417,13 @@
     arrived,
     band,
     smooth_hbm,
-    first_hbm,
-    gap_hbm,
+    first,
+    gap,
     land,
     filled_hbm,
-    out_hbm,
+    out,
     smooth,
-    first,
-    gap,
     filled,
-    out,
     arrivals,
     sent,
 ):
@@ -429,14 +432,7 @@
         copy.start()
         return copy
 
-    waits = [start(smooth_hbm, smooth, arrivals.at[16])]
-    fetches = [
-        (
-            start(first_hbm.at[r], first.at[r], arrivals.at[2 * r]),
-            start(gap_hbm.at[r], gap.at[r], arrivals.at[2 * r + 1]),
-        )
-        for r in range(8)
-    ]
+    waits = [start(smooth_hbm, smooth, arrivals.at[0])]
     total = total_of(arrived)
     extra = jnp.concatenate([total[K:], pltpu.roll(total[K:], 64, 1)], axis=0)
     raw = jnp.concatenate([total[:K], extra], axis=1)
@@ -455,8 +451,6 @@
         copy.wait()
     sends = []
     for r in range(0, 8, 2):
-        for copy in fetches[r] + fetches[r + 1]:
-            copy.wait()
         for q in (r, r + 1):
             surface = mul_deep(mixed, smooth[q])
             absent = gap[q].astype(f32) == 1
@@ -464,8 +458,7 @@
             filled[q] = now
             out[q, :K, :] = mul_few(weights, now)
         for q in (r, r + 1):
-            sends.append(start(filled.at[q], filled_hbm.at[q], sent.at[2 * q]))
-            sends.append(start(out.at[q], out_hbm.at[q], sent.at[2 * q + 1]))
+            sends.append(start(filled.at[q], filled_hbm.at[q], sent.at[q]))
     for copy in sends:
         copy.wait()
 
@@ -624,7 +617,7 @@
         ],
         limit=56,
         anywhere=(1, 2, 3, 4),
-        out_any=(0,),
+        out_any={0: pl.ANY},
     )
     later, taps, part = lax.optimization_barrier((missing, day_weights, part))
     band = band_of(taps)
@@ -636,7 +629,7 @@
         + [pltpu.SemaphoreType.DMA((2,))] * 2,
         limit=56,
         anywhere=(0, 1),
-        out_any=(0, 1),
+        out_any={0: pl.ANY, 1: pl.ANY},
     )
     arrived, first, gap, band = lax.optimization_barrier(
         (swap(part, DAY), first, gap, band)
@@ -652,23 +645,21 @@
     joint, smooth = smooth_beside(joint, low, high, modes)
     filled, part = call(
         refill_body,
-        [(rows, days, cols), (rows, K + 8, cols)],
+        [pltpu.HBM((rows, days, cols), f32), (rows, K + 8, cols)],
         (day, joint, band, smooth, first, gap, land),
         [
             pltpu.VMEM(block, f32),
             turned,
-            pltpu.VMEM((rows, days, cols), bf16),
-            turned,
-            pltpu.VMEM((rows, K + 8, cols), f32),
-            pltpu.SemaphoreType.DMA((17,)),
-            pltpu.SemaphoreType.DMA((16,)),
+            pltpu.SemaphoreType.DMA((1,)),
+            pltpu.SemaphoreType.DMA((8,)),
         ],
-        limit=53,
-        anywhere=(3, 4, 5),
-        out_any=(0, 1),
+        limit=12,
+        anywhere=(3,),
+        out_any={0: pltpu.HBM},
     )
     arrived = swap(part, DAY)
-    modes = swap(call(add_rows_body, block, (arrived,)), DAY)
+    modes = call(add_rows_again_body, block, (arrived, filled), still=(1,), limit=53)
+    modes = swap(modes, DAY)
     factor = call(factor_body, (K, LANES), (arrived,))
     joint, *edges = call(
         project_again_body,
@@ -704,7 +695,7 @@
             pltpu.SemaphoreType.DMA((2,)),
         ],
         anywhere=(12,),
-        out_any=(1,),
+        out_any={1: pl.ANY},
         alias={12: 1},
     )
     return filled, basis_t.T

time: 165 us -> 162 us (0.982)
  no operation moved by 1% of the time
where the time goes in v9:
time: 162 us; the launch traced here: 160 us
  blocking collectives  56.1 us (35%)
  starting transfers between devices  47.1 us (29%)
  waiting for transfers between devices  31.9 us (20%)
  Pallas kernels  23.2 us (14%)
    all_to_all x4, blocking collectives, swap(): return lax.all_to_all(blocks, axes, 0, 0)  56.1 us
    all_to_all x5, starting transfers between devices, swap(): return lax.all_to_all(blocks, axes, 0, 0)  32.5 us
    all_to_all x5, waiting for transfers between devices, swap(): return lax.all_to_all(blocks, axes, 0, 0)  24.6 us
    pallas_call x16, Pallas kernels, call(): pl.pallas_call(body, out_shape=shapes if many else shapes[0], in_specs=sp...  23.2 us
    ppermute x4, starting transfers between devices, near_rows(): return (lax.ppermute(edge_high, PIX, up), lax.ppermute(edge_low, PIX, down))  14.6 us
    ppermute x4, waiting for transfers between devices, near_rows(): return (lax.ppermute(edge_high, PIX, up), lax.ppermute(edge_low, PIX, down))  7.24 us
  transfers between devices with their start and end apart: 9, of which 5 were waited for; matrix products, arithmetic and copies ran while one was open for 0% of the time, Pallas kernels for 6%

profile of v9, /device:TPU:1, one launch (start us, length us, event | category | flops | bytes accessed | tf_op | source)
XLA Modules:
  0.0 160.0 jit_solution(2374010604056873333)
XLA Ops:
  0.6 2.9 %shard_map.68 = f32[8,56,256]{2,1,0:T(8,128)} custom-call(s32[1]{0:T(128)} %bitcast.day, f32[128,8,256]{2,1,0:T(8,128)} %observed.1, s32[128,8,256]{2,1,0:T(8,128)} %missing.1, s32[8,256]{1,0:T(8,128)} %land.15, f32[32,128]{1,0:T(8,128)} %bitcast.18), custom_call_target="tpu_custom_call" | custom-call | flops 1000000 | bytes 1000000 | tf_op jit(solution)/shard_map/pallas_call | solution.py:142
  3.6 13.3 %all-to-all-start = ((f32[8,56,256]{2,1,0:T(8,128)}), f32[8,56,256]{2,1,0:T(8,128)S(1)}, u32[]{:S(2)}, u32[]{:S(2)}) async-start(f32[8,56,256]{2,1,0:T(8,128)} %shard_map.68), calls=%async_computation | async-start | bytes 917504 | tf_op jit(solution)/shard_map/all_to_all | solution.py:552
  16.9 0.0 copy-start.6
  16.9 4.1 %shard_map.69 = (f32[8,128,256]{2,1,0:T(8,128)}, bf16[8,128,256]{2,1,0:T(8,128)(2,1)}) custom-call(f32[128,8,256]{2,1,0:T(8,128)} %observed.1, s32[128,8,256]{2,1,0:T(8,128)} %missing.1, s32[8,256]{1,0:T(8,128)} %land.15), custom_call_target="tpu_custom_call" | custom-call | flops 1000000 | bytes 1000000 | tf_op jit(solution)/shard_map/pallas_call | solution.py:142
  21.0 0.0 copy-start.2
  21.1 0.0 copy-done.6
  21.1 0.7 select_add_fusion.band
  21.8 7.6 %all-to-all-done.arrived = f32[8,56,256]{2,1,0:T(8,128)S(1)} async-done(((f32[8,56,256]{2,1,0:T(8,128)}), f32[8,56,256]{2,1,0:T(8,128)S(1)}, u32[]{:S(2)}, u32[]{:S(2)}) %all-to-all-start) | async-done | bytes 458784 | tf_op jit(solution)/shard_map/all_to_all | solution.py:552
  29.5 0.0 copy-start.4
  29.5 12.6 %all_to_all.45.modes = f32[8,32,256]{2,1,0:T(8,128)S(1)} all-to-all(f32[8,32,256]{2,1,0:T(8,128)S(1)} %shard_map.70), channel_id=1, replica_groups=mesh['zlo'=4,'y'=8,'core'=2,'x'=4,'zhi'=2] {'x','zhi'}, dimensions={0} | all-to-all | bytes 524288 | tf_op jit(solution)/shard_map/all_to_all | solution.py:552
  42.1 0.0 copy-done.2
  42.1 0.0 copy-done.4
  42.1 0.9 shard_map.71
  43.0 18.3 %all_to_all.46.arrived = f32[8,48,128]{2,1,0:T(8,128)S(1)} all-to-all(f32[8,48,128]{2,1,0:T(8,128)S(1)} %get-tuple-element.43), channel_id=1, replica_groups=mesh['zlo'=4,'y'=8,'core'=2,'x'=4,'zhi'=2] {'zlo','core'}, dimensions={0} | all-to-all | bytes 393216 | tf_op jit(solution)/shard_map/all_to_all | solution.py:552
  61.3 0.7 shard_map.72
  62.0 7.0 %all-to-all-start.3 = ((f32[8,48,128]{2,1,0:T(8,128)}), f32[8,48,128]{2,1,0:T(8,128)S(1)}, u32[]{:S(2)}, u32[]{:S(2)}) async-start(f32[8,48,128]{2,1,0:T(8,128)} %shard_map.72), calls=%async_computation.3 | async-start | bytes 393216 | tf_op jit(solution)/shard_map/all_to_all | solution.py:552
  68.9 5.7 %collective-permute-start = (f32[40,256]{1,0:T(8,128)S(1)}, f32[40,256]{1,0:T(8,128)S(1)}, u32[]{:S(2)}, u32[]{:S(2)}) collective-permute-start(f32[40,256]{1,0:T(8,128)S(1)} %get-tuple-element.47), channel_id=1, source_target_pairs={{0,8},{8,16},{16,24},{24,32},{32,40},{40,48},{48,56},{56,64},{64,7... | collective-permute-start | bytes 122888 | tf_op jit(solution)/shard_map/ppermute | solution.py:559
  74.6 1.9 %collective-permute-start.1 = (f32[40,256]{1,0:T(8,128)S(1)}, f32[40,256]{1,0:T(8,128)S(1)}, u32[]{:S(2)}, u32[]{:S(2)}) collective-permute-start(f32[40,256]{1,0:T(8,128)S(1)} %get-tuple-element.48), channel_id=1, source_target_pairs={{8,0},{16,8},{24,16},{32,24},{40,32},{48,40},{56,48},{64,56},{72,6... | collective-permute-start | bytes 122888 | tf_op jit(solution)/shard_map/ppermute | solution.py:559
  76.5 0.0 collective-permute-done.above
  76.6 3.7 %collective-permute-done.1.below = f32[40,256]{1,0:T(8,128)S(1)} collective-permute-done((f32[40,256]{1,0:T(8,128)S(1)}, f32[40,256]{1,0:T(8,128)S(1)}, u32[]{:S(2)}, u32[]{:S(2)}) %collective-permute-start.1) | collective-permute-done | bytes 40992 | tf_op jit(solution)/shard_map/ppermute | solution.py:559
  80.2 0.2 shard_map.73.smooth_hbm
  80.5 0.0 all-to-all-done.3.arrived
  80.5 0.0 copy-done.5
  80.5 3.1 %shard_map.74 = (f32[8,128,256]{2,1,0:T(8,128)}, f32[8,40,256]{2,1,0:T(8,128)S(1)}) custom-call(s32[1]{0:T(128)} %bitcast.day, f32[8,48,128]{2,1,0:T(8,128)S(1)} %all-to-all-done.3.arrived, f32[512,128]{1,0:T(8,128)S(1)} %select_add_fusion.band, f32[8,32,256]{2,1,0:T(8,128)S(1)} %shard_map.73.smooth_hbm, f32[8,128,256]{2,1,0:T(8,128)S(1)} %copy-done.2, ...), custom_call_target="tpu_custom_call" | custom-call | flops 1000000 | bytes 1000000 | tf_op jit(solution)/shard_map/pallas_call | solution.py:142
  83.6 14.7 %all_to_all.47.arrived = f32[8,40,256]{2,1,0:T(8,128)S(1)} all-to-all(f32[8,40,256]{2,1,0:T(8,128)S(1)} %get-tuple-element.53), channel_id=1, replica_groups=mesh['zlo'=4,'y'=8,'core'=2,'x'=4,'zhi'=2] {'x','zhi'}, dimensions={0} | all-to-all | bytes 655360 | tf_op jit(solution)/shard_map/all_to_all | solution.py:552
  98.3 0.7 shard_map.75
  99.0 4.2 %all-to-all-start.5 = ((f32[8,32,256]{2,1,0:T(8,128)}), f32[8,32,256]{2,1,0:T(8,128)S(1)}, u32[]{:S(2)}, u32[]{:S(2)}) async-start(f32[8,32,256]{2,1,0:T(8,128)} %shard_map.75), calls=%async_computation.5 | async-start | bytes 524288 | tf_op jit(solution)/shard_map/all_to_all | solution.py:552
  103.2 0.8 shard_map.76.factor.scale
  104.1 11.5 %all-to-all-done.5.modes = f32[8,32,256]{2,1,0:T(8,128)S(1)} async-done(((f32[8,32,256]{2,1,0:T(8,128)}), f32[8,32,256]{2,1,0:T(8,128)S(1)}, u32[]{:S(2)}, u32[]{:S(2)}) %all-to-all-start.5) | async-done | bytes 262176 | tf_op jit(solution)/shard_map/all_to_all | solution.py:552
  115.5 0.0 copy-done.3
  115.5 1.0 shard_map.77
  116.6 10.5 %all_to_all.48.arrived = f32[8,40,128]{2,1,0:T(8,128)S(1)} all-to-all(f32[8,40,128]{2,1,0:T(8,128)S(1)} %get-tuple-element.55), channel_id=1, replica_groups=mesh['zlo'=4,'y'=8,'core'=2,'x'=4,'zhi'=2] {'zlo','core'}, dimensions={0} | all-to-all | bytes 327680 | tf_op jit(solution)/shard_map/all_to_all | solution.py:552
  127.1 0.7 shard_map.78
  127.8 4.7 %all-to-all-start.7 = ((f32[8,40,128]{2,1,0:T(8,128)}), f32[8,40,128]{2,1,0:T(8,128)S(1)}, u32[]{:S(2)}, u32[]{:S(2)}) async-start(f32[8,40,128]{2,1,0:T(8,128)} %shard_map.78), calls=%async_computation.7 | async-start | bytes 327680 | tf_op jit(solution)/shard_map/all_to_all | solution.py:552
  132.5 5.0 %collective-permute-start.2 = (f32[40,256]{1,0:T(8,128)S(1)}, f32[40,256]{1,0:T(8,128)S(1)}, u32[]{:S(2)}, u32[]{:S(2)}) collective-permute-start(f32[40,256]{1,0:T(8,128)S(1)} %get-tuple-element.59), channel_id=1, source_target_pairs={{0,8},{8,16},{16,24},{24,32},{32,40},{40,48},{48,56},{56,64},{64,7... | collective-permute-start | bytes 122888 | tf_op jit(solution)/shard_map/ppermute | solution.py:559
  137.5 1.9 %collective-permute-start.3 = (f32[40,256]{1,0:T(8,128)S(1)}, f32[40,256]{1,0:T(8,128)S(1)}, u32[]{:S(2)}, u32[]{:S(2)}) collective-permute-start(f32[40,256]{1,0:T(8,128)S(1)} %get-tuple-element.60), channel_id=1, source_target_pairs={{8,0},{16,8},{24,16},{32,24},{40,32},{48,40},{56,48},{64,56},{72,6... | collective-permute-start | bytes 122888 | tf_op jit(solution)/shard_map/ppermute | solution.py:559
  139.5 0.0 copy-done.1
  139.5 0.0 collective-permute-done.2.above
  139.5 3.6 %collective-permute-done.3.below = f32[40,256]{1,0:T(8,128)S(1)} collective-permute-done((f32[40,256]{1,0:T(8,128)S(1)}, f32[40,256]{1,0:T(8,128)S(1)}, u32[]{:S(2)}, u32[]{:S(2)}) %collective-permute-start.3) | collective-permute-done | bytes 40992 | tf_op jit(solution)/shard_map/ppermute | solution.py:559
  143.1 0.2 shard_map.79.smooth
  143.3 0.0 all-to-all-done.7.arrived
  143.3 0.7 shard_map.80
  144.0 3.4 %all-to-all-start.8 = ((f32[8,32,128]{2,1,0:T(8,128)}), f32[8,32,128]{2,1,0:T(8,128)S(1)}, u32[]{:S(2)}, u32[]{:S(2)}) async-start(f32[8,32,128]{2,1,0:T(8,128)} %get-tuple-element.62.raw), calls=%async_computation.8 | async-start | bytes 262144 | tf_op jit(solution)/shard_map/all_to_all | solution.py:552
  147.4 0.0 copy-done
  147.4 2.3 %shard_map.81 = (f32[128,32]{1,0:T(8,128)S(1)}, f32[32,32]{1,0:T(8,128)S(1)}, f32[32,32]{1,0:T(8,128)S(1)}) custom-call(f32[8,32,128]{2,1,0:T(8,128)} %get-tuple-element.62.raw, f32[8,128]{1,0:T(8,128)S(1)} %get-tuple-element.63.extra, f32[512,128]{1,0:T(8,128)S(1)} %select_add_fusion.band, f32[32,128]{1,0:T(8,128)S(1)} %shard_map.76.factor.scale), custom_call_target="tpu_custom_call" | custom-call | flops 1000000 | bytes 1000000 | tf_op jit(solution)/shard_map/pallas_call | solution.py:142
  149.7 1.5 shard_map.82.filled_in
  151.3 5.5 %all-to-all-done.8.arrived = f32[8,32,128]{2,1,0:T(8,128)S(1)} async-done(((f32[8,32,128]{2,1,0:T(8,128)}), f32[8,32,128]{2,1,0:T(8,128)S(1)}, u32[]{:S(2)}, u32[]{:S(2)}) %all-to-all-start.8) | async-done | bytes 131104 | tf_op jit(solution)/shard_map/all_to_all | solution.py:552
  156.8 3.2 %shard_map.83 = (f32[32,128]{1,0:T(8,128)}, f32[128,8,256]{2,1,0:T(8,128)}) custom-call(s32[1]{0:T(128)} %bitcast.day, f32[8,32,128]{2,1,0:T(8,128)S(1)} %all-to-all-done.8.arrived, f32[512,128]{1,0:T(8,128)S(1)} %select_add_fusion.band, f32[32,32]{1,0:T(8,128)S(1)} %get-tuple-element.64.factor, ...), custom_call_target="tpu_custom_call", output_to_operand_aliasing={{1}: (12, {})} | custom-call | flops 1000000 | bytes 1000000 | tf_op jit(solution)/shard_map/pallas_call | solution.py:142
  (13 shorter events, 0.1 us)
Async XLA Ops:
  3.6 25.9 %all-to-all-start = ((f32[8,56,256]{2,1,0:T(8,128)}), f32[8,56,256]{2,1,0:T(8,128)S(1)}, u32[]{:S(2)}, u32[]{:S(2)}) async-start(f32[8,56,256]{2,1,0:T(8,128)} %shard_map.68), calls=%async_computation | async-start | bytes 917504 | tf_op jit(solution)/shard_map/all_to_all | solution.py:552
  16.9 4.2 %copy-start.6 = (f32[128,7]{0,1:T(8,128)S(1)}, f32[128,7]{0,1:T(8,128)}, u32[]{:S(2)}) copy-start(f32[128,7]{0,1:T(8,128)} %param.9) | copy-start | bytes 10756
  21.0 21.0 %copy-start.2 = (f32[8,128,256]{2,1,0:T(8,128)S(1)}, f32[8,128,256]{2,1,0:T(8,128)}, u32[]{:S(2)}) copy-start(f32[8,128,256]{2,1,0:T(8,128)} %get-tuple-element.42.filled.first) | copy-start | bytes 3145732
  29.5 12.6 %copy-start.4 = (s32[8,256]{1,0:T(8,128)S(1)}, s32[8,256]{1,0:T(8,128)}, u32[]{:S(2)}) copy-start(s32[8,256]{1,0:T(8,128)} %land.15) | copy-start | bytes 24580
  62.0 18.5 %copy-start.5 = (bf16[8,128,256]{2,1,0:T(8,128)(2,1)S(1)}, bf16[8,128,256]{2,1,0:T(8,128)(2,1)}, u32[]{:S(2)}) copy-start(bf16[8,128,256]{2,1,0:T(8,128)(2,1)} %get-tuple-element.52.gap) | copy-start | bytes 1572868
  62.0 18.5 %all-to-all-start.3 = ((f32[8,48,128]{2,1,0:T(8,128)}), f32[8,48,128]{2,1,0:T(8,128)S(1)}, u32[]{:S(2)}, u32[]{:S(2)}) async-start(f32[8,48,128]{2,1,0:T(8,128)} %shard_map.72), calls=%async_computation.3 | async-start | bytes 393216 | tf_op jit(solution)/shard_map/all_to_all | solution.py:552
  68.9 7.6 %collective-permute-start = (f32[40,256]{1,0:T(8,128)S(1)}, f32[40,256]{1,0:T(8,128)S(1)}, u32[]{:S(2)}, u32[]{:S(2)}) collective-permute-start(f32[40,256]{1,0:T(8,128)S(1)} %get-tuple-element.47), channel_id=1, source_target_pairs={{0,8},{8,16},{16,24},{24,32},{32,40},{40,48},{48,56},{56,64},{64,7... | collective-permute-start | bytes 122888 | tf_op jit(solution)/shard_map/ppermute | solution.py:559
  74.6 5.6 %collective-permute-start.1 = (f32[40,256]{1,0:T(8,128)S(1)}, f32[40,256]{1,0:T(8,128)S(1)}, u32[]{:S(2)}, u32[]{:S(2)}) collective-permute-start(f32[40,256]{1,0:T(8,128)S(1)} %get-tuple-element.48), channel_id=1, source_target_pairs={{8,0},{16,8},{24,16},{32,24},{40,32},{48,40},{56,48},{64,56},{72,6... | collective-permute-start | bytes 122888 | tf_op jit(solution)/shard_map/ppermute | solution.py:559
  98.3 17.2 %copy-start.3 = (f32[8,128,256]{2,1,0:T(8,128)S(1)}, f32[8,128,256]{2,1,0:T(8,128)}, u32[]{:S(2)}) copy-start(f32[8,128,256]{2,1,0:T(8,128)} %get-tuple-element.54.filled) | copy-start | bytes 3145732
  99.0 16.5 %all-to-all-start.5 = ((f32[8,32,256]{2,1,0:T(8,128)}), f32[8,32,256]{2,1,0:T(8,128)S(1)}, u32[]{:S(2)}, u32[]{:S(2)}) async-start(f32[8,32,256]{2,1,0:T(8,128)} %shard_map.75), calls=%async_computation.5 | async-start | bytes 524288 | tf_op jit(solution)/shard_map/all_to_all | solution.py:552
  104.1 35.4 %copy-start.1 = (s32[128,8,256]{2,1,0:T(8,128)S(1)}, s32[128,8,256]{2,1,0:T(8,128)}, u32[]{:S(2)}) copy-start(s32[128,8,256]{2,1,0:T(8,128)} %missing.1) | copy-start | bytes 3145732
  127.1 20.3 %copy-start = (f32[128,8,256]{2,1,0:T(8,128)S(1)}, f32[128,8,256]{2,1,0:T(8,128)}, u32[]{:S(2)}) copy-start(f32[128,8,256]{2,1,0:T(8,128)} %observed.1) | copy-start | bytes 3145732
  127.8 15.5 %all-to-all-start.7 = ((f32[8,40,128]{2,1,0:T(8,128)}), f32[8,40,128]{2,1,0:T(8,128)S(1)}, u32[]{:S(2)}, u32[]{:S(2)}) async-start(f32[8,40,128]{2,1,0:T(8,128)} %shard_map.78), calls=%async_computation.7 | async-start | bytes 327680 | tf_op jit(solution)/shard_map/all_to_all | solution.py:552
  132.5 7.0 %collective-permute-start.2 = (f32[40,256]{1,0:T(8,128)S(1)}, f32[40,256]{1,0:T(8,128)S(1)}, u32[]{:S(2)}, u32[]{:S(2)}) collective-permute-start(f32[40,256]{1,0:T(8,128)S(1)} %get-tuple-element.59), channel_id=1, source_target_pairs={{0,8},{8,16},{16,24},{24,32},{32,40},{40,48},{48,56},{56,64},{64,7... | collective-permute-start | bytes 122888 | tf_op jit(solution)/shard_map/ppermute | solution.py:559
  137.5 5.5 %collective-permute-start.3 = (f32[40,256]{1,0:T(8,128)S(1)}, f32[40,256]{1,0:T(8,128)S(1)}, u32[]{:S(2)}, u32[]{:S(2)}) collective-permute-start(f32[40,256]{1,0:T(8,128)S(1)} %get-tuple-element.60), channel_id=1, source_target_pairs={{8,0},{16,8},{24,16},{32,24},{40,32},{48,40},{56,48},{64,56},{72,6... | collective-permute-start | bytes 122888 | tf_op jit(solution)/shard_map/ppermute | solution.py:559
  144.0 12.8 %all-to-all-start.8 = ((f32[8,32,128]{2,1,0:T(8,128)}), f32[8,32,128]{2,1,0:T(8,128)S(1)}, u32[]{:S(2)}, u32[]{:S(2)}) async-start(f32[8,32,128]{2,1,0:T(8,128)} %get-tuple-element.62.raw), calls=%async_computation.8 | async-start | bytes 262144 | tf_op jit(solution)/shard_map/all_to_all | solution.py:552

commit v10 on v9

--- a/solution.py
+++ b/solution.py
@@ -641,8 +641,11 @@
         (day, arrived, modes, first, land),
         halo,
     )
-    joint, low, high = add_near(joint, edges)
-    joint, smooth = smooth_beside(joint, low, high, modes)
+    above, below = near_rows(*edges)
+    joint = swap(joint, NEAR)
+    smooth = call(smooth_body, block, (modes, above, below, land))
+    joint, smooth = lax.optimization_barrier((joint, smooth))
+    joint = swap(call(add_all_body, (far,) + joint.shape[1:], (joint,)), "y")
     filled, part = call(
         refill_body,
         [pltpu.HBM((rows, days, cols), f32), (rows, K + 8, cols)],

time: 162 us -> 164 us (1.012)
  blocking collectives: 56.1 us -> 61.1 us
  waiting for transfers between devices: 31.9 us -> 29.3 us
    all_to_all x4, blocking collectives: 56.1 us -> 61.1 us  [swap(): return lax.all_to_all(blocks, axes, 0, 0)]
    all_to_all x5, starting transfers between devices: 32.5 us -> 35.5 us  [swap(): return lax.all_to_all(blocks, axes, 0, 0)]
    ppermute x4, starting transfers between devices: 14.6 us -> 11.6 us  [near_rows(): return (lax.ppermute(edge_high, PIX, up), lax.ppermute(edge_low, PIX, down))]
    all_to_all x5, waiting for transfers between devices: 24.6 us -> 22.3 us  [swap(): return lax.all_to_all(blocks, axes, 0, 0)]
where the time goes in v10:
time: 164 us; the launch traced here: 162 us
  blocking collectives  61.1 us (37%)
  starting transfers between devices  47.1 us (29%)
  waiting for transfers between devices  29.3 us (18%)
  Pallas kernels  23.2 us (14%)
    all_to_all x4, blocking collectives, swap(): return lax.all_to_all(blocks, axes, 0, 0)  61.1 us
    all_to_all x5, starting transfers between devices, swap(): return lax.all_to_all(blocks, axes, 0, 0)  35.5 us
    pallas_call x16, Pallas kernels, call(): pl.pallas_call(body, out_shape=shapes if many else shapes[0], in_specs=sp...  23.2 us
    all_to_all x5, waiting for transfers between devices, swap(): return lax.all_to_all(blocks, axes, 0, 0)  22.3 us
    ppermute x4, starting transfers between devices, near_rows(): return (lax.ppermute(edge_high, PIX, up), lax.ppermute(edge_low, PIX, down))  11.6 us
    ppermute x4, waiting for transfers between devices, near_rows(): return (lax.ppermute(edge_high, PIX, up), lax.ppermute(edge_low, PIX, down))  7.04 us
  transfers between devices with their start and end apart: 9, of which 5 were waited for; matrix products, arithmetic and copies ran while one was open for 0% of the time, Pallas kernels for 6%

profile of v10, /device:TPU:1, one launch (start us, length us, event | category | flops | bytes accessed | tf_op | source)
XLA Modules:
  0.0 162.4 jit_solution(599263578683900173)
XLA Ops:
  0.6 2.9 %shard_map.68 = f32[8,56,256]{2,1,0:T(8,128)} custom-call(s32[1]{0:T(128)} %bitcast.day, f32[128,8,256]{2,1,0:T(8,128)} %observed.1, s32[128,8,256]{2,1,0:T(8,128)} %missing.1, s32[8,256]{1,0:T(8,128)} %land.15, f32[32,128]{1,0:T(8,128)} %bitcast.18), custom_call_target="tpu_custom_call" | custom-call | flops 1000000 | bytes 1000000 | tf_op jit(solution)/shard_map/pallas_call | solution.py:142
  3.6 13.3 %all-to-all-start = ((f32[8,56,256]{2,1,0:T(8,128)}), f32[8,56,256]{2,1,0:T(8,128)S(1)}, u32[]{:S(2)}, u32[]{:S(2)}) async-start(f32[8,56,256]{2,1,0:T(8,128)} %shard_map.68), calls=%async_computation | async-start | bytes 917504 | tf_op jit(solution)/shard_map/all_to_all | solution.py:552
  16.9 0.0 copy-start.6
  16.9 4.1 %shard_map.69 = (f32[8,128,256]{2,1,0:T(8,128)}, bf16[8,128,256]{2,1,0:T(8,128)(2,1)}) custom-call(f32[128,8,256]{2,1,0:T(8,128)} %observed.1, s32[128,8,256]{2,1,0:T(8,128)} %missing.1, s32[8,256]{1,0:T(8,128)} %land.15), custom_call_target="tpu_custom_call" | custom-call | flops 1000000 | bytes 1000000 | tf_op jit(solution)/shard_map/pallas_call | solution.py:142
  21.0 0.0 copy-start.2
  21.1 0.0 copy-done.6
  21.1 0.7 select_add_fusion.band
  21.8 7.6 %all-to-all-done.arrived = f32[8,56,256]{2,1,0:T(8,128)S(1)} async-done(((f32[8,56,256]{2,1,0:T(8,128)}), f32[8,56,256]{2,1,0:T(8,128)S(1)}, u32[]{:S(2)}, u32[]{:S(2)}) %all-to-all-start) | async-done | bytes 458784 | tf_op jit(solution)/shard_map/all_to_all | solution.py:552
  29.5 0.0 copy-start.4
  29.5 12.6 %all_to_all.45.modes = f32[8,32,256]{2,1,0:T(8,128)S(1)} all-to-all(f32[8,32,256]{2,1,0:T(8,128)S(1)} %shard_map.70), channel_id=1, replica_groups=mesh['zlo'=4,'y'=8,'core'=2,'x'=4,'zhi'=2] {'x','zhi'}, dimensions={0} | all-to-all | bytes 524288 | tf_op jit(solution)/shard_map/all_to_all | solution.py:552
  42.1 0.0 copy-done.2
  42.1 0.0 copy-done.4
  42.1 1.6 shard_map.71
  43.6 12.0 %all-to-all-start.2 = ((f32[8,48,128]{2,1,0:T(8,128)}), f32[8,48,128]{2,1,0:T(8,128)S(1)}, u32[]{:S(2)}, u32[]{:S(2)}) async-start(f32[8,48,128]{2,1,0:T(8,128)} %get-tuple-element.40), calls=%async_computation.2 | async-start | bytes 393216 | tf_op jit(solution)/shard_map/all_to_all | solution.py:552
  55.7 3.1 %collective-permute-start = (f32[40,256]{1,0:T(8,128)S(1)}, f32[40,256]{1,0:T(8,128)S(1)}, u32[]{:S(2)}, u32[]{:S(2)}) collective-permute-start(f32[40,256]{1,0:T(8,128)S(1)} %get-tuple-element.41), channel_id=1, source_target_pairs={{0,8},{8,16},{16,24},{24,32},{32,40},{40,48},{48,56},{56,64},{64,7... | collective-permute-start | bytes 122888 | tf_op jit(solution)/shard_map/ppermute | solution.py:559
  58.8 1.9 %collective-permute-start.1 = (f32[40,256]{1,0:T(8,128)S(1)}, f32[40,256]{1,0:T(8,128)S(1)}, u32[]{:S(2)}, u32[]{:S(2)}) collective-permute-start(f32[40,256]{1,0:T(8,128)S(1)} %get-tuple-element.42), channel_id=1, source_target_pairs={{8,0},{16,8},{24,16},{32,24},{40,32},{48,40},{56,48},{64,56},{72,6... | collective-permute-start | bytes 122888 | tf_op jit(solution)/shard_map/ppermute | solution.py:559
  60.7 0.0 collective-permute-done.above
  60.7 3.4 %collective-permute-done.1.below = f32[40,256]{1,0:T(8,128)S(1)} collective-permute-done((f32[40,256]{1,0:T(8,128)S(1)}, f32[40,256]{1,0:T(8,128)S(1)}, u32[]{:S(2)}, u32[]{:S(2)}) %collective-permute-start.1) | collective-permute-done | bytes 40992 | tf_op jit(solution)/shard_map/ppermute | solution.py:559
  64.1 0.2 shard_map.72.smooth_hbm
  64.3 0.0 copy-start.5
  64.4 0.0 all-to-all-done.2.arrived
  64.4 18.0 %all_to_all.46.arrived = f32[8,48,128]{2,1,0:T(8,128)S(1)} all-to-all(f32[8,48,128]{2,1,0:T(8,128)S(1)} %shard_map.73), channel_id=1, replica_groups=mesh['zlo'=4,'y'=8,'core'=2,'x'=4,'zhi'=2] {'y'}, dimensions={0} | all-to-all | bytes 393216 | tf_op jit(solution)/shard_map/all_to_all | solution.py:552
  82.4 0.0 copy-done.5
  82.4 3.1 %shard_map.74 = (f32[8,128,256]{2,1,0:T(8,128)}, f32[8,40,256]{2,1,0:T(8,128)S(1)}) custom-call(s32[1]{0:T(128)} %bitcast.day, f32[8,48,128]{2,1,0:T(8,128)S(1)} %all_to_all.46.arrived, f32[512,128]{1,0:T(8,128)S(1)} %select_add_fusion.band, f32[8,32,256]{2,1,0:T(8,128)S(1)} %shard_map.72.smooth_hbm, f32[8,128,256]{2,1,0:T(8,128)S(1)} %copy-done.2, ...), custom_call_target="tpu_custom_call" | custom-call | flops 1000000 | bytes 1000000 | tf_op jit(solution)/shard_map/pallas_call | solution.py:142
  85.5 14.0 %all_to_all.47.arrived = f32[8,40,256]{2,1,0:T(8,128)S(1)} all-to-all(f32[8,40,256]{2,1,0:T(8,128)S(1)} %get-tuple-element.47), channel_id=1, replica_groups=mesh['zlo'=4,'y'=8,'core'=2,'x'=4,'zhi'=2] {'x','zhi'}, dimensions={0} | all-to-all | bytes 655360 | tf_op jit(solution)/shard_map/all_to_all | solution.py:552
  99.5 0.7 shard_map.75
  100.2 3.4 %all-to-all-start.5 = ((f32[8,32,256]{2,1,0:T(8,128)}), f32[8,32,256]{2,1,0:T(8,128)S(1)}, u32[]{:S(2)}, u32[]{:S(2)}) async-start(f32[8,32,256]{2,1,0:T(8,128)} %shard_map.75), calls=%async_computation.5 | async-start | bytes 524288 | tf_op jit(solution)/shard_map/all_to_all | solution.py:552
  103.6 0.8 shard_map.76.factor.scale
  104.4 9.1 %all-to-all-done.5.modes = f32[8,32,256]{2,1,0:T(8,128)S(1)} async-done(((f32[8,32,256]{2,1,0:T(8,128)}), f32[8,32,256]{2,1,0:T(8,128)S(1)}, u32[]{:S(2)}, u32[]{:S(2)}) %all-to-all-start.5) | async-done | bytes 262176 | tf_op jit(solution)/shard_map/all_to_all | solution.py:552
  113.6 0.0 copy-done.3
  113.6 1.0 shard_map.77
  114.6 16.6 %all_to_all.48.arrived = f32[8,40,128]{2,1,0:T(8,128)S(1)} all-to-all(f32[8,40,128]{2,1,0:T(8,128)S(1)} %get-tuple-element.49), channel_id=1, replica_groups=mesh['zlo'=4,'y'=8,'core'=2,'x'=4,'zhi'=2] {'zlo','core'}, dimensions={0} | all-to-all | bytes 327680 | tf_op jit(solution)/shard_map/all_to_all | solution.py:552
  131.2 0.7 shard_map.78
  131.9 3.4 %all-to-all-start.7 = ((f32[8,40,128]{2,1,0:T(8,128)}), f32[8,40,128]{2,1,0:T(8,128)S(1)}, u32[]{:S(2)}, u32[]{:S(2)}) async-start(f32[8,40,128]{2,1,0:T(8,128)} %shard_map.78), calls=%async_computation.7 | async-start | bytes 327680 | tf_op jit(solution)/shard_map/all_to_all | solution.py:552
  135.3 4.7 %collective-permute-start.2 = (f32[40,256]{1,0:T(8,128)S(1)}, f32[40,256]{1,0:T(8,128)S(1)}, u32[]{:S(2)}, u32[]{:S(2)}) collective-permute-start(f32[40,256]{1,0:T(8,128)S(1)} %get-tuple-element.53), channel_id=1, source_target_pairs={{0,8},{8,16},{16,24},{24,32},{32,40},{40,48},{48,56},{56,64},{64,7... | collective-permute-start | bytes 122888 | tf_op jit(solution)/shard_map/ppermute | solution.py:559
  139.9 1.9 %collective-permute-start.3 = (f32[40,256]{1,0:T(8,128)S(1)}, f32[40,256]{1,0:T(8,128)S(1)}, u32[]{:S(2)}, u32[]{:S(2)}) collective-permute-start(f32[40,256]{1,0:T(8,128)S(1)} %get-tuple-element.54), channel_id=1, source_target_pairs={{8,0},{16,8},{24,16},{32,24},{40,32},{48,40},{56,48},{64,56},{72,6... | collective-permute-start | bytes 122888 | tf_op jit(solution)/shard_map/ppermute | solution.py:559
  141.9 0.0 copy-done.1
  141.9 0.0 collective-permute-done.2.above
  141.9 3.6 %collective-permute-done.3.below = f32[40,256]{1,0:T(8,128)S(1)} collective-permute-done((f32[40,256]{1,0:T(8,128)S(1)}, f32[40,256]{1,0:T(8,128)S(1)}, u32[]{:S(2)}, u32[]{:S(2)}) %collective-permute-start.3) | collective-permute-done | bytes 40992 | tf_op jit(solution)/shard_map/ppermute | solution.py:559
  145.5 0.2 shard_map.79.smooth
  145.8 0.0 all-to-all-done.7.arrived
  145.8 0.7 shard_map.80
  146.5 3.4 %all-to-all-start.8 = ((f32[8,32,128]{2,1,0:T(8,128)}), f32[8,32,128]{2,1,0:T(8,128)S(1)}, u32[]{:S(2)}, u32[]{:S(2)}) async-start(f32[8,32,128]{2,1,0:T(8,128)} %get-tuple-element.56.raw), calls=%async_computation.8 | async-start | bytes 262144 | tf_op jit(solution)/shard_map/all_to_all | solution.py:552
  149.8 0.0 copy-done
  149.9 2.3 %shard_map.81 = (f32[128,32]{1,0:T(8,128)S(1)}, f32[32,32]{1,0:T(8,128)S(1)}, f32[32,32]{1,0:T(8,128)S(1)}) custom-call(f32[8,32,128]{2,1,0:T(8,128)} %get-tuple-element.56.raw, f32[8,128]{1,0:T(8,128)S(1)} %get-tuple-element.57.extra, f32[512,128]{1,0:T(8,128)S(1)} %select_add_fusion.band, f32[32,128]{1,0:T(8,128)S(1)} %shard_map.76.factor.scale), custom_call_target="tpu_custom_call" | custom-call | flops 1000000 | bytes 1000000 | tf_op jit(solution)/shard_map/pallas_call | solution.py:142
  152.2 1.5 shard_map.82.filled_in
  153.7 5.5 %all-to-all-done.8.arrived = f32[8,32,128]{2,1,0:T(8,128)S(1)} async-done(((f32[8,32,128]{2,1,0:T(8,128)}), f32[8,32,128]{2,1,0:T(8,128)S(1)}, u32[]{:S(2)}, u32[]{:S(2)}) %all-to-all-start.8) | async-done | bytes 131104 | tf_op jit(solution)/shard_map/all_to_all | solution.py:552
  159.2 3.2 %shard_map.83 = (f32[32,128]{1,0:T(8,128)}, f32[128,8,256]{2,1,0:T(8,128)}) custom-call(s32[1]{0:T(128)} %bitcast.day, f32[8,32,128]{2,1,0:T(8,128)S(1)} %all-to-all-done.8.arrived, f32[512,128]{1,0:T(8,128)S(1)} %select_add_fusion.band, f32[32,32]{1,0:T(8,128)S(1)} %get-tuple-element.58.factor, ...), custom_call_target="tpu_custom_call", output_to_operand_aliasing={{1}: (12, {})} | custom-call | flops 1000000 | bytes 1000000 | tf_op jit(solution)/shard_map/pallas_call | solution.py:142
  (13 shorter events, 0.1 us)
Async XLA Ops:
  3.6 25.9 %all-to-all-start = ((f32[8,56,256]{2,1,0:T(8,128)}), f32[8,56,256]{2,1,0:T(8,128)S(1)}, u32[]{:S(2)}, u32[]{:S(2)}) async-start(f32[8,56,256]{2,1,0:T(8,128)} %shard_map.68), calls=%async_computation | async-start | bytes 917504 | tf_op jit(solution)/shard_map/all_to_all | solution.py:552
  16.9 4.2 %copy-start.6 = (f32[128,7]{0,1:T(8,128)S(1)}, f32[128,7]{0,1:T(8,128)}, u32[]{:S(2)}) copy-start(f32[128,7]{0,1:T(8,128)} %param.9) | copy-start | bytes 10756
  21.0 21.0 %copy-start.2 = (f32[8,128,256]{2,1,0:T(8,128)S(1)}, f32[8,128,256]{2,1,0:T(8,128)}, u32[]{:S(2)}) copy-start(f32[8,128,256]{2,1,0:T(8,128)} %get-tuple-element.39.filled.first) | copy-start | bytes 3145732
  29.5 12.6 %copy-start.4 = (s32[8,256]{1,0:T(8,128)S(1)}, s32[8,256]{1,0:T(8,128)}, u32[]{:S(2)}) copy-start(s32[8,256]{1,0:T(8,128)} %land.15) | copy-start | bytes 24580
  43.6 20.7 %all-to-all-start.2 = ((f32[8,48,128]{2,1,0:T(8,128)}), f32[8,48,128]{2,1,0:T(8,128)S(1)}, u32[]{:S(2)}, u32[]{:S(2)}) async-start(f32[8,48,128]{2,1,0:T(8,128)} %get-tuple-element.40), calls=%async_computation.2 | async-start | bytes 393216 | tf_op jit(solution)/shard_map/all_to_all | solution.py:552
  55.7 5.0 %collective-permute-start = (f32[40,256]{1,0:T(8,128)S(1)}, f32[40,256]{1,0:T(8,128)S(1)}, u32[]{:S(2)}, u32[]{:S(2)}) collective-permute-start(f32[40,256]{1,0:T(8,128)S(1)} %get-tuple-element.41), channel_id=1, source_target_pairs={{0,8},{8,16},{16,24},{24,32},{32,40},{40,48},{48,56},{56,64},{64,7... | collective-permute-start | bytes 122888 | tf_op jit(solution)/shard_map/ppermute | solution.py:559
  58.8 5.3 %collective-permute-start.1 = (f32[40,256]{1,0:T(8,128)S(1)}, f32[40,256]{1,0:T(8,128)S(1)}, u32[]{:S(2)}, u32[]{:S(2)}) collective-permute-start(f32[40,256]{1,0:T(8,128)S(1)} %get-tuple-element.42), channel_id=1, source_target_pairs={{8,0},{16,8},{24,16},{32,24},{40,32},{48,40},{56,48},{64,56},{72,6... | collective-permute-start | bytes 122888 | tf_op jit(solution)/shard_map/ppermute | solution.py:559
  64.3 18.0 %copy-start.5 = (bf16[8,128,256]{2,1,0:T(8,128)(2,1)S(1)}, bf16[8,128,256]{2,1,0:T(8,128)(2,1)}, u32[]{:S(2)}) copy-start(bf16[8,128,256]{2,1,0:T(8,128)(2,1)} %get-tuple-element.46.gap) | copy-start | bytes 1572868
  99.4 14.1 %copy-start.3 = (f32[8,128,256]{2,1,0:T(8,128)S(1)}, f32[8,128,256]{2,1,0:T(8,128)}, u32[]{:S(2)}) copy-start(f32[8,128,256]{2,1,0:T(8,128)} %get-tuple-element.48.filled) | copy-start | bytes 3145732
  100.2 13.4 %all-to-all-start.5 = ((f32[8,32,256]{2,1,0:T(8,128)}), f32[8,32,256]{2,1,0:T(8,128)S(1)}, u32[]{:S(2)}, u32[]{:S(2)}) async-start(f32[8,32,256]{2,1,0:T(8,128)} %shard_map.75), calls=%async_computation.5 | async-start | bytes 524288 | tf_op jit(solution)/shard_map/all_to_all | solution.py:552
  104.4 37.4 %copy-start.1 = (s32[128,8,256]{2,1,0:T(8,128)S(1)}, s32[128,8,256]{2,1,0:T(8,128)}, u32[]{:S(2)}) copy-start(s32[128,8,256]{2,1,0:T(8,128)} %missing.1) | copy-start | bytes 3145732
  131.2 18.7 %copy-start = (f32[128,8,256]{2,1,0:T(8,128)S(1)}, f32[128,8,256]{2,1,0:T(8,128)}, u32[]{:S(2)}) copy-start(f32[128,8,256]{2,1,0:T(8,128)} %observed.1) | copy-start | bytes 3145732
  131.9 13.9 %all-to-all-start.7 = ((f32[8,40,128]{2,1,0:T(8,128)}), f32[8,40,128]{2,1,0:T(8,128)S(1)}, u32[]{:S(2)}, u32[]{:S(2)}) async-start(f32[8,40,128]{2,1,0:T(8,128)} %shard_map.78), calls=%async_computation.7 | async-start | bytes 327680 | tf_op jit(solution)/shard_map/all_to_all | solution.py:552
  135.3 6.6 %collective-permute-start.2 = (f32[40,256]{1,0:T(8,128)S(1)}, f32[40,256]{1,0:T(8,128)S(1)}, u32[]{:S(2)}, u32[]{:S(2)}) collective-permute-start(f32[40,256]{1,0:T(8,128)S(1)} %get-tuple-element.53), channel_id=1, source_target_pairs={{0,8},{8,16},{16,24},{24,32},{32,40},{40,48},{48,56},{56,64},{64,7... | collective-permute-start | bytes 122888 | tf_op jit(solution)/shard_map/ppermute | solution.py:559
  139.9 5.6 %collective-permute-start.3 = (f32[40,256]{1,0:T(8,128)S(1)}, f32[40,256]{1,0:T(8,128)S(1)}, u32[]{:S(2)}, u32[]{:S(2)}) collective-permute-start(f32[40,256]{1,0:T(8,128)S(1)} %get-tuple-element.54), channel_id=1, source_target_pairs={{8,0},{16,8},{24,16},{32,24},{40,32},{48,40},{56,48},{64,56},{72,6... | collective-permute-start | bytes 122888 | tf_op jit(solution)/shard_map/ppermute | solution.py:559
  146.5 12.8 %all-to-all-start.8 = ((f32[8,32,128]{2,1,0:T(8,128)}), f32[8,32,128]{2,1,0:T(8,128)S(1)}, u32[]{:S(2)}, u32[]{:S(2)}) async-start(f32[8,32,128]{2,1,0:T(8,128)} %get-tuple-element.56.raw), calls=%async_computation.8 | async-start | bytes 262144 | tf_op jit(solution)/shard_map/all_to_all | solution.py:552

commit v11 on v9

--- a/solution.py
+++ b/solution.py
@@ -667,9 +667,11 @@
         (modes, filled, land, factor),
     )
     joint, low, high = add_near(joint, edges)
-    joint, smooth = smooth_beside(joint, low, high, modes)
+    joint = swap(joint, "y")
     raw, extra = call(add_last_body, [(8, K, LANES), (8, LANES)], (joint,))
     arrived = swap(raw, DAY)
+    above, below = near_rows(low, high)
+    smooth = call(smooth_body, block, (modes, above, below, land))
     mixed, right, found = call(
         last_weights_body,
         [(days, K), (K, K), (K, K)],

time: 162 us -> 160 us (0.988)
  waiting for transfers between devices: 31.9 us -> 29.4 us
    ppermute x4, waiting for transfers between devices: 7.24 us -> 3.68 us  [near_rows(): return (lax.ppermute(edge_high, PIX, up), lax.ppermute(edge_low, PIX, down))]
where the time goes in v11:
time: 160 us; the launch traced here: 158 us
  blocking collectives  56.3 us (35%)
  starting transfers between devices  47.1 us (29%)
  waiting for transfers between devices  29.4 us (18%)
  Pallas kernels  23.2 us (14%)
    all_to_all x4, blocking collectives, swap(): return lax.all_to_all(blocks, axes, 0, 0)  56.3 us
    all_to_all x5, starting transfers between devices, swap(): return lax.all_to_all(blocks, axes, 0, 0)  32.5 us
    all_to_all x5, waiting for transfers between devices, swap(): return lax.all_to_all(blocks, axes, 0, 0)  25.7 us
    pallas_call x16, Pallas kernels, call(): pl.pallas_call(body, out_shape=shapes if many else shapes[0], in_specs=sp...  23.2 us
    ppermute x4, starting transfers between devices, near_rows(): return (lax.ppermute(edge_high, PIX, up), lax.ppermute(edge_low, PIX, down))  14.6 us
    ppermute x4, waiting for transfers between devices, near_rows(): return (lax.ppermute(edge_high, PIX, up), lax.ppermute(edge_low, PIX, down))  3.68 us
  transfers between devices with their start and end apart: 9, of which 5 were waited for; matrix products, arithmetic and copies ran while one was open for 0% of the time, Pallas kernels for 6%

profile of v11, /device:TPU:1, one launch (start us, length us, event | category | flops | bytes accessed | tf_op | source)
XLA Modules:
  0.0 157.6 jit_solution(3393878408771137019)
XLA Ops:
  0.6 2.9 %shard_map.68 = f32[8,56,256]{2,1,0:T(8,128)} custom-call(s32[1]{0:T(128)} %bitcast.day, f32[128,8,256]{2,1,0:T(8,128)} %observed.1, s32[128,8,256]{2,1,0:T(8,128)} %missing.1, s32[8,256]{1,0:T(8,128)} %land.15, f32[32,128]{1,0:T(8,128)} %bitcast.18), custom_call_target="tpu_custom_call" | custom-call | flops 1000000 | bytes 1000000 | tf_op jit(solution)/shard_map/pallas_call | solution.py:142
  3.6 13.3 %all-to-all-start = ((f32[8,56,256]{2,1,0:T(8,128)}), f32[8,56,256]{2,1,0:T(8,128)S(1)}, u32[]{:S(2)}, u32[]{:S(2)}) async-start(f32[8,56,256]{2,1,0:T(8,128)} %shard_map.68), calls=%async_computation | async-start | bytes 917504 | tf_op jit(solution)/shard_map/all_to_all | solution.py:552
  16.9 0.0 copy-start.6
  16.9 4.1 %shard_map.69 = (f32[8,128,256]{2,1,0:T(8,128)}, bf16[8,128,256]{2,1,0:T(8,128)(2,1)}) custom-call(f32[128,8,256]{2,1,0:T(8,128)} %observed.1, s32[128,8,256]{2,1,0:T(8,128)} %missing.1, s32[8,256]{1,0:T(8,128)} %land.15), custom_call_target="tpu_custom_call" | custom-call | flops 1000000 | bytes 1000000 | tf_op jit(solution)/shard_map/pallas_call | solution.py:142
  21.0 0.0 copy-start.2
  21.1 0.0 copy-done.6
  21.1 0.7 select_add_fusion.band
  21.8 7.6 %all-to-all-done.arrived = f32[8,56,256]{2,1,0:T(8,128)S(1)} async-done(((f32[8,56,256]{2,1,0:T(8,128)}), f32[8,56,256]{2,1,0:T(8,128)S(1)}, u32[]{:S(2)}, u32[]{:S(2)}) %all-to-all-start) | async-done | bytes 458784 | tf_op jit(solution)/shard_map/all_to_all | solution.py:552
  29.5 0.0 copy-start.4
  29.5 12.6 %all_to_all.45.modes = f32[8,32,256]{2,1,0:T(8,128)S(1)} all-to-all(f32[8,32,256]{2,1,0:T(8,128)S(1)} %shard_map.70), channel_id=1, replica_groups=mesh['zlo'=4,'y'=8,'core'=2,'x'=4,'zhi'=2] {'x','zhi'}, dimensions={0} | all-to-all | bytes 524288 | tf_op jit(solution)/shard_map/all_to_all | solution.py:552
  42.1 0.0 copy-done.2
  42.1 0.0 copy-done.4
  42.1 0.9 shard_map.71
  43.0 18.3 %all_to_all.46.arrived = f32[8,48,128]{2,1,0:T(8,128)S(1)} all-to-all(f32[8,48,128]{2,1,0:T(8,128)S(1)} %get-tuple-element.41), channel_id=1, replica_groups=mesh['zlo'=4,'y'=8,'core'=2,'x'=4,'zhi'=2] {'zlo','core'}, dimensions={0} | all-to-all | bytes 393216 | tf_op jit(solution)/shard_map/all_to_all | solution.py:552
  61.3 0.7 shard_map.72
  62.0 7.0 %all-to-all-start.3 = ((f32[8,48,128]{2,1,0:T(8,128)}), f32[8,48,128]{2,1,0:T(8,128)S(1)}, u32[]{:S(2)}, u32[]{:S(2)}) async-start(f32[8,48,128]{2,1,0:T(8,128)} %shard_map.72), calls=%async_computation.3 | async-start | bytes 393216 | tf_op jit(solution)/shard_map/all_to_all | solution.py:552
  68.9 5.7 %collective-permute-start = (f32[40,256]{1,0:T(8,128)S(1)}, f32[40,256]{1,0:T(8,128)S(1)}, u32[]{:S(2)}, u32[]{:S(2)}) collective-permute-start(f32[40,256]{1,0:T(8,128)S(1)} %get-tuple-element.45), channel_id=1, source_target_pairs={{0,8},{8,16},{16,24},{24,32},{32,40},{40,48},{48,56},{56,64},{64,7... | collective-permute-start | bytes 122888 | tf_op jit(solution)/shard_map/ppermute | solution.py:559
  74.6 1.9 %collective-permute-start.1 = (f32[40,256]{1,0:T(8,128)S(1)}, f32[40,256]{1,0:T(8,128)S(1)}, u32[]{:S(2)}, u32[]{:S(2)}) collective-permute-start(f32[40,256]{1,0:T(8,128)S(1)} %get-tuple-element.46), channel_id=1, source_target_pairs={{8,0},{16,8},{24,16},{32,24},{40,32},{48,40},{56,48},{64,56},{72,6... | collective-permute-start | bytes 122888 | tf_op jit(solution)/shard_map/ppermute | solution.py:559
  76.5 0.0 collective-permute-done.above
  76.6 3.7 %collective-permute-done.1.below = f32[40,256]{1,0:T(8,128)S(1)} collective-permute-done((f32[40,256]{1,0:T(8,128)S(1)}, f32[40,256]{1,0:T(8,128)S(1)}, u32[]{:S(2)}, u32[]{:S(2)}) %collective-permute-start.1) | collective-permute-done | bytes 40992 | tf_op jit(solution)/shard_map/ppermute | solution.py:559
  80.2 0.2 shard_map.73.smooth_hbm
  80.5 0.0 all-to-all-done.3.arrived
  80.5 0.0 copy-done.5
  80.5 3.1 %shard_map.74 = (f32[8,128,256]{2,1,0:T(8,128)}, f32[8,40,256]{2,1,0:T(8,128)S(1)}) custom-call(s32[1]{0:T(128)} %bitcast.day, f32[8,48,128]{2,1,0:T(8,128)S(1)} %all-to-all-done.3.arrived, f32[512,128]{1,0:T(8,128)S(1)} %select_add_fusion.band, f32[8,32,256]{2,1,0:T(8,128)S(1)} %shard_map.73.smooth_hbm, f32[8,128,256]{2,1,0:T(8,128)S(1)} %copy-done.2, ...), custom_call_target="tpu_custom_call" | custom-call | flops 1000000 | bytes 1000000 | tf_op jit(solution)/shard_map/pallas_call | solution.py:142
  83.6 14.7 %all_to_all.47.arrived = f32[8,40,256]{2,1,0:T(8,128)S(1)} all-to-all(f32[8,40,256]{2,1,0:T(8,128)S(1)} %get-tuple-element.51), channel_id=1, replica_groups=mesh['zlo'=4,'y'=8,'core'=2,'x'=4,'zhi'=2] {'x','zhi'}, dimensions={0} | all-to-all | bytes 655360 | tf_op jit(solution)/shard_map/all_to_all | solution.py:552
  98.3 0.7 shard_map.75
  99.0 4.2 %all-to-all-start.5 = ((f32[8,32,256]{2,1,0:T(8,128)}), f32[8,32,256]{2,1,0:T(8,128)S(1)}, u32[]{:S(2)}, u32[]{:S(2)}) async-start(f32[8,32,256]{2,1,0:T(8,128)} %shard_map.75), calls=%async_computation.5 | async-start | bytes 524288 | tf_op jit(solution)/shard_map/all_to_all | solution.py:552
  103.2 0.8 shard_map.76.factor.scale
  104.1 11.5 %all-to-all-done.5.modes = f32[8,32,256]{2,1,0:T(8,128)S(1)} async-done(((f32[8,32,256]{2,1,0:T(8,128)}), f32[8,32,256]{2,1,0:T(8,128)S(1)}, u32[]{:S(2)}, u32[]{:S(2)}) %all-to-all-start.5) | async-done | bytes 262176 | tf_op jit(solution)/shard_map/all_to_all | solution.py:552
  115.5 0.0 copy-done.3
  115.5 1.0 shard_map.77
  116.6 0.0 copy-start
  116.6 10.7 %all_to_all.48.arrived = f32[8,40,128]{2,1,0:T(8,128)S(1)} all-to-all(f32[8,40,128]{2,1,0:T(8,128)S(1)} %get-tuple-element.53), channel_id=1, replica_groups=mesh['zlo'=4,'y'=8,'core'=2,'x'=4,'zhi'=2] {'zlo','core'}, dimensions={0} | all-to-all | bytes 327680 | tf_op jit(solution)/shard_map/all_to_all | solution.py:552
  127.3 0.7 shard_map.78
  127.9 4.7 %all-to-all-start.7 = ((f32[8,40,128]{2,1,0:T(8,128)}), f32[8,40,128]{2,1,0:T(8,128)S(1)}, u32[]{:S(2)}, u32[]{:S(2)}) async-start(f32[8,40,128]{2,1,0:T(8,128)} %shard_map.78), calls=%async_computation.7 | async-start | bytes 327680 | tf_op jit(solution)/shard_map/all_to_all | solution.py:552
  132.6 0.0 copy-done.1
  132.7 5.0 %collective-permute-start.2 = (f32[40,256]{1,0:T(8,128)S(1)}, f32[40,256]{1,0:T(8,128)S(1)}, u32[]{:S(2)}, u32[]{:S(2)}) collective-permute-start(f32[40,256]{1,0:T(8,128)S(1)} %get-tuple-element.62), channel_id=1, source_target_pairs={{0,8},{8,16},{16,24},{24,32},{32,40},{40,48},{48,56},{56,64},{64,7... | collective-permute-start | bytes 122888 | tf_op jit(solution)/shard_map/ppermute | solution.py:559
  137.7 1.9 %collective-permute-start.3 = (f32[40,256]{1,0:T(8,128)S(1)}, f32[40,256]{1,0:T(8,128)S(1)}, u32[]{:S(2)}, u32[]{:S(2)}) collective-permute-start(f32[40,256]{1,0:T(8,128)S(1)} %get-tuple-element.63), channel_id=1, source_target_pairs={{8,0},{16,8},{24,16},{32,24},{40,32},{48,40},{56,48},{64,56},{72,6... | collective-permute-start | bytes 122888 | tf_op jit(solution)/shard_map/ppermute | solution.py:559
  139.6 1.4 all-to-all-done.7.arrived
  141.0 0.7 shard_map.79
  141.7 3.4 %all-to-all-start.8 = ((f32[8,32,128]{2,1,0:T(8,128)}), f32[8,32,128]{2,1,0:T(8,128)S(1)}, u32[]{:S(2)}, u32[]{:S(2)}) async-start(f32[8,32,128]{2,1,0:T(8,128)} %get-tuple-element.57.raw), calls=%async_computation.8 | async-start | bytes 262144 | tf_op jit(solution)/shard_map/all_to_all | solution.py:552
  145.1 0.0 collective-permute-done.2.above
  145.1 0.0 collective-permute-done.3.below
  145.1 0.2 shard_map.81.smooth
  145.3 2.3 %shard_map.80 = (f32[128,32]{1,0:T(8,128)S(1)}, f32[32,32]{1,0:T(8,128)S(1)}, f32[32,32]{1,0:T(8,128)S(1)}) custom-call(f32[8,32,128]{2,1,0:T(8,128)} %get-tuple-element.57.raw, f32[8,128]{1,0:T(8,128)S(1)} %get-tuple-element.58.extra, f32[512,128]{1,0:T(8,128)S(1)} %select_add_fusion.band, f32[32,128]{1,0:T(8,128)S(1)} %shard_map.76.factor.scale), custom_call_target="tpu_custom_call" | custom-call | flops 1000000 | bytes 1000000 | tf_op jit(solution)/shard_map/pallas_call | solution.py:142
  147.6 1.5 shard_map.82.filled_in
  149.2 5.2 %all-to-all-done.8.arrived = f32[8,32,128]{2,1,0:T(8,128)S(1)} async-done(((f32[8,32,128]{2,1,0:T(8,128)}), f32[8,32,128]{2,1,0:T(8,128)S(1)}, u32[]{:S(2)}, u32[]{:S(2)}) %all-to-all-start.8) | async-done | bytes 131104 | tf_op jit(solution)/shard_map/all_to_all | solution.py:552
  154.4 3.2 %shard_map.83 = (f32[32,128]{1,0:T(8,128)}, f32[128,8,256]{2,1,0:T(8,128)}) custom-call(s32[1]{0:T(128)} %bitcast.day, f32[8,32,128]{2,1,0:T(8,128)S(1)} %all-to-all-done.8.arrived, f32[512,128]{1,0:T(8,128)S(1)} %select_add_fusion.band, f32[32,32]{1,0:T(8,128)S(1)} %get-tuple-element.59.factor, ...), custom_call_target="tpu_custom_call", output_to_operand_aliasing={{1}: (12, {})} | custom-call | flops 1000000 | bytes 1000000 | tf_op jit(solution)/shard_map/pallas_call | solution.py:142
  (13 shorter events, 0.1 us)
Async XLA Ops:
  3.6 25.9 %all-to-all-start = ((f32[8,56,256]{2,1,0:T(8,128)}), f32[8,56,256]{2,1,0:T(8,128)S(1)}, u32[]{:S(2)}, u32[]{:S(2)}) async-start(f32[8,56,256]{2,1,0:T(8,128)} %shard_map.68), calls=%async_computation | async-start | bytes 917504 | tf_op jit(solution)/shard_map/all_to_all | solution.py:552
  16.9 4.2 %copy-start.6 = (f32[128,7]{0,1:T(8,128)S(1)}, f32[128,7]{0,1:T(8,128)}, u32[]{:S(2)}) copy-start(f32[128,7]{0,1:T(8,128)} %param.9) | copy-start | bytes 10756
  21.0 21.0 %copy-start.2 = (f32[8,128,256]{2,1,0:T(8,128)S(1)}, f32[8,128,256]{2,1,0:T(8,128)}, u32[]{:S(2)}) copy-start(f32[8,128,256]{2,1,0:T(8,128)} %get-tuple-element.40.filled.first) | copy-start | bytes 3145732
  29.5 12.6 %copy-start.4 = (s32[8,256]{1,0:T(8,128)S(1)}, s32[8,256]{1,0:T(8,128)}, u32[]{:S(2)}) copy-start(s32[8,256]{1,0:T(8,128)} %land.15) | copy-start | bytes 24580
  62.0 18.5 %copy-start.5 = (bf16[8,128,256]{2,1,0:T(8,128)(2,1)S(1)}, bf16[8,128,256]{2,1,0:T(8,128)(2,1)}, u32[]{:S(2)}) copy-start(bf16[8,128,256]{2,1,0:T(8,128)(2,1)} %get-tuple-element.50.gap) | copy-start | bytes 1572868
  62.0 18.5 %all-to-all-start.3 = ((f32[8,48,128]{2,1,0:T(8,128)}), f32[8,48,128]{2,1,0:T(8,128)S(1)}, u32[]{:S(2)}, u32[]{:S(2)}) async-start(f32[8,48,128]{2,1,0:T(8,128)} %shard_map.72), calls=%async_computation.3 | async-start | bytes 393216 | tf_op jit(solution)/shard_map/all_to_all | solution.py:552
  68.9 7.6 %collective-permute-start = (f32[40,256]{1,0:T(8,128)S(1)}, f32[40,256]{1,0:T(8,128)S(1)}, u32[]{:S(2)}, u32[]{:S(2)}) collective-permute-start(f32[40,256]{1,0:T(8,128)S(1)} %get-tuple-element.45), channel_id=1, source_target_pairs={{0,8},{8,16},{16,24},{24,32},{32,40},{40,48},{48,56},{56,64},{64,7... | collective-permute-start | bytes 122888 | tf_op jit(solution)/shard_map/ppermute | solution.py:559
  74.6 5.6 %collective-permute-start.1 = (f32[40,256]{1,0:T(8,128)S(1)}, f32[40,256]{1,0:T(8,128)S(1)}, u32[]{:S(2)}, u32[]{:S(2)}) collective-permute-start(f32[40,256]{1,0:T(8,128)S(1)} %get-tuple-element.46), channel_id=1, source_target_pairs={{8,0},{16,8},{24,16},{32,24},{40,32},{48,40},{56,48},{64,56},{72,6... | collective-permute-start | bytes 122888 | tf_op jit(solution)/shard_map/ppermute | solution.py:559
  98.3 17.2 %copy-start.3 = (f32[8,128,256]{2,1,0:T(8,128)S(1)}, f32[8,128,256]{2,1,0:T(8,128)}, u32[]{:S(2)}) copy-start(f32[8,128,256]{2,1,0:T(8,128)} %get-tuple-element.52.filled) | copy-start | bytes 3145732
  99.0 16.5 %all-to-all-start.5 = ((f32[8,32,256]{2,1,0:T(8,128)}), f32[8,32,256]{2,1,0:T(8,128)S(1)}, u32[]{:S(2)}, u32[]{:S(2)}) async-start(f32[8,32,256]{2,1,0:T(8,128)} %shard_map.75), calls=%async_computation.5 | async-start | bytes 524288 | tf_op jit(solution)/shard_map/all_to_all | solution.py:552
  104.1 28.6 %copy-start.1 = (s32[128,8,256]{2,1,0:T(8,128)S(1)}, s32[128,8,256]{2,1,0:T(8,128)}, u32[]{:S(2)}) copy-start(s32[128,8,256]{2,1,0:T(8,128)} %missing.1) | copy-start | bytes 3145732
  116.6 28.5 %copy-start = (f32[128,8,256]{2,1,0:T(8,128)S(1)}, f32[128,8,256]{2,1,0:T(8,128)}, u32[]{:S(2)}) copy-start(f32[128,8,256]{2,1,0:T(8,128)} %observed.1) | copy-start | bytes 3145732
  127.9 13.1 %all-to-all-start.7 = ((f32[8,40,128]{2,1,0:T(8,128)}), f32[8,40,128]{2,1,0:T(8,128)S(1)}, u32[]{:S(2)}, u32[]{:S(2)}) async-start(f32[8,40,128]{2,1,0:T(8,128)} %shard_map.78), calls=%async_computation.7 | async-start | bytes 327680 | tf_op jit(solution)/shard_map/all_to_all | solution.py:552
  132.7 12.4 %collective-permute-start.2 = (f32[40,256]{1,0:T(8,128)S(1)}, f32[40,256]{1,0:T(8,128)S(1)}, u32[]{:S(2)}, u32[]{:S(2)}) collective-permute-start(f32[40,256]{1,0:T(8,128)S(1)} %get-tuple-element.62), channel_id=1, source_target_pairs={{0,8},{8,16},{16,24},{24,32},{32,40},{40,48},{48,56},{56,64},{64,7... | collective-permute-start | bytes 122888 | tf_op jit(solution)/shard_map/ppermute | solution.py:559
  137.7 7.4 %collective-permute-start.3 = (f32[40,256]{1,0:T(8,128)S(1)}, f32[40,256]{1,0:T(8,128)S(1)}, u32[]{:S(2)}, u32[]{:S(2)}) collective-permute-start(f32[40,256]{1,0:T(8,128)S(1)} %get-tuple-element.63), channel_id=1, source_target_pairs={{8,0},{16,8},{24,16},{32,24},{40,32},{48,40},{56,48},{64,56},{72,6... | collective-permute-start | bytes 122888 | tf_op jit(solution)/shard_map/ppermute | solution.py:559
  141.7 12.8 %all-to-all-start.8 = ((f32[8,32,128]{2,1,0:T(8,128)}), f32[8,32,128]{2,1,0:T(8,128)S(1)}, u32[]{:S(2)}, u32[]{:S(2)}) async-start(f32[8,32,128]{2,1,0:T(8,128)} %get-tuple-element.57.raw), calls=%async_computation.8 | async-start | bytes 262144 | tf_op jit(solution)/shard_map/all_to_all | solution.py:552
